TPU v7x, 32 devices: a whole 2x2x4 slice. The times are simulated.
32 devices in a mesh: dp: 16 (over z, y, core), blk: 2 (over x).
Axes of the slice: x: 2, y: 2, z: 4, core: 2. Of those that a mesh axis runs over, the one named last changes fastest.
Arguments:
- frames: bfloat16 [8192, 768], P(('dp', 'blk')), may hold values from -6 to 6
- cotangent: bfloat16 [8192, 768], P(('dp', 'blk')), may hold values from -6 to 6
- seq_lengths: int32 [16, 4], P('dp'), may hold values from 32 to 257, as said below
- key_mask: int32 [8192], P(('dp', 'blk')), may hold values 0 or 1
- qkv_weight: bfloat16 [768, 2304], P(None, ('dp', 'blk')), may hold values from -0.21875 to 0.21875
- query_value_bias: bfloat16 [1536], P(('dp', 'blk')), may hold values from -3 to 3
- out_weight: bfloat16 [768, 768], P(None, ('dp', 'blk')), may hold values from -0.875 to 0.875
- out_bias: bfloat16 [768], P(('dp', 'blk')), may hold values from -3 to 3
- up_weight: bfloat16 [768, 3072], P(None, ('dp', 'blk')), may hold values from -0.21875 to 0.21875
- up_bias: bfloat16 [3072], P(('dp', 'blk')), may hold values from -3 to 3
- down_weight: bfloat16 [3072, 768], P(None, ('dp', 'blk')), may hold values from -0.109375 to 0.109375
- down_bias: bfloat16 [768], P(('dp', 'blk')), may hold values from -3 to 3
- first_gain: bfloat16 [768], P(('dp', 'blk')), may hold values from 0.5 to 1.5
- first_shift: bfloat16 [768], P(('dp', 'blk')), may hold values from -3 to 3
- second_gain: bfloat16 [768], P(('dp', 'blk')), may hold values from 0.5 to 1.5
- second_shift: bfloat16 [768], P(('dp', 'blk')), may hold values from -3 to 3
- rel_bias: bfloat16 [321, 12], replicated, may hold values from -4 to 4
Outputs:
- layer_out: float32 [8192, 768], P(('dp', 'blk'))
- frames_grad: float32 [8192, 768], P(('dp', 'blk'))
- qkv_weight_grad: float32 [768, 2304], P(None, ('dp', 'blk'))
- query_value_bias_grad: float32 [1536], P(('dp', 'blk'))
- out_weight_grad: float32 [768, 768], P(None, ('dp', 'blk'))
- out_bias_grad: float32 [768], P(('dp', 'blk'))
- up_weight_grad: float32 [768, 3072], P(None, ('dp', 'blk'))
- up_bias_grad: float32 [3072], P(('dp', 'blk'))
- down_weight_grad: float32 [3072, 768], P(None, ('dp', 'blk'))
- down_bias_grad: float32 [768], P(('dp', 'blk'))
- first_gain_grad: float32 [768], P(('dp', 'blk'))
- first_shift_grad: float32 [768], P(('dp', 'blk'))
- second_gain_grad: float32 [768], P(('dp', 'blk'))
- second_shift_grad: float32 [768], P(('dp', 'blk'))
- rel_bias_grad: float32 [321, 12], replicated
Inputs may be any that keep to these rules, and one draw needn't show every extreme that they name: `seq_lengths`: in each row, the 4 lengths sum to 256 * 2; each row holds one sequence of exactly the largest length.
All inputs are finite; a program needn't handle non-finite values. No bound on the sum of `key_mask` on one device may be relied on, other than what follows from the above.
Results may differ from a plain program's by a relative error of at most 0.014.
Values may be sent and summed in bfloat16 or wider, within the bound.
No kernel may reach another device: no remote copies, remote signals or barrier semaphores. Data moves between devices by JAX's collectives and lax.ppermute only.
A program may use at most 192 MiB of HBM per device.

v0:
```python
import math

import jax
import jax.numpy as jnp
from jax import lax
from jax.sharding import PartitionSpec as P

H = 12
HD = 64
MAXREL = 160
BLOCK = 256
BUCKETS = 321


EPSILON = 1e-05
MASKED = -2e30
START_PEAK = -1e30
HIGHEST = lax.Precision.HIGHEST


def from_behind(block, axis, distance):
    devices = range(lax.axis_size(axis))
    route = [((i - distance) % len(devices), i) for i in devices]
    return lax.ppermute(block, axis, route)


def layer_norm(values, gain_vec, shift_vec):
    center = values - jnp.mean(values, axis=-1, keepdims=True)
    inv_std = lax.rsqrt(jnp.mean(center * center, axis=-1, keepdims=True) + EPSILON)
    normed = center * inv_std
    return (normed * gain_vec + shift_vec, normed, inv_std)


def norm_back(gradient, normed, inv_std, gain_vec):
    scaled = gradient * gain_vec
    inner = (
        scaled
        - jnp.mean(scaled, axis=-1, keepdims=True)
        - normed * jnp.mean(scaled * normed, axis=-1, keepdims=True)
    )
    return (inner * inv_std, jnp.sum(gradient * normed, axis=0), jnp.sum(gradient, axis=0))


def gelu_parts(values):
    normal_cdf = 0.5 * (1.0 + lax.erf(values * 0.7071067811865476))
    density = jnp.exp(-0.5 * values * values) * 0.3989422804014327
    return (values * normal_cdf, normal_cdf + values * density)


def doc_numbers(seq_ends, positions):
    return jnp.sum((positions[:, None] >= seq_ends[None, :]).astype(jnp.int32), axis=1)


def pair_logits(
    query_block, key_block, query_pos, key_pos, query_doc, key_doc, key_live, table_heads
):
    block_len = query_block.shape[0]
    raw = jnp.einsum(
        "qhd,khd->hqk",
        query_block.reshape(block_len, H, HD),
        key_block.reshape(-1, H, HD),
        preferred_element_type=jnp.float32,
    )
    relative = jnp.clip(key_pos[None, :] - query_pos[:, None], -MAXREL, MAXREL) + MAXREL
    bias = jnp.take(table_heads, relative, axis=1)
    allowed = (query_doc[:, None] == key_doc[None, :]) & (
        (key_live[None, :] > 0.5) | (query_pos[:, None] == key_pos[None, :])
    )
    return jnp.where(allowed[None], raw * (1.0 / math.sqrt(HD)) + bias, MASKED)


def diagonal_sums(gradient, offset):
    heads, block_len, _ = gradient.shape
    flipped = gradient[:, ::-1, :]
    padded = jnp.pad(flipped, ((0, 0), (0, 0), (0, block_len)))
    sheared = padded.reshape(heads, 2 * block_len * block_len)[:, : block_len * (2 * block_len - 1)]
    sheared = sheared.reshape(heads, block_len, 2 * block_len - 1)
    diag_sums = jnp.sum(sheared, axis=1)
    distance = offset + jnp.arange(2 * block_len - 1, dtype=jnp.int32) - (block_len - 1)
    bucket = jnp.clip(distance, -MAXREL, MAXREL) + MAXREL
    onehot = (bucket[:, None] == jnp.arange(BUCKETS, dtype=jnp.int32)[None, :]).astype(jnp.float32)
    return jnp.dot(diag_sums, onehot, precision=HIGHEST)


def body(
    frames,
    cotangent,
    seq_lengths,
    key_mask,
    qkv_weight,
    query_value_bias,
    out_weight,
    out_bias,
    up_weight,
    up_bias,
    down_weight,
    down_bias,
    first_gain,
    first_shift,
    second_gain,
    second_shift,
    rel_bias,
):
    cycle_size = lax.axis_size("blk")
    cycle_place = lax.axis_index("blk")
    shard_len = frames.shape[0]
    width = frames.shape[1]
    block_count = shard_len // BLOCK
    score_scale = 1.0 / math.sqrt(HD)
    seq_ends = jnp.cumsum(seq_lengths[0])
    local_pos = jnp.arange(shard_len, dtype=jnp.int32)
    positions = cycle_place * shard_len + local_pos
    own_docs = doc_numbers(seq_ends, positions)
    table_heads = rel_bias.astype(jnp.float32).T

    def blocked(array):
        return array.reshape((block_count, BLOCK) + array.shape[1:])

    def key_meta(turn):
        source = (cycle_place - turn) % cycle_size
        key_pos = source * shard_len + local_pos
        return (key_pos, doc_numbers(seq_ends, key_pos))

    gathered = (
        lax.all_gather(qkv_weight, ("dp", "blk"), axis=1, tiled=True),
        lax.all_gather(query_value_bias, ("dp", "blk"), axis=0, tiled=True),
        lax.all_gather(out_weight, ("dp", "blk"), axis=1, tiled=True),
        lax.all_gather(out_bias, ("dp", "blk"), axis=0, tiled=True),
        lax.all_gather(up_weight, ("dp", "blk"), axis=1, tiled=True),
        lax.all_gather(up_bias, ("dp", "blk"), axis=0, tiled=True),
        lax.all_gather(down_weight, ("dp", "blk"), axis=1, tiled=True),
        lax.all_gather(down_bias, ("dp", "blk"), axis=0, tiled=True),
        lax.all_gather(first_gain, ("dp", "blk"), axis=0, tiled=True),
        lax.all_gather(first_shift, ("dp", "blk"), axis=0, tiled=True),
        lax.all_gather(second_gain, ("dp", "blk"), axis=0, tiled=True),
        lax.all_gather(second_shift, ("dp", "blk"), axis=0, tiled=True),
    )
    (
        qkv_full,
        qv_bias_full,
        out_full,
        out_bias_full,
        up_full,
        up_bias_full,
        down_full,
        down_bias_full,
        gain_one,
        shift_one,
        gain_two,
        shift_two,
    ) = gathered
    frames_wide = frames.astype(jnp.float32)
    first_out, first_normed, first_inv = layer_norm(
        frames_wide, gain_one.astype(jnp.float32), shift_one.astype(jnp.float32)
    )
    first_low = first_out.astype(jnp.bfloat16)
    projected = jnp.dot(first_low, qkv_full, preferred_element_type=jnp.float32)
    bias_vec = qv_bias_full.astype(jnp.float32)
    queries = (projected[:, :width] + bias_vec[:width]).astype(jnp.bfloat16)
    key_rows = projected[:, width : 2 * width].astype(jnp.bfloat16)
    value_rows = (projected[:, 2 * width :] + bias_vec[width:]).astype(jnp.bfloat16)
    live_rows = key_mask.astype(jnp.bfloat16)
    query_blocks = (blocked(queries), blocked(positions), blocked(own_docs))

    def forward_hop(turn, online_state, key_part, value_part, live_part):
        key_pos, key_doc = key_meta(turn)
        key_items = (
            blocked(key_part),
            blocked(value_part),
            blocked(key_pos),
            blocked(key_doc),
            blocked(live_part),
        )

        def forward_per_query(query_items):
            query_block, query_pos, query_doc, row_peak, row_total, accum = query_items

            def online(carried, key_block_items):
                row_peak, row_total, accum = carried
                key_block, value_block, key_bpos, key_bdoc, key_blive = key_block_items
                logits = pair_logits(
                    query_block,
                    key_block,
                    query_pos,
                    key_bpos,
                    query_doc,
                    key_bdoc,
                    key_blive,
                    table_heads,
                )
                new_peak = jnp.maximum(row_peak, jnp.max(logits, axis=2))
                decay = jnp.exp(row_peak - new_peak)
                weights = jnp.exp(logits - new_peak[:, :, None])
                row_total = row_total * decay + jnp.sum(weights, axis=2)
                accum = accum * decay.T[:, :, None] + jnp.einsum(
                    "hqk,khd->qhd",
                    weights.astype(jnp.bfloat16),
                    value_block.reshape(-1, H, HD),
                    preferred_element_type=jnp.float32,
                )
                return ((new_peak, row_total, accum), None)

            result, unused = lax.scan(online, (row_peak, row_total, accum), key_items)
            return result

        return lax.map(forward_per_query, query_blocks + online_state)

    def cycle_turn(turn, carried):
        online_state, key_part, value_part, live_part = carried
        online_state = forward_hop(turn, online_state, key_part, value_part, live_part)
        key_part, value_part, live_part = from_behind((key_part, value_part, live_part), "blk", 1)
        return (online_state, key_part, value_part, live_part)

    start_state = (
        jnp.full((block_count, H, BLOCK), START_PEAK, jnp.float32),
        jnp.zeros((block_count, H, BLOCK), jnp.float32),
        jnp.zeros((block_count, BLOCK, H, HD), jnp.float32),
    )
    carried = lax.fori_loop(
        0, cycle_size - 1, cycle_turn, (start_state, key_rows, value_rows, live_rows)
    )
    row_peak, row_total, accum = forward_hop(
        cycle_size - 1, carried[0], carried[1], carried[2], carried[3]
    )
    mixed = accum / jnp.transpose(row_total, (0, 2, 1))[:, :, :, None]
    mixed_flat = mixed.reshape(shard_len, width)
    context = mixed_flat.astype(jnp.bfloat16)
    branch = jnp.dot(context, out_full, preferred_element_type=jnp.float32) + out_bias_full.astype(
        jnp.float32
    )
    middle = frames_wide + branch
    second_out, second_normed, second_inv = layer_norm(
        middle, gain_two.astype(jnp.float32), shift_two.astype(jnp.float32)
    )
    second_low = second_out.astype(jnp.bfloat16)
    hidden = jnp.dot(second_low, up_full, preferred_element_type=jnp.float32) + up_bias_full.astype(
        jnp.float32
    )
    active, slope = gelu_parts(hidden)
    active_low = active.astype(jnp.bfloat16)
    layer_out = (
        middle
        + jnp.dot(active_low, down_full, preferred_element_type=jnp.float32)
        + down_bias_full.astype(jnp.float32)
    )
    weights_back = (
        lax.all_gather(qkv_weight, ("dp", "blk"), axis=1, tiled=True),
        lax.all_gather(query_value_bias, ("dp", "blk"), axis=0, tiled=True),
        lax.all_gather(out_weight, ("dp", "blk"), axis=1, tiled=True),
        lax.all_gather(out_bias, ("dp", "blk"), axis=0, tiled=True),
        lax.all_gather(up_weight, ("dp", "blk"), axis=1, tiled=True),
        lax.all_gather(up_bias, ("dp", "blk"), axis=0, tiled=True),
        lax.all_gather(down_weight, ("dp", "blk"), axis=1, tiled=True),
        lax.all_gather(down_bias, ("dp", "blk"), axis=0, tiled=True),
        lax.all_gather(first_gain, ("dp", "blk"), axis=0, tiled=True),
        lax.all_gather(first_shift, ("dp", "blk"), axis=0, tiled=True),
        lax.all_gather(second_gain, ("dp", "blk"), axis=0, tiled=True),
        lax.all_gather(second_shift, ("dp", "blk"), axis=0, tiled=True),
    )
    qkv_back = weights_back[0]
    out_back = weights_back[2]
    up_back = weights_back[4]
    down_back = weights_back[6]
    gain_one_back = weights_back[8].astype(jnp.float32)
    gain_two_back = weights_back[10].astype(jnp.float32)
    grad_wide = cotangent.astype(jnp.float32)
    down_grad = jnp.einsum("tf,td->fd", active_low, cotangent, preferred_element_type=jnp.float32)
    down_bias_grad = jnp.sum(grad_wide, axis=0)
    active_grad = jnp.einsum("td,fd->tf", cotangent, down_back, preferred_element_type=jnp.float32)
    hidden_low = (active_grad * slope).astype(jnp.bfloat16)
    up_grad = jnp.einsum("td,tf->df", second_low, hidden_low, preferred_element_type=jnp.float32)
    up_bias_grad = jnp.sum(hidden_low.astype(jnp.float32), axis=0)
    second_grad = jnp.einsum("tf,df->td", hidden_low, up_back, preferred_element_type=jnp.float32)
    middle_norm, gain_two_grad, shift_two_grad = norm_back(
        second_grad, second_normed, second_inv, gain_two_back
    )
    middle_grad = grad_wide + middle_norm
    branch_low = middle_grad.astype(jnp.bfloat16)
    out_grad = jnp.einsum("td,te->de", context, branch_low, preferred_element_type=jnp.float32)
    out_bias_grad = jnp.sum(branch_low.astype(jnp.float32), axis=0)
    context_low = jnp.einsum(
        "te,de->td", branch_low, out_back, preferred_element_type=jnp.float32
    ).astype(jnp.bfloat16)
    delta = jnp.sum(
        (context_low.astype(jnp.float32) * mixed_flat).reshape(shard_len, H, HD), axis=2
    )
    delta_blocks = jnp.transpose(blocked(delta), (0, 2, 1))
    query_back = (
        blocked(queries),
        blocked(context_low),
        blocked(positions),
        blocked(own_docs),
        row_peak,
        row_total,
        delta_blocks,
    )

    def backward_hop(
        turn, query_grad, table_grad, key_part, value_part, live_part, key_grad, value_grad
    ):
        key_pos, key_doc = key_meta(turn)

        def per_key(carried, key_block_items):
            query_grad, table_grad = carried
            key_block, value_block, key_bpos, key_bdoc, key_blive, key_bgrad, value_bgrad = (
                key_block_items
            )
            key_heads = key_block.reshape(-1, H, HD)
            value_heads = value_block.reshape(-1, H, HD)

            def per_per_query(inner, query_items):
                key_bgrad, value_bgrad, table_grad = inner
                (
                    query_block,
                    dout_block,
                    query_pos,
                    query_doc,
                    peak_block,
                    total_block,
                    delta_block,
                ) = query_items
                logits = pair_logits(
                    query_block,
                    key_block,
                    query_pos,
                    key_bpos,
                    query_doc,
                    key_bdoc,
                    key_blive,
                    table_heads,
                )
                attn_prob = jnp.exp(logits - peak_block[:, :, None]) / total_block[:, :, None]
                dout_heads = dout_block.reshape(-1, H, HD)
                prob_grad = jnp.einsum(
                    "qhd,khd->hqk", dout_heads, value_heads, preferred_element_type=jnp.float32
                )
                logit_grad = attn_prob * (prob_grad - delta_block[:, :, None])
                raw_low = (logit_grad * score_scale).astype(jnp.bfloat16)
                query_part = jnp.einsum(
                    "hqk,khd->qhd", raw_low, key_heads, preferred_element_type=jnp.float32
                ).reshape(-1, width)
                key_bgrad = key_bgrad + jnp.einsum(
                    "hqk,qhd->khd",
                    raw_low,
                    query_block.reshape(-1, H, HD),
                    preferred_element_type=jnp.float32,
                ).reshape(-1, width)
                value_bgrad = value_bgrad + jnp.einsum(
                    "hqk,qhd->khd",
                    attn_prob.astype(jnp.bfloat16),
                    dout_heads,
                    preferred_element_type=jnp.float32,
                ).reshape(-1, width)
                table_grad = table_grad + diagonal_sums(logit_grad, key_bpos[0] - query_pos[0])
                return ((key_bgrad, value_bgrad, table_grad), query_part)

            (key_bgrad, value_bgrad, table_grad), query_parts = lax.scan(
                per_per_query, (key_bgrad, value_bgrad, table_grad), query_back
            )
            return ((query_grad + query_parts, table_grad), (key_bgrad, value_bgrad))

        (query_grad, table_grad), (key_new, value_new) = lax.scan(
            per_key,
            (query_grad, table_grad),
            (
                blocked(key_part),
                blocked(value_part),
                blocked(key_pos),
                blocked(key_doc),
                blocked(live_part),
                blocked(key_grad),
                blocked(value_grad),
            ),
        )
        return (
            query_grad,
            table_grad,
            key_new.reshape(shard_len, width),
            value_new.reshape(shard_len, width),
        )

    def pass_grads(key_grad, value_grad):
        return (
            from_behind(key_grad.astype(jnp.bfloat16), "blk", 1).astype(key_grad.dtype),
            from_behind(value_grad.astype(jnp.bfloat16), "blk", 1).astype(value_grad.dtype),
        )

    def back_turn(turn, carried):
        query_grad, table_grad, key_part, value_part, live_part, key_grad, value_grad = carried
        query_grad, table_grad, key_grad, value_grad = backward_hop(
            turn, query_grad, table_grad, key_part, value_part, live_part, key_grad, value_grad
        )
        key_part, value_part, live_part = from_behind((key_part, value_part, live_part), "blk", 1)
        key_grad, value_grad = pass_grads(key_grad, value_grad)
        return (query_grad, table_grad, key_part, value_part, live_part, key_grad, value_grad)

    zero_rows = jnp.zeros((shard_len, width), jnp.float32)
    back_start = (
        jnp.zeros((block_count, BLOCK, width), jnp.float32),
        jnp.zeros((H, BUCKETS), jnp.float32),
        key_rows,
        value_rows,
        live_rows,
        zero_rows,
        zero_rows,
    )
    carried = lax.fori_loop(0, cycle_size - 1, back_turn, back_start)
    query_grad, table_grad, key_grad, value_grad = backward_hop(
        cycle_size - 1,
        carried[0],
        carried[1],
        carried[2],
        carried[3],
        carried[4],
        carried[5],
        carried[6],
    )
    key_grad, value_grad = pass_grads(key_grad, value_grad)
    query_low = query_grad.reshape(shard_len, width).astype(jnp.bfloat16)
    key_low = key_grad.astype(jnp.bfloat16)
    value_low = value_grad.astype(jnp.bfloat16)
    qkv_low = jnp.concatenate([query_low, key_low, value_low], axis=1)
    qkv_grad = jnp.einsum("td,te->de", first_low, qkv_low, preferred_element_type=jnp.float32)
    query_value_grad = jnp.concatenate(
        [
            jnp.sum(query_low.astype(jnp.float32), axis=0),
            jnp.sum(value_low.astype(jnp.float32), axis=0),
        ]
    )
    first_grad = jnp.einsum("te,de->td", qkv_low, qkv_back, preferred_element_type=jnp.float32)
    frames_norm, gain_one_grad, shift_one_grad = norm_back(
        first_grad, first_normed, first_inv, gain_one_back
    )
    frames_grad = middle_grad + frames_norm
    summed = (
        lax.psum_scatter(qkv_grad, ("dp", "blk"), scatter_dimension=1, tiled=True),
        lax.psum_scatter(query_value_grad, ("dp", "blk"), scatter_dimension=0, tiled=True),
        lax.psum_scatter(out_grad, ("dp", "blk"), scatter_dimension=1, tiled=True),
        lax.psum_scatter(out_bias_grad, ("dp", "blk"), scatter_dimension=0, tiled=True),
        lax.psum_scatter(up_grad, ("dp", "blk"), scatter_dimension=1, tiled=True),
        lax.psum_scatter(up_bias_grad, ("dp", "blk"), scatter_dimension=0, tiled=True),
        lax.psum_scatter(down_grad, ("dp", "blk"), scatter_dimension=1, tiled=True),
        lax.psum_scatter(down_bias_grad, ("dp", "blk"), scatter_dimension=0, tiled=True),
        lax.psum_scatter(gain_one_grad, ("dp", "blk"), scatter_dimension=0, tiled=True),
        lax.psum_scatter(shift_one_grad, ("dp", "blk"), scatter_dimension=0, tiled=True),
        lax.psum_scatter(gain_two_grad, ("dp", "blk"), scatter_dimension=0, tiled=True),
        lax.psum_scatter(shift_two_grad, ("dp", "blk"), scatter_dimension=0, tiled=True),
    )
    table_sum = lax.psum(table_grad, ("dp", "blk"))
    return (
        layer_out,
        frames_grad,
        summed[0],
        summed[1],
        summed[2],
        summed[3],
        summed[4],
        summed[5],
        summed[6],
        summed[7],
        summed[8],
        summed[9],
        summed[10],
        summed[11],
        table_sum.T,
    )


def solution(mesh):
    placed = (
        P(("dp", "blk"), None),
        P(("dp", "blk"), None),
        P("dp", None),
        P(("dp", "blk")),
        P(None, ("dp", "blk")),
        P(("dp", "blk")),
        P(None, ("dp", "blk")),
        P(("dp", "blk")),
        P(None, ("dp", "blk")),
        P(("dp", "blk")),
        P(None, ("dp", "blk")),
        P(("dp", "blk")),
        P(("dp", "blk")),
        P(("dp", "blk")),
        P(("dp", "blk")),
        P(("dp", "blk")),
        P(),
    )
    return jax.shard_map(
        body,
        mesh=mesh,
        in_specs=placed,
        out_specs=(
            P(("dp", "blk"), None),
            P(("dp", "blk"), None),
            P(None, ("dp", "blk")),
            P(("dp", "blk")),
            P(None, ("dp", "blk")),
            P(("dp", "blk")),
            P(None, ("dp", "blk")),
            P(("dp", "blk")),
            P(None, ("dp", "blk")),
            P(("dp", "blk")),
            P(("dp", "blk")),
            P(("dp", "blk")),
            P(("dp", "blk")),
            P(("dp", "blk")),
            P(),
        ),
        check_vma=False,
    )
```

profile of v0, /device:TPU:0, one launch (start us, length us, event | category | flops | bytes accessed | tf_op | source)
XLA Modules:
  0.0 1129.1 jit_solution(2441477048410347644)
XLA Ops:
  10.1 2.9 collective-permute-start
  14.5 217.1 %gather_fusion.1 = f32[65536,12]{1,0:T(8,128)} fusion(f32[12,321]{0,1:T(8,128)S(1)} %bitcast.137, s32[65536]{0:T(1024)S(1)} %broadcast_clamp_fusion), kind=kCustom, calls=%fused_computation.1.clone | custom fusion | bytes 6553600 | tf_op jit(solution)/shard_map/while/body/eval_jaxpr/while/body/eval_jaxpr/jit(_take)/gather | solution.py:65
  231.6 20.7 %copy.131 = f32[256,256,12]{0,1,2:T(8,128)} copy(f32[256,256,12]{2,1,0:T(8,128)} %bitcast.140) | data formatting | bytes 6291456 | tf_op jit(solution)/shard_map/while/body/eval_jaxpr/while/body/eval_jaxpr/jit(_take)/gather | solution.py:65
  254.4 40.1 %all-reduce.19 = (bf16[768]{0:T(1024)(128)(2,1)S(1)}, bf16[768]{0:T(1024)(128)(2,1)S(1)}, bf16[768]{0:T(1024)(128)(2,1)S(1)}, bf16[1536]{0:T(1024)(128)(2,1)S(1)...) all-reduce(bf16[768]{0:T(1024)(128)(2,1)S(1)} %dynamic-update-slice, ...), channel_id=1, replica_groups=mesh['dp'=16,'blk'=2] {'dp','blk'}, use_global_device_ids=true, to_apply=%add.5 | all-reduce | flops 9216 | bytes 36864
  294.7 217.1 %gather_fusion = f32[65536,12]{1,0:T(8,128)} fusion(f32[12,321]{0,1:T(8,128)S(1)} %bitcast.138, s32[65536]{0:T(1024)S(1)} %broadcast_clamp_fusion.1), kind=kCustom, calls=%fused_computation.clone | custom fusion | bytes 6553600 | tf_op jit(solution)/shard_map/while/body/eval_jaxpr/while/body/eval_jaxpr/while/body/eval_jaxpr/jit(_take)/gather | solution.py:65
  512.4 20.5 %copy.124 = f32[256,256,12]{0,1,2:T(8,128)} copy(f32[256,256,12]{2,1,0:T(8,128)} %bitcast.139) | data formatting | bytes 6291456 | tf_op jit(solution)/shard_map/while/body/eval_jaxpr/while/body/eval_jaxpr/while/body/eval_jaxpr/jit(_take)/gather | solution.py:65
  538.8 3.2 fusion.103
  542.8 2.3 collective-permute-start.1
  545.1 2.0 copy.120
  547.9 1.9 copy.125
  550.0 2.9 fusion.108
  552.9 2.5 collective-permute-done.1
  555.4 1.9 copy.128
  557.3 4.9 collective-permute-done.2
  562.2 2.0 copy.132
  564.2 2.9 fusion.107
  569.1 1.5 fusion.31
  570.7 2.3 copy.135
  573.0 2.2 fusion.109
  577.6 6.2 multiply_convert_fusion.2
  583.9 6.3 convert_reduce_fusion
  590.2 2.6 multiply_reduce_fusion
  594.7 1.9 fusion.81
  596.6 2.8 convolution_convert_fusion.1
  599.3 1.9 copy.134
  601.3 2.2 convert_multiply_fusion
  603.4 2.3 copy.136
  605.8 1.8 reduce_sum.264
  607.6 2.5 fusion.42
  610.1 2.6 subtract_multiply_fusion.1
  612.7 1.7 collective-permute-start.5
  614.6 2.8 fusion.16
  621.1 3.1 collective-permute-done.5
  625.4 2.4 collective-permute-start.6
  627.8 4.7 collective-permute-done.3
  632.7 2.4 collective-permute-start.4
  636.6 4.4 collective-permute-done.6
  641.0 6.8 collective-permute-done.4
  648.5 4.1 fusion.69
  654.3 5.2 fusion.105
  659.6 1.3 copy-done.16
  661.0 5.1 fusion.110
  670.8 1.2 convert_element_type.211
  672.1 17.6 %rev.11 = f32[12,256,256]{1,2,0:T(8,128)} reverse(f32[12,256,256]{1,2,0:T(8,128)S(1)} %copy-done.3), dimensions={1} | reverse | bytes 6291456 | tf_op jit(solution)/shard_map/while/body/eval_jaxpr/while/body/eval_jaxpr/while/body/eval_jaxpr/rev | solution.py:74
  689.6 22.4 %rev.12 = f32[12,256,256]{1,2,0:T(8,128)S(1)} reverse(f32[12,256,256]{1,2,0:T(8,128)} %copy-done.4), dimensions={1} | reverse | bytes 6291456 | tf_op jit(solution)/shard_map/while/body/eval_jaxpr/while/body/eval_jaxpr/rev | solution.py:74
  712.0 3.5 copy.161
  715.5 2.7 pad.12.clone
  719.2 4.9 copy.165
  724.1 3.9 slice.66
  728.0 9.1 reshape.683
  737.1 4.3 reduce_sum.277
  741.4 2.6 copy.162
  744.1 2.8 pad.13.clone
  747.9 4.9 copy.166
  752.7 3.9 slice.67
  756.7 9.4 reshape.685
  766.1 3.6 reduce_sum.278
  771.3 4.8 fusion.41
  776.5 1.4 fusion.60
  777.9 41.4 %all-reduce.18 = (f32[1536]{0:T(1024)S(1)}, f32[768]{0:T(1024)S(1)}, f32[3072]{0:T(1024)S(1)}, f32[768]{0:T(1024)S(1)}, f32[768]{0:T(1024)S(1)}, /*index=5*/f32[...) all-reduce(f32[1536]{0:T(1024)S(1)} %pad_maximum_fusion.3, ...), channel_id=3, replica_groups=mesh['dp'=16,'blk'=2] {'dp','blk'}, use_global_device_ids=true, to_apply=%region_20.22.clone | all-reduce | flops 13068 | bytes 104544
  824.0 1.2 fusion.59
  825.1 13.4 %reduce-scatter.5.cloned.1.call-done = f32[768,72]{0,1:T(8,128)} async-done(((f32[768,2304]{0,1:T(8,128)}), f32[768,72]{0,1:T(8,128)}) %reduce-scatter.5.cloned.1.call-update) | async-done | bytes 221200 | tf_op jit(solution)/shard_map/reduce_scatter | solution.py:436
  838.5 141.4 %reduce-scatter.9.cloned.1.call-done = f32[768,96]{0,1:T(8,128)} async-done(((f32[768,3072]{0,1:T(8,128)}), f32[768,96]{0,1:T(8,128)}) %reduce-scatter.9.cloned.1.call-update) | async-done | bytes 294928 | tf_op jit(solution)/shard_map/reduce_scatter | solution.py:440
  979.9 141.9 %reduce-scatter.11.cloned.1.call-done = f32[3072,24]{0,1:T(8,128)} async-done(((f32[3072,768]{0,1:T(8,128)}), f32[3072,24]{0,1:T(8,128)}) %reduce-scatter.11.cloned.1.call-update) | async-done | bytes 294928 | tf_op jit(solution)/shard_map/reduce_scatter | solution.py:442
  (286 shorter events, 40.5 us)
Async XLA Ops:
  7.2 531.6 %all-gather.5.cloned.1.call-start = ((), (), s32[]{:S(2)}) async-start(), calls=%async_computation.4 | async-start | bytes 3649536 | tf_op jit(solution)/shard_map/all_gather | solution.py:125
  7.9 565.1 %all-gather.7.cloned.1.call-start = ((), (), s32[]{:S(2)}) async-start(), calls=%async_computation.5 | async-start | bytes 1216512 | tf_op jit(solution)/shard_map/all_gather | solution.py:127
  8.7 568.9 %all-gather.9.cloned.1.call-start = ((), (), s32[]{:S(2)}) async-start(), calls=%async_computation.6 | async-start | bytes 4866048 | tf_op jit(solution)/shard_map/all_gather | solution.py:129
  9.4 574.4 %all-gather.11.cloned.1.call-start = ((), (), s32[]{:S(2)}) async-start(), calls=%async_computation.7 | async-start | bytes 4866048 | tf_op jit(solution)/shard_map/all_gather | solution.py:131
  10.1 525.1 %collective-permute-start = (bf16[256]{0:T(256)(128)(2,1)S(1)}, bf16[256]{0:T(256)(128)(2,1)S(1)}, u32[]{:S(2)}, u32[]{:S(2)}) collective-permute-start(bf16[256]{0:T(256)(128)(2,1)S(1)} %get-tuple-element.692), channel_id=1, source_target_pairs={{1,0},{0,1},{3,2},{2,3},{5,4},{4,5},{7,6},{6,7},{9,8},{8,9},{11,10... | collective-permute-start | bytes 1544 | tf_op jit(solution)/shard_map/while/body/eval_jaxpr/ppermute | solution.py:24
  13.1 812.1 %reduce-scatter.7.cloned.1.call-start = ((), (), s32[]{:S(2)}) async-start(), calls=%async_computation.9 | async-start | bytes 2433024 | tf_op jit(solution)/shard_map/reduce_scatter | solution.py:438
  13.2 522.0 %copy-start.72 = (s32[256]{0:T(256)}, s32[256]{0:T(256)S(1)}, u32[]{:S(2)}) copy-start(s32[256]{0:T(256)S(1)} %iota_add_fusion.2) | copy-start | bytes 3076
  13.2 522.0 %copy-start.60 = (s32[256]{0:T(256)}, s32[256]{0:T(256)S(1)}, u32[]{:S(2)}) copy-start(s32[256]{0:T(256)S(1)} %get-tuple-element.722) | copy-start | bytes 3076
  13.2 522.0 %copy-start.62 = (s32[256]{0:T(256)}, s32[256]{0:T(256)S(1)}, u32[]{:S(2)}) copy-start(s32[256]{0:T(256)S(1)} %get-tuple-element.723) | copy-start | bytes 3076
  231.6 20.8 %copy-start.78 = (s32[1,4]{1,0:T(1,128)S(1)}, s32[1,4]{1,0:T(1,128)}, u32[]{:S(2)}) copy-start(s32[1,4]{1,0:T(1,128)} %param.21) | copy-start | bytes 52
  231.6 20.9 %copy-start.79 = (bf16[24]{0:T(256)(128)(2,1)S(1)}, bf16[24]{0:T(256)(128)(2,1)}, u32[]{:S(2)}) copy-start(bf16[24]{0:T(256)(128)(2,1)} %param.31) | copy-start | bytes 148
  231.6 21.2 %copy-start.80 = (bf16[24]{0:T(256)(128)(2,1)S(1)}, bf16[24]{0:T(256)(128)(2,1)}, u32[]{:S(2)}) copy-start(bf16[24]{0:T(256)(128)(2,1)} %param.32) | copy-start | bytes 148
  231.6 21.4 %copy-start.81 = (bf16[24]{0:T(256)(128)(2,1)S(1)}, bf16[24]{0:T(256)(128)(2,1)}, u32[]{:S(2)}) copy-start(bf16[24]{0:T(256)(128)(2,1)} %param.26) | copy-start | bytes 148
  231.6 21.6 %copy-start.82 = (bf16[24]{0:T(256)(128)(2,1)S(1)}, bf16[24]{0:T(256)(128)(2,1)}, u32[]{:S(2)}) copy-start(bf16[24]{0:T(256)(128)(2,1)} %param.33) | copy-start | bytes 148
  231.6 21.8 %copy-start.83 = (bf16[24]{0:T(256)(128)(2,1)S(1)}, bf16[24]{0:T(256)(128)(2,1)}, u32[]{:S(2)}) copy-start(bf16[24]{0:T(256)(128)(2,1)} %param.34) | copy-start | bytes 148
  231.6 22.1 %copy-start.84 = (bf16[24]{0:T(256)(128)(2,1)S(1)}, bf16[24]{0:T(256)(128)(2,1)}, u32[]{:S(2)}) copy-start(bf16[24]{0:T(256)(128)(2,1)} %param.30) | copy-start | bytes 148
  231.6 22.3 %copy-start.85 = (bf16[96]{0:T(256)(128)(2,1)S(1)}, bf16[96]{0:T(256)(128)(2,1)}, u32[]{:S(2)}) copy-start(bf16[96]{0:T(256)(128)(2,1)} %param.28) | copy-start | bytes 580
  231.6 22.5 %copy-start.86 = (bf16[48]{0:T(256)(128)(2,1)S(1)}, bf16[48]{0:T(256)(128)(2,1)}, u32[]{:S(2)}) copy-start(bf16[48]{0:T(256)(128)(2,1)} %param.24) | copy-start | bytes 292
  294.5 244.3 %copy-start.45 = (f32[768]{0:T(1024)}, f32[768]{0:T(1024)S(1)}, u32[]{:S(2)}) copy-start(f32[768]{0:T(1024)S(1)} %convert_element_type.195) | copy-start | bytes 9220
  294.5 244.3 %copy-start.53 = (f32[768]{0:T(1024)}, f32[768]{0:T(1024)S(1)}, u32[]{:S(2)}) copy-start(f32[768]{0:T(1024)S(1)} %convert_element_type.196) | copy-start | bytes 9220
  294.7 217.2 %copy-start.12 = (bf16[256,768]{1,0:T(8,128)(2,1)S(1)}, bf16[256,768]{1,0:T(8,128)(2,1)}, u32[]{:S(2)}) copy-start(bf16[256,768]{1,0:T(8,128)(2,1)} %param.19) | copy-start | bytes 1179652
  512.1 26.7 %copy-start.55 = (f32[256]{0:T(256)}, f32[256]{0:T(256)S(1)}, u32[]{:S(2)}) copy-start(f32[256]{0:T(256)S(1)} %broadcast_multiply_fusion.5) | copy-start | bytes 3076
  512.3 26.5 %copy-start.69 = (f32[256]{0:T(256)}, f32[256]{0:T(256)S(1)}, u32[]{:S(2)}) copy-start(f32[256]{0:T(256)S(1)} %add_rsqrt_fusion.1) | copy-start | bytes 3076
  542.8 12.6 %collective-permute-start.1 = (bf16[256,768]{1,0:T(8,128)(2,1)}, bf16[256,768]{1,0:T(8,128)(2,1)}, u32[]{:S(2)}, u32[]{:S(2)}) collective-permute-start(bf16[256,768]{1,0:T(8,128)(2,1)} %slice.75), channel_id=1, source_target_pairs={{1,0},{0,1},{3,2},{2,3},{5,4},{4,5},{7,6},{6,7},{9,8},{8,9},{11,10... | collective-permute-start | bytes 1179656 | tf_op jit(solution)/shard_map/while/body/eval_jaxpr/ppermute | solution.py:24
  549.8 12.4 %collective-permute-start.2 = (bf16[256,768]{1,0:T(8,128)(2,1)}, bf16[256,768]{1,0:T(8,128)(2,1)}, u32[]{:S(2)}, u32[]{:S(2)}) collective-permute-start(bf16[256,768]{1,0:T(8,128)(2,1)} %get-tuple-element.694), channel_id=1, source_target_pairs={{1,0},{0,1},{3,2},{2,3},{5,4},{4,5},{7,6},{6,7},{9,8},{8,9},{11,10... | collective-permute-start | bytes 1179656 | tf_op jit(solution)/shard_map/while/body/eval_jaxpr/ppermute | solution.py:24
  573.0 3.9 copy-start.31
  573.0 3.9 copy-start.42
  573.0 3.9 copy-start.44
  583.8 6.3 copy-start.6
  583.8 6.3 copy-start.36
  583.8 6.3 copy-start.48
  583.8 6.3 copy-start.51
  583.8 6.3 copy-start.76
  612.7 11.5 %collective-permute-start.5 = (bf16[256,768]{0,1:T(8,128)(2,1)}, bf16[256,768]{0,1:T(8,128)(2,1)}, u32[]{:S(2)}, u32[]{:S(2)}) collective-permute-start(bf16[256,768]{0,1:T(8,128)(2,1)} %bitcast.35), channel_id=1, source_target_pairs={{1,0},{0,1},{3,2},{2,3},{5,4},{4,5},{7,6},{6,7},{9,8},{8,9},{11,10... | collective-permute-start | bytes 1179656 | tf_op jit(solution)/shard_map/while/body/eval_jaxpr/ppermute | solution.py:24
  614.5 224.0 %reduce-scatter.5.cloned.1.call-start = ((), (), s32[]{:S(2)}) async-start(), calls=%async_computation.8 | async-start | bytes 7299072 | tf_op jit(solution)/shard_map/reduce_scatter | solution.py:436
  614.6 3.1 copy-start.35
  614.6 3.1 copy-start.40
  619.6 15.9 %copy-start.4 = (f32[12,256,256]{1,2,0:T(8,128)}, f32[12,256,256]{1,2,0:T(8,128)S(1)}, u32[]{:S(2)}) copy-start(f32[12,256,256]{1,2,0:T(8,128)S(1)} %subtract_multiply_fusion) | copy-start | bytes 9437188
  620.2 14.9 %copy-start.14 = (bf16[256,768]{0,1:T(8,128)(2,1)S(1)}, bf16[256,768]{0,1:T(8,128)(2,1)}, u32[]{:S(2)}) copy-start(bf16[256,768]{0,1:T(8,128)(2,1)} %copy.120) | copy-start | bytes 1179652
  620.2 12.3 %collective-permute-start.3 = (bf16[256,768]{0,1:T(8,128)(2,1)S(1)}, bf16[256,768]{0,1:T(8,128)(2,1)S(1)}, u32[]{:S(2)}, u32[]{:S(2)}) collective-permute-start(bf16[256,768]{0,1:T(8,128)(2,1)S(1)} %bitcast.169), channel_id=1, source_target_pairs={{1,0},{0,1},{3,2},{2,3},{5,4},{4,5},{7,6},{6,7},{9,8},{8,9},{11,10... | collective-permute-start | bytes 1179656 | tf_op jit(solution)/shard_map/while/body/eval_jaxpr/ppermute | solution.py:24
  625.4 10.1 copy-start.15
  625.4 15.6 %collective-permute-start.6 = (bf16[256,768]{0,1:T(8,128)(2,1)S(1)}, bf16[256,768]{0,1:T(8,128)(2,1)S(1)}, u32[]{:S(2)}, u32[]{:S(2)}) collective-permute-start(bf16[256,768]{0,1:T(8,128)(2,1)S(1)} %fusion.64), channel_id=1, source_target_pairs={{1,0},{0,1},{3,2},{2,3},{5,4},{4,5},{7,6},{6,7},{9,8},{8,9},{11,10... | collective-permute-start | bytes 1179656 | tf_op jit(solution)/shard_map/ppermute | solution.py:24
  632.7 15.1 %collective-permute-start.4 = (bf16[256,768]{0,1:T(8,128)(2,1)S(1)}, bf16[256,768]{0,1:T(8,128)(2,1)S(1)}, u32[]{:S(2)}, u32[]{:S(2)}) collective-permute-start(bf16[256,768]{0,1:T(8,128)(2,1)S(1)} %fusion.65), channel_id=1, source_target_pairs={{1,0},{0,1},{3,2},{2,3},{5,4},{4,5},{7,6},{6,7},{9,8},{8,9},{11,10... | collective-permute-start | bytes 1179656 | tf_op jit(solution)/shard_map/ppermute | solution.py:24
  635.5 13.0 %copy-start.13 = (bf16[256,768]{1,0:T(8,128)(2,1)S(1)}, bf16[256,768]{1,0:T(8,128)(2,1)}, u32[]{:S(2)}) copy-start(bf16[256,768]{1,0:T(8,128)(2,1)} %param.19) | copy-start | bytes 1179652
  635.5 13.0 %copy-start.46 = (f32[768]{0:T(1024)S(1)}, f32[768]{0:T(1024)}, u32[]{:S(2)}) copy-start(f32[768]{0:T(1024)} %copy-done.45) | copy-start | bytes 9220
  635.5 13.0 %copy-start.54 = (f32[768]{0:T(1024)S(1)}, f32[768]{0:T(1024)}, u32[]{:S(2)}) copy-start(f32[768]{0:T(1024)} %copy-done.53) | copy-start | bytes 9220
  635.5 13.0 %copy-start.56 = (f32[256]{0:T(256)S(1)}, f32[256]{0:T(256)}, u32[]{:S(2)}) copy-start(f32[256]{0:T(256)} %copy-done.55) | copy-start | bytes 3076
  635.5 13.0 %copy-start.70 = (f32[256]{0:T(256)S(1)}, f32[256]{0:T(256)}, u32[]{:S(2)}) copy-start(f32[256]{0:T(256)} %copy-done.69) | copy-start | bytes 3076
  636.6 11.1 copy-start.18
  641.0 6.8 copy-start.20
  652.7 327.2 %reduce-scatter.9.cloned.1.call-start = ((), (), s32[]{:S(2)}) async-start(), calls=%async_computation.10 | async-start | bytes 9732096 | tf_op jit(solution)/shard_map/reduce_scatter | solution.py:440
  659.6 462.3 %reduce-scatter.11.cloned.1.call-start = ((), (), s32[]{:S(2)}) async-start(), calls=%async_computation.11 | async-start | bytes 9732096 | tf_op jit(solution)/shard_map/reduce_scatter | solution.py:442
  666.1 6.0 copy-start.3
  766.0 3.7 copy-start.50
  766.1 3.8 copy-start.49
  766.1 5.2 copy-start.8
  766.1 5.2 copy-start.17
  771.3 4.8 copy-start.21
  771.3 5.0 copy-start.19
  771.3 5.0 copy-start.33
  771.3 5.0 copy-start.57
  771.3 5.0 copy-start.71
  771.3 5.0 copy-start.77
  776.4 47.5 %copy-start.11 = (f32[256,768]{1,0:T(8,128)S(1)}, f32[256,768]{1,0:T(8,128)}, u32[]{:S(2)}) copy-start(f32[256,768]{1,0:T(8,128)} %copy-done.10) | copy-start | bytes 2359300
  (38 other events, 68.4 us)
Sparse Core Ops, SparseCore 0:
  10.9 62.8 all-gather.4
  76.8 52.9 all-gather.6
  132.7 62.5 all-gather.8
  198.0 62.4 all-gather.10
  614.6 97.9 reduce-scatter.6
  719.7 118.7 reduce-scatter.4
  845.0 134.8 reduce-scatter.8
  987.4 134.4 reduce-scatter.10
where the time goes:
time: 1140 us; the launch traced here: 1130 us
  local copies, waits for them, and re-layouts  601 us (53%)
  waiting for transfers between devices  325 us (29%)
  blocking collectives  81.5 us (7%)
  matrix products  66.7 us (6%)
  other arithmetic  24.4 us (2%)
  between operations  18.3 us (2%)
  starting transfers between devices  12.4 us (1%)
    gather x4, local copies, waits for them, and re-layouts, pair_logits(): bias = jnp.take(table_heads, relative, axis=1)  475 us
    reduce_scatter x1, waiting for transfers between devices, body(): lax.psum_scatter(down_grad, ('dp', 'blk'), scatter_dimension=1, tiled=True)  142 us
    reduce_scatter x1, waiting for transfers between devices, body(): lax.psum_scatter(up_grad, ('dp', 'blk'), scatter_dimension=1, tiled=True)  141 us
    unnamed x2, blocking collectives  81.5 us
    rev x2, local copies, waits for them, and re-layouts, diagonal_sums(): flipped = gradient[:, ::-1, :]  39.9 us
    unnamed x206, local copies, waits for them, and re-layouts  32.6 us
    ppermute x7, waiting for transfers between devices, from_behind(): return lax.ppermute(block, axis, route)  26.4 us
  transfers between devices with their start and end apart: 15, of which 9 were waited for; matrix products, arithmetic and copies ran while one was open for 58% of the time, Pallas kernels for 0%

commit v1 on v0

--- a/solution.py
+++ b/solution.py
@@ -2,7 +2,10 @@
 
 import jax
 import jax.numpy as jnp
+import numpy as np
 from jax import lax
+from jax.experimental import pallas as pl
+from jax.experimental.pallas import tpu as pltpu
 from jax.sharding import PartitionSpec as P
 
 H = 12
@@ -466,6 +469,741 @@
     )
 
 
+AXES = ("dp", "blk")
+VMEM_BYTES = 56 * 1024 * 1024
+F32 = jnp.float32
+LOW = jnp.bfloat16
+LANES = 128
+NARROW = 6
+PAD = 8
+
+
+def route(move):
+    n_dp, n_blk = lax.axis_size("dp"), lax.axis_size("blk")
+    pairs = []
+    for d in range(n_dp):
+        d_bits, b_bits = move[d % 2]
+        for b in range(n_blk):
+            pairs.append((d * n_blk + b, (d ^ d_bits) * n_blk + (b ^ b_bits)))
+    return pairs
+
+
+def shift(array, move):
+    return lax.ppermute(array, AXES, route(move))
+
+
+CORE = ((1, 0), (1, 0))
+SIDE = ((0, 1), (2, 0))
+OTHER_SIDE = ((2, 0), (0, 1))
+PACK = ((0, 1), (0, 1))
+NEAR_Z = ((4, 0), (8, 0))
+FAR_Z = ((12, 0), (12, 0))
+
+
+def gather_units(unit, core):
+    first = core == 0
+    twin = shift(unit, CORE)
+    far = shift(unit, FAR_Z)
+    both = jnp.where(first, jnp.stack([unit, twin]), jnp.stack([twin, unit]))
+    near = shift(both, NEAR_Z)
+    far_twin = shift(far, CORE)
+    near_twin = shift(near, CORE)
+    column = jnp.where(
+        first,
+        jnp.stack([both, near, near_twin, jnp.stack([far, far_twin])], axis=1),
+        jnp.stack([both, near_twin, near, jnp.stack([far_twin, far])], axis=1),
+    )
+    side = shift(column, SIDE)
+    corner = shift(lax.dynamic_index_in_dim(side, core, 0, keepdims=False), OTHER_SIDE)
+    return (column, side, shift(side, CORE), corner, shift(corner, CORE))
+
+
+def scatter_units(parts, core):
+    corner_send, corner_keep, side_send, side_keep, own = parts
+    corner_got = shift(corner_send, CORE)
+    side_got = shift(side_send, CORE)
+    corner = (corner_keep.astype(F32) + corner_got.astype(F32)).astype(LOW)
+    turned = shift(corner, OTHER_SIDE)
+    plane = (jnp.arange(2) == core)[:, None, None, None]
+    side = (
+        side_keep.astype(F32)
+        + side_got.astype(F32)
+        + jnp.where(plane, turned[None].astype(F32), 0.0)
+    ).astype(LOW)
+    column = (own.astype(F32) + shift(side, SIDE).astype(F32)).astype(LOW)
+    of_first = jnp.stack([column[0, 1], column[1, 1], column[0, 3], column[0, 0]])
+    of_second = jnp.stack([column[0, 2], column[1, 2], column[1, 3], column[1, 0]])
+    first = core == 0
+    got = shift(jnp.where(first, of_second, of_first), CORE)
+    total = jnp.where(first, of_first, of_second).astype(F32) + got.astype(F32)
+    total_low = total.astype(LOW)
+    near = shift(total_low[:2], NEAR_Z)
+    far = shift(total_low[2], FAR_Z)
+    near_twin = shift(lax.dynamic_index_in_dim(near, 1 - core, 0, keepdims=False), CORE)
+    near_own = lax.dynamic_index_in_dim(near, core, 0, keepdims=False)
+    return total[3] + near_own.astype(F32) + far.astype(F32) + near_twin.astype(F32)
+
+
+def unit_of(place, x_turn, y_turn, z_turn, c):
+    x, y, z = place[0] ^ x_turn, place[1] ^ y_turn, place[2] ^ z_turn
+    return ((z * 2 + y) * 2 + c) * 2 + x
+
+
+def gathered_copies(place, pieces):
+    column, side, side_twin, corner, corner_twin = pieces
+    c0 = place[3]
+    found = []
+    for z in range(4):
+        for c in range(2):
+            found.append((column.at[c, z], unit_of(place, 0, 0, z, c)))
+            found.append((side.at[c, z], unit_of(place, 1 - c0, c0, z, c)))
+            found.append((side_twin.at[c, z], unit_of(place, c0, 1 - c0, z, c)))
+        found.append((corner.at[z], unit_of(place, 1, 1, z, c0)))
+        found.append((corner_twin.at[z], unit_of(place, 1, 1, z, 1 - c0)))
+    return found
+
+
+def scattered_copies(place, parts):
+    corner_send, corner_keep, side_send, side_keep, own = parts
+    c0 = place[3]
+    found = []
+    for z in range(4):
+        for c in range(2):
+            found.append((own.at[c, z], unit_of(place, 0, 0, z, c)))
+            found.append((side_keep.at[c, z], unit_of(place, 1 - c0, c0, z, c)))
+            found.append((side_send.at[c, z], unit_of(place, c0, 1 - c0, z, c)))
+        found.append((corner_keep.at[z], unit_of(place, 1, 1, z, c0)))
+        found.append((corner_send.at[z], unit_of(place, 1, 1, z, 1 - c0)))
+    return found
+
+
+def load_units(place, pieces, stage, sems):
+    copies = [
+        pltpu.make_async_copy(ref, stage.at[unit], sems.at[n])
+        for n, (ref, unit) in enumerate(gathered_copies(place, pieces))
+    ]
+    for copy in copies:
+        copy.start()
+    return copies
+
+
+def store_units(place, stage, parts, sems):
+    copies = [
+        pltpu.make_async_copy(stage.at[unit], ref, sems.at[n])
+        for n, (ref, unit) in enumerate(scattered_copies(place, parts))
+    ]
+    for copy in copies:
+        copy.start()
+    for copy in copies:
+        copy.wait()
+
+
+def part_shapes(rows, width):
+    quarter = jax.ShapeDtypeStruct((4, rows, width), LOW)
+    half = jax.ShapeDtypeStruct((2, 4, rows, width), LOW)
+    return [quarter, quarter, half, half, half]
+
+
+def dot_nn(a, b):
+    return lax.dot_general(a, b, (((1,), (0,)), ((), ())), preferred_element_type=F32)
+
+
+def dot_nt(a, b):
+    return lax.dot_general(a, b, (((1,), (1,)), ((), ())), preferred_element_type=F32)
+
+
+def dot_tn(a, b):
+    return lax.dot_general(a, b, (((0,), (0,)), ((), ())), preferred_element_type=F32)
+
+
+ANY = pl.BlockSpec(memory_space=pl.ANY)
+SMEM = pl.BlockSpec(memory_space=pltpu.SMEM)
+VMEM = pl.BlockSpec(memory_space=pltpu.VMEM)
+
+
+def call(kernel, in_specs, outs, out_specs, scratch, args, flops, **kwargs):
+    moved = sum(math.prod(a.shape) * a.dtype.itemsize for a in list(args) + list(outs))
+    return pl.pallas_call(
+        kernel,
+        out_shape=outs,
+        in_specs=in_specs,
+        out_specs=out_specs,
+        scratch_shapes=scratch,
+        compiler_params=pltpu.CompilerParams(vmem_limit_bytes=VMEM_BYTES),
+        cost_estimate=pl.CostEstimate(flops=flops, bytes_accessed=moved, transcendentals=0),
+        **kwargs,
+    )(*args)
+
+
+def spread_tables(units, width):
+    tables = []
+    for n in (width // units, 2 * width // units, 4 * width // units):
+        lane = np.arange(units * n)
+        keep = lane[None, :] // n == np.arange(units)[:, None]
+        pick = lane[None, :] % n == np.arange(LANES)[:, None]
+        tables.append(jnp.asarray(np.concatenate([keep, pick]), LOW))
+    return tables
+
+
+def project_kernel(
+    place, own, mate, column, side, side_twin, corner, corner_twin, wide_one, wide_two, wide_four,
+    first, queries, keys, values, weight, vectors, up_bias, stage, small, sems,
+):
+    units = stage.shape[0]
+    width = own.shape[1]
+    rows = stage.shape[1] - PAD
+    shard_len = own.shape[0]
+    copies = load_units(place, (column, side, side_twin, corner, corner_twin), stage, sems)
+
+    def normed(frames):
+        wide = frames.astype(F32)
+        center = wide - jnp.mean(wide, axis=1, keepdims=True)
+        return center * lax.rsqrt(jnp.mean(center * center, axis=1, keepdims=True) + EPSILON)
+
+    own_normed, mate_normed = normed(own[...]), normed(mate[...])
+    for copy in copies:
+        copy.wait()
+    for unit in range(units):
+        top = stage[unit, rows : rows + PAD, :].astype(F32)
+        small[0, unit : unit + 1, :] = top[0:1]
+        small[1, unit : unit + 1, :] = top[1:2]
+
+    def spread(row, slot, table):
+        held = small[row, :, slot * LANES : (slot + 1) * LANES].astype(LOW)
+        laid = dot_nn(held, table[units:, :]) * table[:units, :].astype(F32)
+        return jnp.sum(laid, axis=0, keepdims=True)
+
+    for n in range(NARROW):
+        vectors[n : n + 1, :] = spread(0, n, wide_one)
+    qv_bias = spread(1, 0, wide_two)
+    up_bias[...] = jnp.broadcast_to(spread(1, 1, wide_four), up_bias.shape)
+    vectors[NARROW : NARROW + 1, :] = qv_bias[:, :width]
+    vectors[NARROW + 1 : NARROW + 2, :] = qv_bias[:, width:]
+    for pair in range(units // 2):
+        joined = jnp.concatenate(
+            [stage[2 * pair, :rows, :].astype(F32), stage[2 * pair + 1, :rows, :].astype(F32)], axis=0
+        )
+        weight[2 * rows * pair : 2 * rows * (pair + 1), :] = joined.astype(LOW)
+    gain, offset = vectors[0:1, :], vectors[1:2, :]
+    x = place[0]
+    own_at = pl.multiple_of(x * shard_len, shard_len)
+    mate_at = pl.multiple_of((1 - x) * shard_len, shard_len)
+    first[pl.ds(own_at, shard_len), :] = (own_normed * gain + offset).astype(LOW)
+    first[pl.ds(mate_at, shard_len), :] = (mate_normed * gain + offset).astype(LOW)
+    mine = first[pl.ds(own_at, shard_len), :]
+    queries[...] = (dot_nt(mine, weight[:width, :]) + vectors[NARROW : NARROW + 1, :]).astype(LOW)
+    keys[...] = dot_nt(first[...], weight[width : 2 * width, :]).astype(LOW)
+    values[...] = (
+        dot_nt(first[...], weight[2 * width :, :]) + vectors[NARROW + 1 : NARROW + 2, :]
+    ).astype(LOW)
+
+
+def half_mask(shape, head):
+    return (lax.broadcasted_iota(jnp.int32, shape, 1) // HD) == head
+
+
+def attend_kernel(place, queries, keys, values, curve, hidden_pairs, probs, mixed):
+    q, k, v = queries[...], keys[...], values[...]
+    block_len, span = hidden_pairs.shape
+    total = jnp.zeros(q.shape, F32)
+    for head in range(2):
+        q_head = jnp.where(half_mask(q.shape, head), q, 0) * (1.0 / math.sqrt(HD))
+        bias = pltpu.roll(
+            jnp.broadcast_to(curve[0, head : head + 1, :], (block_len, block_len + span)),
+            span + 1, 1, stride=1, stride_axis=0,
+        )[:, :span]
+        logits = dot_nt(q_head.astype(LOW), k) + bias + hidden_pairs[...]
+        weights = jnp.exp(logits - jnp.max(logits, axis=1, keepdims=True))
+        prob = (weights * (1.0 / jnp.sum(weights, axis=1, keepdims=True))).astype(LOW)
+        probs[head] = prob
+        total = total + dot_nn(prob, jnp.where(half_mask(v.shape, head), v, 0))
+    mixed[...] = total
+
+
+def expand_kernel(
+    place, frames, mixed, vectors, up_bias, column, side, side_twin, corner, corner_twin,
+    middle, second, active, slope, context, up, out, stage, sems, out_sems,
+):
+    units, kept, width = stage.shape
+    rows = column.shape[2] - kept
+    found = gathered_copies(place, (column, side, side_twin, corner, corner_twin))
+    copies = []
+    for n, (ref, unit) in enumerate(found):
+        at = pl.multiple_of(unit * rows, rows)
+        copies.append(pltpu.make_async_copy(ref.at[:rows], up.at[pl.ds(at, rows)], sems.at[n]))
+        copies.append(pltpu.make_async_copy(ref.at[rows:], stage.at[unit], out_sems.at[n]))
+    for copy in copies:
+        copy.start()
+    for copy in copies:
+        copy.wait()
+    each = width // units
+    for pair in range(units // 2):
+        joined = jnp.concatenate(
+            [stage[2 * pair].astype(F32)[:each], stage[2 * pair + 1].astype(F32)[:each]], axis=0
+        )
+        out[2 * each * pair : 2 * each * (pair + 1), :] = joined.astype(LOW)
+    context[...] = mixed[...].astype(LOW)
+    mid = frames[...].astype(F32) + (dot_nt(context[...], out[...]) + vectors[4:5, :])
+    middle[...] = mid
+    center = mid - jnp.mean(mid, axis=1, keepdims=True)
+    normed = center * lax.rsqrt(jnp.mean(center * center, axis=1, keepdims=True) + EPSILON)
+    second[...] = (normed * vectors[2:3, :] + vectors[3:4, :]).astype(LOW)
+    tile = 2 * LANES
+
+    @pl.loop(0, up.shape[0] // tile)
+    def _(n):
+        at = pl.multiple_of(n * tile, tile)
+        hidden = dot_nt(second[...], up[pl.ds(at, tile), :]) + up_bias[0:1, pl.ds(at, tile)]
+        cdf = 0.5 * (1.0 + lax.erf(hidden * 0.7071067811865476))
+        density = jnp.exp(-0.5 * hidden * hidden) * 0.3989422804014327
+        active[:, pl.ds(at, tile)] = (hidden * cdf).astype(LOW)
+        slope[:, pl.ds(at, tile)] = cdf + hidden * density
+
+
+def down_grad_kernel(
+    place, active, cotangent, corner_send, corner_keep, side_send, side_keep, own, bias_grad, stage, sems
+):
+    units, rows, width = stage.shape
+    each = width // units
+    folds = rows // each
+    dy = cotangent[...]
+    bias_grad[...] = jnp.broadcast_to(
+        jnp.sum(dy.astype(F32), axis=0, keepdims=True), bias_grad.shape
+    )
+    group = 2 * LANES // each if 2 * LANES % each == 0 else 8
+    for start in range(0, units, group):
+        lane = slice(start * each, (start + group) * each)
+        grads = [
+            dot_tn(dy[:, lane], active[:, fold * width : (fold + 1) * width]) for fold in range(folds)
+        ]
+        for n in range(group):
+            stage[start + n] = jnp.concatenate(
+                [grad[n * each : (n + 1) * each] for grad in grads], axis=0
+            ).astype(LOW)
+    store_units(place, stage, (corner_send, corner_keep, side_send, side_keep, own), sems)
+
+
+def back_kernel(
+    place, cotangent, slope, second, middle, context, vectors, up, out,
+    column, side, side_twin, corner, corner_twin,
+    corner_send, corner_keep, side_send, side_keep, own,
+    down, middle_grad, context_grad, vector_grads, up_bias_grad,
+    stage, hidden_grad, out_stage, up_stage, sems,
+):
+    units, rows, width = stage.shape
+    each = width // units
+    folds = rows // each
+    shard_len = cotangent.shape[0]
+    copies = load_units(place, (column, side, side_twin, corner, corner_twin), stage, sems)
+    for copy in copies:
+        copy.wait()
+    for pair in range(units // 2):
+        one, two = stage[2 * pair].astype(F32), stage[2 * pair + 1].astype(F32)
+        for fold in range(folds):
+            joined = jnp.concatenate(
+                [one[fold * each : (fold + 1) * each], two[fold * each : (fold + 1) * each]], axis=0
+            )
+            down[2 * each * pair : 2 * each * (pair + 1), fold * width : (fold + 1) * width] = (
+                joined.astype(LOW)
+            )
+    dy = cotangent[...]
+    tile = 2 * LANES
+    up_rows = up.shape[0] // units
+    second_grad = jnp.zeros((shard_len, width), F32)
+    for n in range(up.shape[0] // tile):
+        at = slice(n * tile, (n + 1) * tile)
+        grad = (dot_nn(dy, down[:, at]) * slope[:, at]).astype(LOW)
+        hidden_grad[:, at] = grad
+        up_bias_grad[:, at] = jnp.broadcast_to(
+            jnp.sum(grad.astype(F32), axis=0, keepdims=True), (up_bias_grad.shape[0], tile)
+        )
+        second_grad = second_grad + dot_nn(grad, up[at, :])
+    mid = middle[...]
+    center = mid - jnp.mean(mid, axis=1, keepdims=True)
+    inv_std = lax.rsqrt(jnp.mean(center * center, axis=1, keepdims=True) + EPSILON)
+    normed = center * inv_std
+    scaled = second_grad * vectors[2:3, :]
+    inner = (
+        scaled
+        - jnp.mean(scaled, axis=1, keepdims=True)
+        - normed * jnp.mean(scaled * normed, axis=1, keepdims=True)
+    )
+    mid_grad = dy.astype(F32) + inner * inv_std
+    middle_grad[...] = mid_grad
+    branch = mid_grad.astype(LOW)
+    vector_grads[...] = jnp.concatenate(
+        [
+            jnp.sum(second_grad * normed, axis=0, keepdims=True),
+            jnp.sum(second_grad, axis=0, keepdims=True),
+            jnp.sum(branch.astype(F32), axis=0, keepdims=True),
+            jnp.zeros((5, width), F32),
+        ],
+        axis=0,
+    )
+    context_grad[...] = dot_nn(branch, out[...]).astype(LOW)
+    out_grad = dot_tn(branch, context[...])
+    blank = jnp.zeros((rows_left(each), width), F32)
+    for unit in range(units):
+        out_stage[unit] = jnp.concatenate(
+            [out_grad[unit * each : (unit + 1) * each], blank], axis=0
+        ).astype(LOW)
+    batch = 8
+    for start in range(0, units, batch):
+        at = slice(start * up_rows, (start + batch) * up_rows)
+        grad = dot_tn(hidden_grad[:, at], second[...]).astype(LOW)
+        for n in range(batch):
+            up_stage[start + n, :up_rows] = grad[n * up_rows : (n + 1) * up_rows]
+            up_stage[start + n, up_rows:] = out_stage[start + n]
+    store_units(place, up_stage, (corner_send, corner_keep, side_send, side_keep, own), sems)
+
+
+def rows_left(each):
+    return -each % 16
+
+
+def finish_kernel(active, down, middle, vectors, layer_out):
+    layer_out[...] = middle[...] + dot_nt(active[...], down[...]) + vectors[5:6, :]
+
+
+def attend_back_kernel(
+    queries, keys, values, context_grad, mixed, probs, query_grad, key_grad, value_grad, diagonals
+):
+    q, k, v, dout = queries[...], keys[...], values[...], context_grad[...]
+    block_len, span = probs.shape[1:]
+    weighted = dout.astype(F32) * mixed[...]
+    row = lax.broadcasted_iota(jnp.int32, (block_len, block_len), 0)
+    lane = lax.broadcasted_iota(jnp.int32, (block_len, block_len), 1)
+    turn = (row + lane == block_len - 1).astype(LOW)
+    blank = jnp.zeros((block_len, block_len), F32)
+    dq, dk, dv = jnp.zeros(q.shape, F32), jnp.zeros(k.shape, F32), jnp.zeros(v.shape, F32)
+    for head in range(2):
+        mine = half_mask(q.shape, head)
+        dout_head = jnp.where(mine, dout, 0)
+        delta = jnp.sum(jnp.where(mine, weighted, 0.0), axis=1, keepdims=True)
+        prob = probs[head]
+        grad = prob.astype(F32) * (dot_nt(dout_head, v) - delta)
+        raw = (grad * (1.0 / math.sqrt(HD))).astype(LOW)
+        dq = dq + dot_nn(raw, jnp.where(half_mask(k.shape, head), k, 0))
+        dk = dk + dot_tn(raw, jnp.where(mine, q, 0))
+        dv = dv + dot_tn(prob, dout_head)
+        turned = jnp.concatenate([dot_nn(turn, raw), blank], axis=1)
+        sheared = pltpu.roll(turned, 0, 1, stride=1, stride_axis=0)
+        diagonals[0, head : head + 1, :] = jnp.sum(sheared, axis=0, keepdims=True) * math.sqrt(HD)
+    query_grad[...] = dq.astype(LOW)
+    key_grad[...] = dk.astype(LOW)
+    value_grad[...] = dv.astype(LOW)
+
+
+def qkv_grad_kernel(
+    place, own_frames, mate_frames, first, query_grad, key_grad, value_grad, weight, vectors,
+    diagonals, buckets, vector_grads, down_bias_grad, up_bias_grad, wide_one, wide_two, wide_four,
+    corner_send, corner_keep, side_send, side_keep, own, own_grad, mate_grad, grads, small, stage, sems,
+):
+    units, full, width = stage.shape
+    rows = full - PAD
+    shard_len = own_frames.shape[0]
+    x = place[0]
+    own_at = pl.multiple_of(x * shard_len, shard_len)
+    mate_at = pl.multiple_of((1 - x) * shard_len, shard_len)
+    dq, dk, dv = query_grad[...], key_grad[...], value_grad[...]
+    grads[:width, :] = dot_tn(dq, first[pl.ds(own_at, shard_len), :])
+    grads[width : 2 * width, :] = dot_tn(dk, first[...])
+    grads[2 * width :, :] = dot_tn(dv, first[...])
+
+    def first_grad(at):
+        return dot_nn(key_grad[pl.ds(at, shard_len), :], weight[width : 2 * width, :]) + dot_nn(
+            value_grad[pl.ds(at, shard_len), :], weight[2 * width :, :]
+        )
+
+    def normed(frames):
+        wide = frames.astype(F32)
+        center = wide - jnp.mean(wide, axis=1, keepdims=True)
+        return center * lax.rsqrt(jnp.mean(center * center, axis=1, keepdims=True) + EPSILON)
+
+    of_own = first_grad(own_at) + dot_nn(dq, weight[:width, :])
+    of_mate = first_grad(mate_at)
+    own_grad[...] = of_own
+    mate_grad[...] = of_mate.astype(LOW)
+
+    def total(array):
+        return jnp.sum(array, axis=0, keepdims=True)
+
+    gain_grad = total(of_own * normed(own_frames[...])) + total(of_mate * normed(mate_frames[...]))
+    shift_grad = total(of_own) + total(of_mate)
+    narrow = (
+        gain_grad, shift_grad, vector_grads[0:1, :], vector_grads[1:2, :], vector_grads[2:3, :],
+        down_bias_grad[0:1, :],
+    )
+
+    def fold(vector, table):
+        kept = (vector * table[:units, :].astype(F32)).astype(LOW)
+        return dot_nt(kept, table[units:, :])
+
+    for n, vector in enumerate(narrow):
+        small[0, :, n * LANES : (n + 1) * LANES] = fold(vector, wide_one)
+    small[1, :, :] = jnp.zeros((units, width), F32)
+    both = jnp.concatenate([total(dq.astype(F32)), total(dv.astype(F32))], axis=1)
+    small[1, :, :LANES] = fold(both, wide_two)
+    small[1, :, LANES : 2 * LANES] = fold(up_bias_grad[0:1, :], wide_four)
+    table = lax.dot_general(
+        diagonals[...], buckets[...], (((1,), (0,)), ((), ())), precision=HIGHEST, preferred_element_type=F32
+    )
+    table = jnp.concatenate([table[: H // 2], table[H // 2 :]], axis=1)
+    for unit in range(units):
+        stage[unit] = jnp.concatenate(
+            [
+                grads[unit * rows : (unit + 1) * rows, :],
+                small[0, unit : unit + 1, :],
+                small[1, unit : unit + 1, :],
+                table,
+            ],
+            axis=0,
+        ).astype(LOW)
+    store_units(place, stage, (corner_send, corner_keep, side_send, side_keep, own), sems)
+
+
+def input_grad_kernel(frames, own_grad, mate_part, middle_grad, vectors, frames_grad):
+    wide = frames[...].astype(F32)
+    center = wide - jnp.mean(wide, axis=1, keepdims=True)
+    inv_std = lax.rsqrt(jnp.mean(center * center, axis=1, keepdims=True) + EPSILON)
+    normed = center * inv_std
+    scaled = (own_grad[...] + mate_part[...].astype(F32)) * vectors[0:1, :]
+    inner = (
+        scaled
+        - jnp.mean(scaled, axis=1, keepdims=True)
+        - normed * jnp.mean(scaled * normed, axis=1, keepdims=True)
+    )
+    frames_grad[...] = middle_grad[...] + inner * inv_std
+
+
+def paired_body(
+    frames, cotangent, seq_lengths, key_mask, qkv_weight, query_value_bias, out_weight, out_bias,
+    up_weight, up_bias, down_weight, down_bias, first_gain, first_shift, second_gain, second_shift,
+    rel_bias,
+):
+    shard_len, width = frames.shape
+    x = lax.axis_index("blk")
+    d = lax.axis_index("dp")
+    core = d % 2
+    units = lax.axis_size("dp") * lax.axis_size("blk")
+    span = shard_len * lax.axis_size("blk")
+    place = jnp.stack([x, (d // 2) % 2, d // 4, core]).astype(jnp.int32)
+    each = width // units
+    ff = up_weight.shape[1] * units
+    qkv_rows, up_rows = qkv_weight.shape[1], up_weight.shape[1]
+    folds = ff // width
+    down_rows = each * folds
+    out_rows = each + rows_left(each)
+
+    def slot(vector):
+        return jnp.pad(vector, (0, LANES - vector.shape[0]))
+
+    narrow_row = jnp.concatenate(
+        [slot(v) for v in (first_gain, first_shift, second_gain, second_shift, out_bias, down_bias)]
+    )
+    wide_row = jnp.pad(
+        jnp.concatenate([slot(query_value_bias), slot(up_bias)]), (0, width - 2 * LANES)
+    )
+    small_rows = jnp.pad(jnp.stack([narrow_row, wide_row]), ((0, PAD - 2), (0, 0)))
+    qkv_unit = jnp.concatenate([qkv_weight.T, small_rows])
+    out_unit = jnp.concatenate(
+        [up_weight.T, out_weight.T, jnp.zeros((out_rows - each, width), LOW)]
+    )
+    down_unit = jnp.concatenate(
+        [down_weight.T[:, fold * width : (fold + 1) * width] for fold in range(folds)]
+    )
+    live_row = jnp.pad(key_mask.astype(LOW), (0, width - shard_len))
+    sent = jnp.concatenate([frames, jnp.pad(live_row[None], ((0, 15), (0, 0)))])
+    got = shift(sent, PACK)
+    mate_frames, mate_live = got[:shard_len], got[shard_len, :shard_len]
+    qkv_pieces = gather_units(qkv_unit, core)
+    up_pieces = gather_units(out_unit, core)
+    down_pieces = gather_units(down_unit, core)
+
+    seq_ends = jnp.cumsum(seq_lengths[0])
+    key_pos = jnp.arange(span, dtype=jnp.int32)
+    key_doc = doc_numbers(seq_ends, key_pos)
+    query_pos = x * shard_len + jnp.arange(shard_len, dtype=jnp.int32)
+    query_doc = doc_numbers(seq_ends, query_pos)
+    own_live = key_mask.astype(LOW)
+    live = jnp.where(
+        x == 0, jnp.concatenate([own_live, mate_live]), jnp.concatenate([mate_live, own_live])
+    )
+    allowed = (query_doc[:, None] == key_doc[None, :]) & (
+        (live[None, :] > 0.5) | (query_pos[:, None] == key_pos[None, :])
+    )
+    hidden_pairs = jnp.where(allowed, 0.0, MASKED).astype(F32)
+    distance = jnp.arange(span + shard_len, dtype=jnp.int32) - (shard_len - 1) - x * shard_len
+    bucket = jnp.clip(distance, -MAXREL, MAXREL) + MAXREL
+    bucket_lanes = 3 * LANES
+    buckets = (bucket[:, None] == jnp.arange(bucket_lanes, dtype=jnp.int32)[None, :]).astype(LOW)
+    curve = jnp.dot(buckets[:, :BUCKETS], rel_bias, preferred_element_type=F32).T
+    curve = curve.reshape(H // 2, 2, span + shard_len)
+    spreads = spread_tables(units, width)
+
+    def shape(*dims, kind=LOW):
+        return jax.ShapeDtypeStruct(dims, kind)
+
+    unit_sems = pltpu.SemaphoreType.DMA((units,))
+    first, queries, keys, values, weight, vectors, up_bias_all = call(
+        project_kernel,
+        [SMEM, VMEM, VMEM] + [ANY] * 5 + [VMEM] * 3,
+        [
+            shape(span, width), shape(shard_len, width), shape(span, width), shape(span, width),
+            shape(3 * width, width), shape(8, width, kind=F32), shape(8, ff, kind=F32),
+        ],
+        [VMEM] * 7,
+        [
+            pltpu.VMEM((units, qkv_rows + PAD, width), LOW), pltpu.VMEM((2, units, width), F32), unit_sems,
+        ],
+        (place, frames, mate_frames) + qkv_pieces + tuple(spreads),
+        2 * shard_len * width * 5 * width,
+        name="project",
+    )
+    pairs = H // 2
+    pair_lanes = 2 * HD
+
+    def lanes_of(rows):
+        return pl.BlockSpec((rows, pair_lanes), lambda n: (0, n))
+
+    def heads_of(*dims):
+        return pl.BlockSpec(dims, lambda n: (n,) + (0,) * (len(dims) - 1))
+
+    probs, mixed = call(
+        attend_kernel,
+        [
+            SMEM, lanes_of(shard_len), lanes_of(span), lanes_of(span), heads_of(1, 2, span + shard_len),
+            pl.BlockSpec((shard_len, span), lambda n: (0, 0)),
+        ],
+        [shape(H, shard_len, span), shape(shard_len, width, kind=F32)],
+        [heads_of(2, shard_len, span), lanes_of(shard_len)],
+        [],
+        (place, queries, keys, values, curve, hidden_pairs),
+        8 * shard_len * span * width,
+        grid=(pairs,),
+        name="attend",
+    )
+    middle, second, active, slope, context, up, out = call(
+        expand_kernel,
+        [SMEM] + [VMEM] * 4 + [ANY] * 5,
+        [
+            shape(shard_len, width, kind=F32), shape(shard_len, width), shape(shard_len, ff),
+            shape(shard_len, ff, kind=F32), shape(shard_len, width), shape(ff, width), shape(width, width),
+        ],
+        [VMEM] * 7,
+        [pltpu.VMEM((units, out_rows, width), LOW), unit_sems, unit_sems],
+        (place, frames, mixed, vectors, up_bias_all) + up_pieces,
+        2 * shard_len * width * (width + ff),
+        name="expand",
+    )
+    down_parts = call(
+        down_grad_kernel,
+        [SMEM, VMEM, VMEM],
+        part_shapes(down_rows, width) + [shape(8, width, kind=F32)],
+        [ANY] * 5 + [VMEM],
+        [pltpu.VMEM((units, down_rows, width), LOW), unit_sems],
+        (place, active, cotangent),
+        2 * shard_len * width * ff,
+        name="down_grad",
+    )
+    down_bias_grad = down_parts[5]
+    down_sum = scatter_units(down_parts[:5], core)
+    back = call(
+        back_kernel,
+        [SMEM] + [VMEM] * 8 + [ANY] * 5,
+        part_shapes(up_rows + out_rows, width)
+        + [
+            shape(width, ff), shape(shard_len, width, kind=F32), shape(shard_len, width),
+            shape(8, width, kind=F32), shape(8, ff, kind=F32),
+        ],
+        [ANY] * 5 + [VMEM] * 5,
+        [
+            pltpu.VMEM((units, down_rows, width), LOW), pltpu.VMEM((shard_len, ff), LOW),
+            pltpu.VMEM((units, out_rows, width), LOW),
+            pltpu.VMEM((units, up_rows + out_rows, width), LOW), unit_sems,
+        ],
+        (place, cotangent, slope, second, middle, context, vectors, up, out) + down_pieces,
+        2 * shard_len * width * (3 * ff + 2 * width),
+        name="back",
+    )
+    down, middle_grad, context_grad, vector_grads, up_bias_grad = back[5:]
+    up_sum = scatter_units(back[:5], core)
+    layer_out = call(
+        finish_kernel, [VMEM] * 4, shape(shard_len, width, kind=F32), VMEM, [],
+        (active, down, middle, vectors), 2 * shard_len * width * ff, name="finish",
+    ) if False else pl.pallas_call(
+        finish_kernel,
+        out_shape=shape(shard_len, width, kind=F32),
+        compiler_params=pltpu.CompilerParams(vmem_limit_bytes=VMEM_BYTES),
+        cost_estimate=pl.CostEstimate(
+            flops=2 * shard_len * width * ff, bytes_accessed=8 * shard_len * ff, transcendentals=0
+        ),
+        name="finish",
+    )(active, down, middle, vectors)
+    query_grad, key_grad, value_grad, diagonals = call(
+        attend_back_kernel,
+        [
+            lanes_of(shard_len), lanes_of(span), lanes_of(span), lanes_of(shard_len), lanes_of(shard_len),
+            heads_of(2, shard_len, span),
+        ],
+        [
+            shape(shard_len, width), shape(span, width), shape(span, width),
+            shape(pairs, 2, span + shard_len, kind=F32),
+        ],
+        [lanes_of(shard_len), lanes_of(span), lanes_of(span), heads_of(1, 2, span + shard_len)],
+        [],
+        (queries, keys, values, context_grad, mixed, probs),
+        16 * shard_len * span * width,
+        grid=(pairs,),
+        name="attend_back",
+    )
+    qkv_parts = call(
+        qkv_grad_kernel,
+        [SMEM] + [VMEM] * 16,
+        part_shapes(qkv_rows + PAD, width) + [shape(shard_len, width, kind=F32), shape(shard_len, width)],
+        [ANY] * 5 + [VMEM] * 2,
+        [
+            pltpu.VMEM((3 * width, width), F32), pltpu.VMEM((2, units, width), F32),
+            pltpu.VMEM((units, qkv_rows + PAD, width), LOW), unit_sems,
+        ],
+        (
+            place, frames, mate_frames, first, query_grad, key_grad, value_grad, weight, vectors,
+            diagonals.reshape(H, span + shard_len), buckets.astype(F32), vector_grads, down_bias_grad,
+            up_bias_grad,
+        ) + tuple(spreads),
+        2 * shard_len * width * 10 * width,
+        name="qkv_grad",
+    )
+    own_grad, mate_grad = qkv_parts[5:]
+    mate_part = shift(mate_grad, PACK)
+    qkv_sum = scatter_units(qkv_parts[:5], core)
+    frames_grad = pl.pallas_call(
+        input_grad_kernel,
+        out_shape=shape(shard_len, width, kind=F32),
+        compiler_params=pltpu.CompilerParams(vmem_limit_bytes=VMEM_BYTES),
+        name="input_grad",
+    )(frames, own_grad, mate_part, middle_grad, vectors)
+
+    down_grad = jnp.concatenate(
+        [down_sum[fold * each : (fold + 1) * each] for fold in range(folds)], axis=1
+    )
+    narrow_sum, wide_sum, table_sum = (
+        qkv_sum[qkv_rows], qkv_sum[qkv_rows + 1], qkv_sum[qkv_rows + 2 :],
+    )
+    table = jnp.concatenate([table_sum[:, :BUCKETS], table_sum[:, bucket_lanes : bucket_lanes + BUCKETS]])
+    pieces = [narrow_sum[n * LANES : n * LANES + each] for n in range(NARROW)]
+    return (
+        layer_out, frames_grad, qkv_sum[:qkv_rows].T, wide_sum[: 2 * each],
+        up_sum[up_rows : up_rows + each].T, pieces[4], up_sum[:up_rows].T,
+        wide_sum[LANES : LANES + up_rows], down_grad.T, pieces[5], pieces[0], pieces[1], pieces[2],
+        pieces[3], table.T,
+    )
+
+
+def paired(mesh):
+    return mesh.shape["blk"] == 2 and mesh.shape["dp"] == 16
+
+
 def solution(mesh):
     placed = (
         P(("dp", "blk"), None),
@@ -487,7 +1225,7 @@
         P(),
     )
     return jax.shard_map(
-        body,
+        paired_body if paired(mesh) else body,
         mesh=mesh,
         in_specs=placed,
         out_specs=(

time: 1140 us -> 330 us (0.29)
  local copies, waits for them, and re-layouts: 601 us -> 27.3 us
  waiting for transfers between devices: 325 us -> 114 us
  Pallas kernels: 0 us -> 88.1 us
  blocking collectives: 81.5 us -> 0 us
  matrix products: 66.7 us -> 1.9 us
  starting transfers between devices: 12.4 us -> 73.9 us
  between operations: 18.3 us -> 1.43 us
    gather x4 -> x0, local copies, waits for them, and re-layouts: 475 us -> none  [pair_logits(): bias = jnp.take(table_heads, relative, axis=1)]
    reduce_scatter x4 -> x0, waiting for transfers between devices: 297 us -> none  [the longest x1 142 us: body(): lax.psum_scatter(down_grad, ('dp', 'blk'), scatter_dimension=1, tiled=True)]
    pallas_call x0 -> x9, Pallas kernels: none -> 88.1 us  [the longest x7 79.8 us: call(): pl.pallas_call(kernel, out_shape=outs, in_specs=in_specs, out_specs=out_s...]
    ppermute x7 -> x53, waiting for transfers between devices: 26.4 us -> 114 us  [shift(): return lax.ppermute(array, AXES, route(move))]
    unnamed x2 -> x0, blocking collectives: 81.5 us -> none
    dot_general x26 -> x1, matrix products: 66.7 us -> 1.9 us  [paired_body(): jnp.dot(buckets[:, :BUCKETS], rel_bias, preferred_element_type=F32)]
    ppermute x7 -> x53, starting transfers between devices: 12.1 us -> 73.9 us  [shift(): return lax.ppermute(array, AXES, route(move))]
    rev x2 -> x0, local copies, waits for them, and re-layouts: 39.9 us -> none  [diagonal_sums(): flipped = gradient[:, ::-1, :]]
  transfers between devices with their start and end apart: 15 -> 53, of which waited for: 9 -> 17; matrix products, arithmetic and copies ran while one was open for 58% -> 11% of each run, Pallas kernels for 0% -> 12%
where the time goes in v1:
time: 330 us; the launch traced here: 329 us
  waiting for transfers between devices  114 us (35%)
  Pallas kernels  88.1 us (27%)
  starting transfers between devices  73.9 us (22%)
  local copies, waits for them, and re-layouts  27.3 us (8%)
  other arithmetic  22.5 us (7%)
    ppermute x53, waiting for transfers between devices, shift(): return lax.ppermute(array, AXES, route(move))  114 us
    pallas_call x7, Pallas kernels, call(): pl.pallas_call(kernel, out_shape=outs, in_specs=in_specs, out_specs=out_s...  79.8 us
    ppermute x53, starting transfers between devices, shift(): return lax.ppermute(array, AXES, route(move))  73.9 us
    unnamed x57, local copies, waits for them, and re-layouts  7.8 us
  transfers between devices with their start and end apart: 53, of which 17 were waited for; matrix products, arithmetic and copies ran while one was open for 11% of the time, Pallas kernels for 12%

profile of v1, /device:TPU:0, one launch (start us, length us, event | category | flops | bytes accessed | tf_op | source)
XLA Modules:
  0.0 329.2 jit_solution(12609717715594902580)
XLA Ops:
  6.5 0.9 fusion.25
  7.4 5.1 %collective-permute-start.4 = (bf16[80,768]{1,0:T(8,128)(2,1)S(1)}, bf16[80,768]{1,0:T(8,128)(2,1)S(1)}, u32[]{:S(2)}, u32[]{:S(2)}) collective-permute-start(bf16[80,768]{1,0:T(8,128)(2,1)S(1)} %get-tuple-element.161), channel_id=1, source_target_pairs={{0,24},{1,25},{2,26},{3,27},{4,28},{5,29},{6,30},{7,31},{8,16},{9,... | collective-permute-start | bytes 368648 | tf_op jit(solution)/shard_map/ppermute | solution.py:492
  12.6 1.0 fusion.29
  15.2 3.5 %collective-permute-start.22 = (bf16[96,768]{1,0:T(8,128)(2,1)S(1)}, bf16[96,768]{1,0:T(8,128)(2,1)S(1)}, u32[]{:S(2)}, u32[]{:S(2)}) collective-permute-start(bf16[96,768]{1,0:T(8,128)(2,1)S(1)} %get-tuple-element.154), channel_id=1, source_target_pairs={{0,24},{1,25},{2,26},{3,27},{4,28},{5,29},{6,30},{7,31},{8,16},{9,... | collective-permute-start | bytes 442376 | tf_op jit(solution)/shard_map/ppermute | solution.py:492
  19.0 7.4 %collective-permute-start.2 = (bf16[2,80,768]{2,1,0:T(8,128)(2,1)S(1)}, bf16[2,80,768]{2,1,0:T(8,128)(2,1)S(1)}, u32[]{:S(2)}, u32[]{:S(2)}) collective-permute-start(bf16[2,80,768]{2,1,0:T(8,128)(2,1)S(1)} %maximum_select_fusion.8), channel_id=1, source_target_pairs={{0,8},{1,9},{2,18},{3,19},{4,12},{5,13},{6,22},{7,23},{8,0},{9,1},... | collective-permute-start | bytes 737288 | tf_op jit(solution)/shard_map/ppermute | solution.py:492
  26.5 4.9 %collective-permute-done.11 = bf16[2,128,768]{2,1,0:T(8,128)(2,1)S(1)} collective-permute-done((bf16[2,128,768]{2,1,0:T(8,128)(2,1)S(1)}, bf16[2,128,768]{2,1,0:T(8,128)(2,1)S(1)}, u32[]{:S(2)}, u32[]{:S(2)}) %collective-permute-start.11) | collective-permute-done | bytes 393248 | tf_op jit(solution)/shard_map/ppermute | solution.py:492
  31.4 11.9 %collective-permute-start.12 = (bf16[2,128,768]{2,1,0:T(8,128)(2,1)S(1)}, bf16[2,128,768]{2,1,0:T(8,128)(2,1)S(1)}, u32[]{:S(2)}, u32[]{:S(2)}) collective-permute-start(bf16[2,128,768]{2,1,0:T(8,128)(2,1)S(1)} %collective-permute-done.11), channel_id=1, source_target_pairs={{0,2},{1,3},{2,0},{3,1},{4,6},{5,7},{6,4},{7,5},{8,10},{9,11},{10,... | collective-permute-start | bytes 1179656 | tf_op jit(solution)/shard_map/ppermute | solution.py:492
  43.6 2.3 collective-permute-start.23
  46.4 1.6 collective-permute-start.15
  48.0 5.0 %collective-permute-done.20 = bf16[2,96,768]{2,1,0:T(8,128)(2,1)S(1)} collective-permute-done((bf16[2,96,768]{2,1,0:T(8,128)(2,1)S(1)}, bf16[2,96,768]{2,1,0:T(8,128)(2,1)S(1)}, u32[]{:S(2)}, u32[]{:S(2)}) %collective-permute-start.20) | collective-permute-done | bytes 294944 | tf_op jit(solution)/shard_map/ppermute | solution.py:492
  53.6 1.2 maximum_select_fusion.2.column
  54.8 1.5 collective-permute-start.6
  57.8 1.6 collective-permute-start
  60.2 22.8 %collective-permute-done.6.side = bf16[2,4,80,768]{3,2,1,0:T(8,128)(2,1)} collective-permute-done((bf16[2,4,80,768]{3,2,1,0:T(8,128)(2,1)}, bf16[2,4,80,768]{3,2,1,0:T(8,128)(2,1)}, u32[]{:S(2)}, u32[]{:S(2)}) %collective-permute-start.6) | collective-permute-done | bytes 983072 | tf_op jit(solution)/shard_map/ppermute | solution.py:492
  83.0 1.1 dynamic-slice_bitcast_fusion.2
  84.0 1.6 collective-permute-start.8
  85.6 2.1 dynamic-slice_bitcast_fusion
  88.2 20.0 %collective-permute-done.24.side = bf16[2,4,96,768]{3,2,1,0:T(8,128)(2,1)} collective-permute-done((bf16[2,4,96,768]{3,2,1,0:T(8,128)(2,1)S(1)}, bf16[2,4,96,768]{3,2,1,0:T(8,128)(2,1)}, u32[]{:S(2)}, u32[]{:S(2)}) %collective-permute-start.24) | collective-permute-done | bytes 1179680 | tf_op jit(solution)/shard_map/ppermute | solution.py:492
  108.3 1.9 dynamic-slice_bitcast_fusion.1
  110.2 2.7 collective-permute-done
  112.9 1.5 collective-permute-start.26
  114.4 1.4 convert_convert_fusion
  116.6 1.9 fusion.2
  118.5 4.4 %collective-permute-done.26.corner = bf16[4,96,768]{2,1,0:T(8,128)(2,1)S(1)} collective-permute-done((bf16[4,96,768]{2,1,0:T(8,128)(2,1)}, bf16[4,96,768]{2,1,0:T(8,128)(2,1)S(1)}, u32[]{:S(2)}, u32[]{:S(2)}) %collective-permute-start.26) | collective-permute-done | bytes 589856 | tf_op jit(solution)/shard_map/ppermute | solution.py:492
  124.4 1.4 reshape.305.curve
  125.8 1.8 slice.273.mate.mate_frames
  129.6 1.7 fusion.8.hidden_pairs
  131.3 8.7 %project.1 = (bf16[512,768]{1,0:T(8,128)(2,1)}, bf16[256,768]{1,0:T(8,128)(2,1)}, bf16[512,768]{1,0:T(8,128)(2,1)}, bf16[512,768]{1,0:T(8,128)(2,1)}, bf16[2304,...) custom-call(s32[4]{0:T(128)} %pad_add_fusion.place, bf16[256,768]{1,0:T(8,128)(2,1)} %frames.3, ...), custom_call_target="tpu_custom_call" | custom-call | flops 1509949440 | bytes 12853264 | tf_op jit(solution)/shard_map/project/pallas_call | solution.py:626
  140.0 9.5 %attend.1 = (bf16[12,256,512]{2,1,0:T(8,128)(2,1)}, f32[256,768]{1,0:T(8,128)}) custom-call(s32[4]{0:T(128)} %pad_add_fusion.place, bf16[256,768]{1,0:T(8,128)(2,1)} %get-tuple-element.58.queries, bf16[512,768]{1,0:T(8,128)(2,1)} %get-tuple-element.59.keys, bf16[512,768]{1,0:T(8,128)(2,1)} %get-tuple-element.60.values, f32[6,2,768]{2,1,0:T(2,128)} %reshape.305.curve, ...), custom_call_target="tpu_custom_call" | custom-call | flops 805306368 | bytes 6459408 | tf_op jit(solution)/shard_map/attend/pallas_call | solution.py:626
  149.6 1.2 copy-done.7
  151.0 14.3 %expand.1 = (f32[256,768]{1,0:T(8,128)}, bf16[256,768]{1,0:T(8,128)(2,1)}, bf16[256,3072]{1,0:T(8,128)(2,1)}, f32[256,3072]{1,0:T(8,128)}, bf16[256,768]{1,0:T(8...) custom-call(s32[4]{0:T(128)} %pad_add_fusion.place, bf16[256,768]{1,0:T(8,128)(2,1)} %frames.3, ...), custom_call_target="tpu_custom_call" | custom-call | flops 1509949440 | bytes 19783696 | tf_op jit(solution)/shard_map/expand/pallas_call | solution.py:626
  165.4 1.0 copy-done.8
  166.6 18.8 %back.1 = (bf16[4,128,768]{2,1,0:T(8,128)(2,1)}, bf16[4,128,768]{2,1,0:T(8,128)(2,1)}, bf16[2,4,128,768]{3,2,1,0:T(8,128)(2,1)}, bf16[2,4,128,768]{3,2,1,0:T(8,1...) custom-call(s32[4]{0:T(128)} %pad_add_fusion.place, ...), custom_call_target="tpu_custom_call" | custom-call | flops 4227858432 | bytes 28065808 | tf_op jit(solution)/shard_map/back/pallas_call | solution.py:626
  185.3 9.8 %attend_back.1 = (bf16[256,768]{1,0:T(8,128)(2,1)}, bf16[512,768]{1,0:T(8,128)(2,1)}, bf16[512,768]{1,0:T(8,128)(2,1)}, f32[6,2,768]{2,1,0:T(2,128)}) custom-call(bf16[256,768]{1,0:T(8,128)(2,1)} %get-tuple-element.58.queries, bf16[512,768]{1,0:T(8,128)(2,1)} %get-tuple-element.59.keys, bf16[512,768]{1,0:T(8,128)(2,1)} %get-tuple-element.60.values, ...), custom_call_target="tpu_custom_call" | custom-call | flops 1610612736 | bytes 8294400 | tf_op jit(solution)/shard_map/attend_back/pallas_call | solution.py:626
  195.1 1.4 reshape.308.diagonals
  196.5 6.0 %down_grad.1 = (bf16[4,96,768]{2,1,0:T(8,128)(2,1)}, bf16[4,96,768]{2,1,0:T(8,128)(2,1)}, bf16[2,4,96,768]{3,2,1,0:T(8,128)(2,1)}, bf16[2,4,96,768]{3,2,1,0:T(8,...) custom-call(s32[4]{0:T(128)} %pad_add_fusion.place, bf16[256,3072]{1,0:T(8,128)(2,1)} %get-tuple-element.64.active, ...), custom_call_target="tpu_custom_call" | custom-call | flops 1207959552 | bytes 6709264 | tf_op jit(solution)/shard_map/down_grad/pallas_call | solution.py:626
  202.5 12.7 %qkv_grad.1 = (bf16[4,80,768]{2,1,0:T(8,128)(2,1)}, bf16[4,80,768]{2,1,0:T(8,128)(2,1)}, bf16[2,4,80,768]{3,2,1,0:T(8,128)(2,1)}, bf16[2,4,80,768]{3,2,1,0:T(8,1...) custom-call(s32[4]{0:T(128)} %pad_add_fusion.place, ...), custom_call_target="tpu_custom_call" | custom-call | flops 3019898880 | bytes 15298576 | tf_op jit(solution)/shard_map/qkv_grad/pallas_call | solution.py:626
  215.9 1.5 collective-permute-done.30
  217.4 1.2 add_convert_fusion.8
  218.6 1.6 collective-permute-start.31
  220.9 6.6 %collective-permute-done.31 = bf16[4,80,768]{2,1,0:T(8,128)(2,1)S(1)} collective-permute-done((bf16[4,80,768]{2,1,0:T(8,128)(2,1)S(1)}, bf16[4,80,768]{2,1,0:T(8,128)(2,1)S(1)}, u32[]{:S(2)}, u32[]{:S(2)}) %collective-permute-start.31) | collective-permute-done | bytes 491552 | tf_op jit(solution)/shard_map/ppermute | solution.py:492
  227.5 1.5 collective-permute-start.47
  229.1 1.4 add_convert_fusion.5
  230.5 1.5 collective-permute-start.32
  232.8 9.7 %collective-permute-done.47 = bf16[4,96,768]{2,1,0:T(8,128)(2,1)S(1)} collective-permute-done((bf16[4,96,768]{2,1,0:T(8,128)(2,1)S(1)}, bf16[4,96,768]{2,1,0:T(8,128)(2,1)S(1)}, u32[]{:S(2)}, u32[]{:S(2)}) %collective-permute-start.47) | collective-permute-done | bytes 589856 | tf_op jit(solution)/shard_map/ppermute | solution.py:492
  242.4 2.5 collective-permute-start.28
  245.6 5.4 %finish.1 = f32[256,768]{1,0:T(8,128)} custom-call(bf16[256,3072]{1,0:T(8,128)(2,1)} %get-tuple-element.64.active, bf16[768,3072]{1,0:T(8,128)(2,1)} %get-tuple-element.71.down, f32[256,768]{1,0:T(8,128)} %get-tuple-element.67.middle, f32[8,768]{1,0:T(8,128)} %get-tuple-element.62.vectors), custom_call_target="tpu_custom_call" | custom-call | flops 1207959552 | bytes 6291456 | tf_op jit(solution)/shard_map/finish/pallas_call | solution.py:1134
  250.9 12.2 %collective-permute-done.28.mate_part = bf16[256,768]{1,0:T(8,128)(2,1)} collective-permute-done((bf16[256,768]{1,0:T(8,128)(2,1)}, bf16[256,768]{1,0:T(8,128)(2,1)}, u32[]{:S(2)}, u32[]{:S(2)}) %collective-permute-start.28) | collective-permute-done | bytes 393248 | tf_op jit(solution)/shard_map/ppermute | solution.py:492
  263.2 3.0 input_grad.1
  266.2 1.3 convert_element_type.211
  267.6 1.4 add_convert_fusion.4
  269.3 1.1 copy-done.6
  271.1 1.6 collective-permute-start.40
  272.6 3.1 collective-permute-done.48
  275.8 1.8 add_convert_fusion.2
  277.8 1.1 collective-permute-start.34
  279.0 1.8 collective-permute-start.35
  280.8 8.0 %collective-permute-done.34 = bf16[2,80,768]{2,1,0:T(8,128)(2,1)S(1)} collective-permute-done((bf16[2,80,768]{2,1,0:T(8,128)(2,1)S(1)}, bf16[2,80,768]{2,1,0:T(8,128)(2,1)S(1)}, u32[]{:S(2)}, u32[]{:S(2)}) %collective-permute-start.34) | collective-permute-done | bytes 245792 | tf_op jit(solution)/shard_map/ppermute | solution.py:492
  294.4 2.3 collective-permute-start.51
  296.7 4.4 %collective-permute-done.50 = bf16[2,96,768]{2,1,0:T(8,128)(2,1)S(1)} collective-permute-done((bf16[2,96,768]{2,1,0:T(8,128)(2,1)S(1)}, bf16[2,96,768]{2,1,0:T(8,128)(2,1)S(1)}, u32[]{:S(2)}, u32[]{:S(2)}) %collective-permute-start.50) | collective-permute-done | bytes 294944 | tf_op jit(solution)/shard_map/ppermute | solution.py:492
  301.1 5.5 %collective-permute-start.52 = (bf16[96,768]{1,0:T(8,128)(2,1)S(1)}, bf16[96,768]{1,0:T(8,128)(2,1)S(1)}, u32[]{:S(2)}, u32[]{:S(2)}) collective-permute-start(bf16[96,768]{1,0:T(8,128)(2,1)S(1)} %dynamic-slice_bitcast_fusion.4), channel_id=1, source_target_pairs={{0,2},{1,3},{2,0},{3,1},{4,6},{5,7},{6,4},{7,5},{8,10},{9,11},{10,... | collective-permute-start | bytes 442376 | tf_op jit(solution)/shard_map/ppermute | solution.py:492
  308.3 2.0 collective-permute-start.43
  310.3 7.6 %collective-permute-done.42 = bf16[2,128,768]{2,1,0:T(8,128)(2,1)S(1)} collective-permute-done((bf16[2,128,768]{2,1,0:T(8,128)(2,1)S(1)}, bf16[2,128,768]{2,1,0:T(8,128)(2,1)S(1)}, u32[]{:S(2)}, u32[]{:S(2)}) %collective-permute-start.42) | collective-permute-done | bytes 393248 | tf_op jit(solution)/shard_map/ppermute | solution.py:492
  317.9 8.7 %collective-permute-start.44 = (bf16[128,768]{1,0:T(8,128)(2,1)S(1)}, bf16[128,768]{1,0:T(8,128)(2,1)S(1)}, u32[]{:S(2)}, u32[]{:S(2)}) collective-permute-start(bf16[128,768]{1,0:T(8,128)(2,1)S(1)} %dynamic-slice_bitcast_fusion.3), channel_id=1, source_target_pairs={{0,2},{1,3},{2,0},{3,1},{4,6},{5,7},{6,4},{7,5},{8,10},{9,11},{10,... | collective-permute-start | bytes 589832 | tf_op jit(solution)/shard_map/ppermute | solution.py:492
  (207 shorter events, 30.7 us)
Async XLA Ops:
  0.6 116.0 %copy-start = (bf16[321,12]{0,1:T(8,128)(2,1)S(1)}, bf16[321,12]{0,1:T(8,128)(2,1)}, u32[]{:S(2)}) copy-start(bf16[321,12]{0,1:T(8,128)(2,1)} %param.36) | copy-start | bytes 23116
  7.4 11.6 %collective-permute-start.4 = (bf16[80,768]{1,0:T(8,128)(2,1)S(1)}, bf16[80,768]{1,0:T(8,128)(2,1)S(1)}, u32[]{:S(2)}, u32[]{:S(2)}) collective-permute-start(bf16[80,768]{1,0:T(8,128)(2,1)S(1)} %get-tuple-element.161), channel_id=1, source_target_pairs={{0,24},{1,25},{2,26},{3,27},{4,28},{5,29},{6,30},{7,31},{8,16},{9,... | collective-permute-start | bytes 368648 | tf_op jit(solution)/shard_map/ppermute | solution.py:492
  12.5 6.2 %collective-permute-start.1 = (bf16[80,768]{1,0:T(8,128)(2,1)S(1)}, bf16[80,768]{1,0:T(8,128)(2,1)S(1)}, u32[]{:S(2)}, u32[]{:S(2)}) collective-permute-start(bf16[80,768]{1,0:T(8,128)(2,1)S(1)} %get-tuple-element.161), channel_id=1, source_target_pairs={{0,2},{1,3},{2,0},{3,1},{4,6},{5,7},{6,4},{7,5},{8,10},{9,11},{10,... | collective-permute-start | bytes 368648 | tf_op jit(solution)/shard_map/ppermute | solution.py:492
  13.7 29.6 %collective-permute-start.13 = (bf16[128,768]{1,0:T(8,128)(2,1)S(1)}, bf16[128,768]{1,0:T(8,128)(2,1)S(1)}, u32[]{:S(2)}, u32[]{:S(2)}) collective-permute-start(bf16[128,768]{1,0:T(8,128)(2,1)S(1)} %get-tuple-element.151), channel_id=1, source_target_pairs={{0,24},{1,25},{2,26},{3,27},{4,28},{5,29},{6,30},{7,31},{8,16},{9,... | collective-permute-start | bytes 589832 | tf_op jit(solution)/shard_map/ppermute | solution.py:492
  13.8 4.9 %collective-permute-start.10 = (bf16[128,768]{1,0:T(8,128)(2,1)S(1)}, bf16[128,768]{1,0:T(8,128)(2,1)S(1)}, u32[]{:S(2)}, u32[]{:S(2)}) collective-permute-start(bf16[128,768]{1,0:T(8,128)(2,1)S(1)} %get-tuple-element.151), channel_id=1, source_target_pairs={{0,2},{1,3},{2,0},{3,1},{4,6},{5,7},{6,4},{7,5},{8,10},{9,11},{10,... | collective-permute-start | bytes 589832 | tf_op jit(solution)/shard_map/ppermute | solution.py:492
  15.2 28.3 %collective-permute-start.22 = (bf16[96,768]{1,0:T(8,128)(2,1)S(1)}, bf16[96,768]{1,0:T(8,128)(2,1)S(1)}, u32[]{:S(2)}, u32[]{:S(2)}) collective-permute-start(bf16[96,768]{1,0:T(8,128)(2,1)S(1)} %get-tuple-element.154), channel_id=1, source_target_pairs={{0,24},{1,25},{2,26},{3,27},{4,28},{5,29},{6,30},{7,31},{8,16},{9,... | collective-permute-start | bytes 442376 | tf_op jit(solution)/shard_map/ppermute | solution.py:492
  18.7 7.7 %collective-permute-start.19 = (bf16[96,768]{1,0:T(8,128)(2,1)S(1)}, bf16[96,768]{1,0:T(8,128)(2,1)S(1)}, u32[]{:S(2)}, u32[]{:S(2)}) collective-permute-start(bf16[96,768]{1,0:T(8,128)(2,1)S(1)} %get-tuple-element.154), channel_id=1, source_target_pairs={{0,2},{1,3},{2,0},{3,1},{4,6},{5,7},{6,4},{7,5},{8,10},{9,11},{10,... | collective-permute-start | bytes 442376 | tf_op jit(solution)/shard_map/ppermute | solution.py:492
  18.8 12.6 %collective-permute-start.11 = (bf16[2,128,768]{2,1,0:T(8,128)(2,1)S(1)}, bf16[2,128,768]{2,1,0:T(8,128)(2,1)S(1)}, u32[]{:S(2)}, u32[]{:S(2)}) collective-permute-start(bf16[2,128,768]{2,1,0:T(8,128)(2,1)S(1)} %maximum_select_fusion.4), channel_id=1, source_target_pairs={{0,8},{1,9},{2,18},{3,19},{4,12},{5,13},{6,22},{7,23},{8,0},{9,1},... | collective-permute-start | bytes 1179656 | tf_op jit(solution)/shard_map/ppermute | solution.py:492
  19.0 24.6 %collective-permute-start.2 = (bf16[2,80,768]{2,1,0:T(8,128)(2,1)S(1)}, bf16[2,80,768]{2,1,0:T(8,128)(2,1)S(1)}, u32[]{:S(2)}, u32[]{:S(2)}) collective-permute-start(bf16[2,80,768]{2,1,0:T(8,128)(2,1)S(1)} %maximum_select_fusion.8), channel_id=1, source_target_pairs={{0,8},{1,9},{2,18},{3,19},{4,12},{5,13},{6,22},{7,23},{8,0},{9,1},... | collective-permute-start | bytes 737288 | tf_op jit(solution)/shard_map/ppermute | solution.py:492
  26.4 21.6 %collective-permute-start.5 = (bf16[80,768]{1,0:T(8,128)(2,1)S(1)}, bf16[80,768]{1,0:T(8,128)(2,1)S(1)}, u32[]{:S(2)}, u32[]{:S(2)}) collective-permute-start(bf16[80,768]{1,0:T(8,128)(2,1)S(1)} %collective-permute-done.4), channel_id=1, source_target_pairs={{0,2},{1,3},{2,0},{3,1},{4,6},{5,7},{6,4},{7,5},{8,10},{9,11},{10,... | collective-permute-start | bytes 368648 | tf_op jit(solution)/shard_map/ppermute | solution.py:492
  31.4 14.6 %collective-permute-start.12 = (bf16[2,128,768]{2,1,0:T(8,128)(2,1)S(1)}, bf16[2,128,768]{2,1,0:T(8,128)(2,1)S(1)}, u32[]{:S(2)}, u32[]{:S(2)}) collective-permute-start(bf16[2,128,768]{2,1,0:T(8,128)(2,1)S(1)} %collective-permute-done.11), channel_id=1, source_target_pairs={{0,2},{1,3},{2,0},{3,1},{4,6},{5,7},{6,4},{7,5},{8,10},{9,11},{10,... | collective-permute-start | bytes 1179656 | tf_op jit(solution)/shard_map/ppermute | solution.py:492
  43.3 2.6 collective-permute-start.14
  43.5 9.5 %collective-permute-start.20 = (bf16[2,96,768]{2,1,0:T(8,128)(2,1)S(1)}, bf16[2,96,768]{2,1,0:T(8,128)(2,1)S(1)}, u32[]{:S(2)}, u32[]{:S(2)}) collective-permute-start(bf16[2,96,768]{2,1,0:T(8,128)(2,1)S(1)} %maximum_select_fusion.6), channel_id=1, source_target_pairs={{0,8},{1,9},{2,18},{3,19},{4,12},{5,13},{6,22},{7,23},{8,0},{9,1},... | collective-permute-start | bytes 884744 | tf_op jit(solution)/shard_map/ppermute | solution.py:492
  43.6 9.9 %collective-permute-start.23 = (bf16[96,768]{1,0:T(8,128)(2,1)S(1)}, bf16[96,768]{1,0:T(8,128)(2,1)S(1)}, u32[]{:S(2)}, u32[]{:S(2)}) collective-permute-start(bf16[96,768]{1,0:T(8,128)(2,1)S(1)} %collective-permute-done.22), channel_id=1, source_target_pairs={{0,2},{1,3},{2,0},{3,1},{4,6},{5,7},{6,4},{7,5},{8,10},{9,11},{10,... | collective-permute-start | bytes 442376 | tf_op jit(solution)/shard_map/ppermute | solution.py:492
  45.9 7.7 %collective-permute-start.3 = (bf16[2,80,768]{2,1,0:T(8,128)(2,1)S(1)}, bf16[2,80,768]{2,1,0:T(8,128)(2,1)S(1)}, u32[]{:S(2)}, u32[]{:S(2)}) collective-permute-start(bf16[2,80,768]{2,1,0:T(8,128)(2,1)S(1)} %collective-permute-done.2), channel_id=1, source_target_pairs={{0,2},{1,3},{2,0},{3,1},{4,6},{5,7},{6,4},{7,5},{8,10},{9,11},{10,... | collective-permute-start | bytes 737288 | tf_op jit(solution)/shard_map/ppermute | solution.py:492
  46.4 8.4 %copy-start.3 = (bf16[2,4,128,768]{3,2,1,0:T(8,128)(2,1)}, bf16[2,4,128,768]{3,2,1,0:T(8,128)(2,1)S(1)}, u32[]{:S(2)}) copy-start(bf16[2,4,128,768]{3,2,1,0:T(8,128)(2,1)S(1)} %maximum_select_fusion.column) | copy-start | bytes 4718596
  46.4 39.2 %collective-permute-start.15 = (bf16[2,4,128,768]{3,2,1,0:T(8,128)(2,1)S(1)}, bf16[2,4,128,768]{3,2,1,0:T(8,128)(2,1)}, u32[]{:S(2)}, u32[]{:S(2)}) collective-permute-start(bf16[2,4,128,768]{3,2,1,0:T(8,128)(2,1)S(1)} %maximum_select_fusion.column), channel_id=1, source_target_pairs={{0,1},{1,0},{2,6},{3,7},{4,5},{5,4},{6,2},{7,3},{8,9},{9,8},{10,14... | collective-permute-start | bytes 4718600 | tf_op jit(solution)/shard_map/ppermute | solution.py:492
  53.0 3.3 collective-permute-start.21
  54.8 28.2 %collective-permute-start.6 = (bf16[2,4,80,768]{3,2,1,0:T(8,128)(2,1)}, bf16[2,4,80,768]{3,2,1,0:T(8,128)(2,1)}, u32[]{:S(2)}, u32[]{:S(2)}) collective-permute-start(bf16[2,4,80,768]{3,2,1,0:T(8,128)(2,1)} %maximum_select_fusion.2.column), channel_id=1, source_target_pairs={{0,1},{1,0},{2,6},{3,7},{4,5},{5,4},{6,2},{7,3},{8,9},{9,8},{10,14... | collective-permute-start | bytes 2949128 | tf_op jit(solution)/shard_map/ppermute | solution.py:492
  56.6 31.1 %copy-start.4 = (bf16[2,4,96,768]{3,2,1,0:T(8,128)(2,1)}, bf16[2,4,96,768]{3,2,1,0:T(8,128)(2,1)S(1)}, u32[]{:S(2)}) copy-start(bf16[2,4,96,768]{3,2,1,0:T(8,128)(2,1)S(1)} %maximum_select_fusion.1.column) | copy-start | bytes 3538948
  56.6 51.6 %collective-permute-start.24 = (bf16[2,4,96,768]{3,2,1,0:T(8,128)(2,1)S(1)}, bf16[2,4,96,768]{3,2,1,0:T(8,128)(2,1)}, u32[]{:S(2)}, u32[]{:S(2)}) collective-permute-start(bf16[2,4,96,768]{3,2,1,0:T(8,128)(2,1)S(1)} %maximum_select_fusion.1.column), channel_id=1, source_target_pairs={{0,1},{1,0},{2,6},{3,7},{4,5},{5,4},{6,2},{7,3},{8,9},{9,8},{10,14... | collective-permute-start | bytes 3538952 | tf_op jit(solution)/shard_map/ppermute | solution.py:492
  57.8 55.0 %collective-permute-start = (bf16[272,768]{1,0:T(8,128)(2,1)S(1)}, bf16[272,768]{1,0:T(8,128)(2,1)}, u32[]{:S(2)}, u32[]{:S(2)}) collective-permute-start(bf16[272,768]{1,0:T(8,128)(2,1)S(1)} %fusion.9), channel_id=1, source_target_pairs={{0,1},{1,0},{2,3},{3,2},{4,5},{5,4},{6,7},{7,6},{8,9},{9,8},{10,11... | collective-permute-start | bytes 1253384 | tf_op jit(solution)/shard_map/ppermute | solution.py:492
  84.0 31.7 %collective-permute-start.8 = (bf16[4,80,768]{2,1,0:T(8,128)(2,1)S(1)}, bf16[4,80,768]{2,1,0:T(8,128)(2,1)S(1)}, u32[]{:S(2)}, u32[]{:S(2)}) collective-permute-start(bf16[4,80,768]{2,1,0:T(8,128)(2,1)S(1)} %dynamic-slice_bitcast_fusion.2), channel_id=1, source_target_pairs={{0,4},{1,5},{2,3},{3,2},{4,0},{5,1},{6,7},{7,6},{8,12},{9,13},{10,... | collective-permute-start | bytes 1474568 | tf_op jit(solution)/shard_map/ppermute | solution.py:492
  87.7 36.1 %collective-permute-start.17 = (bf16[4,128,768]{2,1,0:T(8,128)(2,1)}, bf16[4,128,768]{2,1,0:T(8,128)(2,1)}, u32[]{:S(2)}, u32[]{:S(2)}) collective-permute-start(bf16[4,128,768]{2,1,0:T(8,128)(2,1)} %dynamic-slice_bitcast_fusion), channel_id=1, source_target_pairs={{0,4},{1,5},{2,3},{3,2},{4,0},{5,1},{6,7},{7,6},{8,12},{9,13},{10,... | collective-permute-start | bytes 2359304 | tf_op jit(solution)/shard_map/ppermute | solution.py:492
  88.2 61.4 %collective-permute-start.16 = (bf16[2,4,128,768]{3,2,1,0:T(8,128)(2,1)}, bf16[2,4,128,768]{3,2,1,0:T(8,128)(2,1)S(1)}, u32[]{:S(2)}, u32[]{:S(2)}) collective-permute-start(bf16[2,4,128,768]{3,2,1,0:T(8,128)(2,1)} %collective-permute-done.15.side), channel_id=1, source_target_pairs={{0,2},{1,3},{2,0},{3,1},{4,6},{5,7},{6,4},{7,5},{8,10},{9,11},{10,... | collective-permute-start | bytes 4718600 | tf_op jit(solution)/shard_map/ppermute | solution.py:492
  108.2 20.8 %collective-permute-start.7 = (bf16[2,4,80,768]{3,2,1,0:T(8,128)(2,1)}, bf16[2,4,80,768]{3,2,1,0:T(8,128)(2,1)}, u32[]{:S(2)}, u32[]{:S(2)}) collective-permute-start(bf16[2,4,80,768]{3,2,1,0:T(8,128)(2,1)} %collective-permute-done.6.side), channel_id=1, source_target_pairs={{0,2},{1,3},{2,0},{3,1},{4,6},{5,7},{6,4},{7,5},{8,10},{9,11},{10,... | collective-permute-start | bytes 2949128 | tf_op jit(solution)/shard_map/ppermute | solution.py:492
  112.9 10.1 %collective-permute-start.26 = (bf16[4,96,768]{2,1,0:T(8,128)(2,1)}, bf16[4,96,768]{2,1,0:T(8,128)(2,1)S(1)}, u32[]{:S(2)}, u32[]{:S(2)}) collective-permute-start(bf16[4,96,768]{2,1,0:T(8,128)(2,1)} %dynamic-slice_bitcast_fusion.1), channel_id=1, source_target_pairs={{0,4},{1,5},{2,3},{3,2},{4,0},{5,1},{6,7},{7,6},{8,12},{9,13},{10,... | collective-permute-start | bytes 1769480 | tf_op jit(solution)/shard_map/ppermute | solution.py:492
  116.5 48.8 %collective-permute-start.25 = (bf16[2,4,96,768]{3,2,1,0:T(8,128)(2,1)}, bf16[2,4,96,768]{3,2,1,0:T(8,128)(2,1)S(1)}, u32[]{:S(2)}, u32[]{:S(2)}) collective-permute-start(bf16[2,4,96,768]{3,2,1,0:T(8,128)(2,1)} %collective-permute-done.24.side), channel_id=1, source_target_pairs={{0,2},{1,3},{2,0},{3,1},{4,6},{5,7},{6,4},{7,5},{8,10},{9,11},{10,... | collective-permute-start | bytes 3538952 | tf_op jit(solution)/shard_map/ppermute | solution.py:492
  122.9 8.4 %collective-permute-start.9 = (bf16[4,80,768]{2,1,0:T(8,128)(2,1)}, bf16[4,80,768]{2,1,0:T(8,128)(2,1)}, u32[]{:S(2)}, u32[]{:S(2)}) collective-permute-start(bf16[4,80,768]{2,1,0:T(8,128)(2,1)} %copy-done.18), channel_id=1, source_target_pairs={{0,2},{1,3},{2,0},{3,1},{4,6},{5,7},{6,4},{7,5},{8,10},{9,11},{10,... | collective-permute-start | bytes 1474568 | tf_op jit(solution)/shard_map/ppermute | solution.py:492
  123.8 25.8 %collective-permute-start.18 = (bf16[4,128,768]{2,1,0:T(8,128)(2,1)}, bf16[4,128,768]{2,1,0:T(8,128)(2,1)S(1)}, u32[]{:S(2)}, u32[]{:S(2)}) collective-permute-start(bf16[4,128,768]{2,1,0:T(8,128)(2,1)} %collective-permute-done.17.corner), channel_id=1, source_target_pairs={{0,2},{1,3},{2,0},{3,1},{4,6},{5,7},{6,4},{7,5},{8,10},{9,11},{10,... | collective-permute-start | bytes 2359304 | tf_op jit(solution)/shard_map/ppermute | solution.py:492
  129.0 36.3 %collective-permute-start.27 = (bf16[4,96,768]{2,1,0:T(8,128)(2,1)}, bf16[4,96,768]{2,1,0:T(8,128)(2,1)S(1)}, u32[]{:S(2)}, u32[]{:S(2)}) collective-permute-start(bf16[4,96,768]{2,1,0:T(8,128)(2,1)} %copy-done.15), channel_id=1, source_target_pairs={{0,2},{1,3},{2,0},{3,1},{4,6},{5,7},{6,4},{7,5},{8,10},{9,11},{10,... | collective-permute-start | bytes 1769480 | tf_op jit(solution)/shard_map/ppermute | solution.py:492
  202.5 13.4 %copy-start.23 = (bf16[4,96,768]{2,1,0:T(8,128)(2,1)S(1)}, bf16[4,96,768]{2,1,0:T(8,128)(2,1)}, u32[]{:S(2)}) copy-start(bf16[4,96,768]{2,1,0:T(8,128)(2,1)} %get-tuple-element.100) | copy-start | bytes 1769476
  202.5 17.7 %copy-start.22 = (bf16[4,128,768]{2,1,0:T(8,128)(2,1)S(1)}, bf16[4,128,768]{2,1,0:T(8,128)(2,1)}, u32[]{:S(2)}) copy-start(bf16[4,128,768]{2,1,0:T(8,128)(2,1)} %get-tuple-element.95) | copy-start | bytes 2359300
  202.5 18.2 %copy-start.21 = (bf16[2,4,96,768]{3,2,1,0:T(8,128)(2,1)S(1)}, bf16[2,4,96,768]{3,2,1,0:T(8,128)(2,1)}, u32[]{:S(2)}) copy-start(bf16[2,4,96,768]{3,2,1,0:T(8,128)(2,1)} %get-tuple-element.98) | copy-start | bytes 3538948
  215.2 5.5 %copy-start.17 = (bf16[4,96,768]{2,1,0:T(8,128)(2,1)S(1)}, bf16[4,96,768]{2,1,0:T(8,128)(2,1)}, u32[]{:S(2)}) copy-start(bf16[4,96,768]{2,1,0:T(8,128)(2,1)} %get-tuple-element.99) | copy-start | bytes 1769476
  215.3 2.1 collective-permute-start.30
  215.3 13.7 %collective-permute-start.29 = (bf16[2,4,80,768]{3,2,1,0:T(8,128)(2,1)}, bf16[2,4,80,768]{3,2,1,0:T(8,128)(2,1)S(1)}, u32[]{:S(2)}, u32[]{:S(2)}) collective-permute-start(bf16[2,4,80,768]{3,2,1,0:T(8,128)(2,1)} %get-tuple-element.88), channel_id=1, source_target_pairs={{0,2},{1,3},{2,0},{3,1},{4,6},{5,7},{6,4},{7,5},{8,10},{9,11},{10,... | collective-permute-start | bytes 2949128 | tf_op jit(solution)/shard_map/ppermute | solution.py:492
  215.8 4.8 %collective-permute-start.46 = (bf16[4,96,768]{2,1,0:T(8,128)(2,1)S(1)}, bf16[4,96,768]{2,1,0:T(8,128)(2,1)S(1)}, u32[]{:S(2)}, u32[]{:S(2)}) collective-permute-start(bf16[4,96,768]{2,1,0:T(8,128)(2,1)S(1)} %copy-done.23), channel_id=1, source_target_pairs={{0,2},{1,3},{2,0},{3,1},{4,6},{5,7},{6,4},{7,5},{8,10},{9,11},{10,... | collective-permute-start | bytes 1769480 | tf_op jit(solution)/shard_map/ppermute | solution.py:492
  218.6 8.9 %collective-permute-start.31 = (bf16[4,80,768]{2,1,0:T(8,128)(2,1)S(1)}, bf16[4,80,768]{2,1,0:T(8,128)(2,1)S(1)}, u32[]{:S(2)}, u32[]{:S(2)}) collective-permute-start(bf16[4,80,768]{2,1,0:T(8,128)(2,1)S(1)} %add_convert_fusion.8), channel_id=1, source_target_pairs={{0,4},{1,5},{2,3},{3,2},{4,0},{5,1},{6,7},{7,6},{8,12},{9,13},{10,... | collective-permute-start | bytes 1474568 | tf_op jit(solution)/shard_map/ppermute | solution.py:492
  220.2 11.8 %collective-permute-start.38 = (bf16[4,128,768]{2,1,0:T(8,128)(2,1)S(1)}, bf16[4,128,768]{2,1,0:T(8,128)(2,1)S(1)}, u32[]{:S(2)}, u32[]{:S(2)}) collective-permute-start(bf16[4,128,768]{2,1,0:T(8,128)(2,1)S(1)} %copy-done.22), channel_id=1, source_target_pairs={{0,2},{1,3},{2,0},{3,1},{4,6},{5,7},{6,4},{7,5},{8,10},{9,11},{10,... | collective-permute-start | bytes 2359304 | tf_op jit(solution)/shard_map/ppermute | solution.py:492
  220.2 49.1 %collective-permute-start.37 = (bf16[2,4,128,768]{3,2,1,0:T(8,128)(2,1)}, bf16[2,4,128,768]{3,2,1,0:T(8,128)(2,1)S(1)}, u32[]{:S(2)}, u32[]{:S(2)}) collective-permute-start(bf16[2,4,128,768]{3,2,1,0:T(8,128)(2,1)} %get-tuple-element.93), channel_id=1, source_target_pairs={{0,2},{1,3},{2,0},{3,1},{4,6},{5,7},{6,4},{7,5},{8,10},{9,11},{10,... | collective-permute-start | bytes 4718600 | tf_op jit(solution)/shard_map/ppermute | solution.py:492
  220.7 24.3 %collective-permute-start.45 = (bf16[2,4,96,768]{3,2,1,0:T(8,128)(2,1)S(1)}, bf16[2,4,96,768]{3,2,1,0:T(8,128)(2,1)S(1)}, u32[]{:S(2)}, u32[]{:S(2)}) collective-permute-start(bf16[2,4,96,768]{3,2,1,0:T(8,128)(2,1)S(1)} %copy-done.21), channel_id=1, source_target_pairs={{0,2},{1,3},{2,0},{3,1},{4,6},{5,7},{6,4},{7,5},{8,10},{9,11},{10,... | collective-permute-start | bytes 3538952 | tf_op jit(solution)/shard_map/ppermute | solution.py:492
  220.8 8.3 %copy-start.12 = (bf16[2,4,80,768]{3,2,1,0:T(8,128)(2,1)S(1)}, bf16[2,4,80,768]{3,2,1,0:T(8,128)(2,1)}, u32[]{:S(2)}) copy-start(bf16[2,4,80,768]{3,2,1,0:T(8,128)(2,1)} %get-tuple-element.87) | copy-start | bytes 2949124
  227.5 15.0 %collective-permute-start.47 = (bf16[4,96,768]{2,1,0:T(8,128)(2,1)S(1)}, bf16[4,96,768]{2,1,0:T(8,128)(2,1)S(1)}, u32[]{:S(2)}, u32[]{:S(2)}) collective-permute-start(bf16[4,96,768]{2,1,0:T(8,128)(2,1)S(1)} %add_convert_fusion.7), channel_id=1, source_target_pairs={{0,4},{1,5},{2,3},{3,2},{4,0},{5,1},{6,7},{7,6},{8,12},{9,13},{10,... | collective-permute-start | bytes 1769480 | tf_op jit(solution)/shard_map/ppermute | solution.py:492
  230.5 37.0 %collective-permute-start.32 = (bf16[2,4,80,768]{3,2,1,0:T(8,128)(2,1)}, bf16[2,4,80,768]{3,2,1,0:T(8,128)(2,1)}, u32[]{:S(2)}, u32[]{:S(2)}) collective-permute-start(bf16[2,4,80,768]{3,2,1,0:T(8,128)(2,1)} %add_convert_fusion.5), channel_id=1, source_target_pairs={{0,1},{1,0},{2,6},{3,7},{4,5},{5,4},{6,2},{7,3},{8,9},{9,8},{10,14... | collective-permute-start | bytes 2949128 | tf_op jit(solution)/shard_map/ppermute | solution.py:492
  232.0 13.0 %copy-start.10 = (bf16[2,4,96,768]{3,2,1,0:T(8,128)(2,1)S(1)}, bf16[2,4,96,768]{3,2,1,0:T(8,128)(2,1)}, u32[]{:S(2)}) copy-start(bf16[2,4,96,768]{3,2,1,0:T(8,128)(2,1)} %get-tuple-element.97) | copy-start | bytes 3538948
  232.2 34.0 %collective-permute-start.39 = (bf16[4,128,768]{2,1,0:T(8,128)(2,1)S(1)}, bf16[4,128,768]{2,1,0:T(8,128)(2,1)}, u32[]{:S(2)}, u32[]{:S(2)}) collective-permute-start(bf16[4,128,768]{2,1,0:T(8,128)(2,1)S(1)} %add_convert_fusion.6), channel_id=1, source_target_pairs={{0,4},{1,5},{2,3},{3,2},{4,0},{5,1},{6,7},{7,6},{8,12},{9,13},{10,... | collective-permute-start | bytes 2359304 | tf_op jit(solution)/shard_map/ppermute | solution.py:492
  242.4 20.7 %collective-permute-start.28 = (bf16[256,768]{1,0:T(8,128)(2,1)}, bf16[256,768]{1,0:T(8,128)(2,1)}, u32[]{:S(2)}, u32[]{:S(2)}) collective-permute-start(bf16[256,768]{1,0:T(8,128)(2,1)} %get-tuple-element.84), channel_id=1, source_target_pairs={{0,1},{1,0},{2,3},{3,2},{4,5},{5,4},{6,7},{7,6},{8,9},{9,8},{10,11... | collective-permute-start | bytes 1179656 | tf_op jit(solution)/shard_map/ppermute | solution.py:492
  245.5 30.3 %collective-permute-start.48 = (bf16[2,4,96,768]{3,2,1,0:T(8,128)(2,1)S(1)}, bf16[2,4,96,768]{3,2,1,0:T(8,128)(2,1)}, u32[]{:S(2)}, u32[]{:S(2)}) collective-permute-start(bf16[2,4,96,768]{3,2,1,0:T(8,128)(2,1)S(1)} %add_convert_fusion.3), channel_id=1, source_target_pairs={{0,1},{1,0},{2,6},{3,7},{4,5},{5,4},{6,2},{7,3},{8,9},{9,8},{10,14... | collective-permute-start | bytes 3538952 | tf_op jit(solution)/shard_map/ppermute | solution.py:492
  269.2 8.4 %collective-permute-start.33 = (bf16[4,80,768]{2,1,0:T(8,128)(2,1)S(1)}, bf16[4,80,768]{2,1,0:T(8,128)(2,1)S(1)}, u32[]{:S(2)}, u32[]{:S(2)}) collective-permute-start(bf16[4,80,768]{2,1,0:T(8,128)(2,1)S(1)} %broadcast_select_fusion.2), channel_id=1, source_target_pairs={{0,2},{1,3},{2,0},{3,1},{4,6},{5,7},{6,4},{7,5},{8,10},{9,11},{10,... | collective-permute-start | bytes 1474568 | tf_op jit(solution)/shard_map/ppermute | solution.py:492
  270.4 5.4 %copy-start.9 = (bf16[2,4,96,768]{3,2,1,0:T(8,128)(2,1)S(1)}, bf16[2,4,96,768]{3,2,1,0:T(8,128)(2,1)}, u32[]{:S(2)}) copy-start(bf16[2,4,96,768]{3,2,1,0:T(8,128)(2,1)} %get-tuple-element.96) | copy-start | bytes 3538948
  271.1 21.4 %collective-permute-start.40 = (bf16[2,4,128,768]{3,2,1,0:T(8,128)(2,1)S(1)}, bf16[2,4,128,768]{3,2,1,0:T(8,128)(2,1)S(1)}, u32[]{:S(2)}, u32[]{:S(2)}) collective-permute-start(bf16[2,4,128,768]{3,2,1,0:T(8,128)(2,1)S(1)} %add_convert_fusion.1), channel_id=1, source_target_pairs={{0,1},{1,0},{2,6},{3,7},{4,5},{5,4},{6,2},{7,3},{8,9},{9,8},{10,14... | collective-permute-start | bytes 4718600 | tf_op jit(solution)/shard_map/ppermute | solution.py:492
  277.8 11.0 %collective-permute-start.34 = (bf16[2,80,768]{2,1,0:T(8,128)(2,1)S(1)}, bf16[2,80,768]{2,1,0:T(8,128)(2,1)S(1)}, u32[]{:S(2)}, u32[]{:S(2)}) collective-permute-start(bf16[2,80,768]{2,1,0:T(8,128)(2,1)S(1)} %slice.289), channel_id=1, source_target_pairs={{0,8},{1,9},{2,18},{3,19},{4,12},{5,13},{6,22},{7,23},{8,0},{9,1},... | collective-permute-start | bytes 737288 | tf_op jit(solution)/shard_map/ppermute | solution.py:492
  279.0 10.6 %collective-permute-start.35 = (bf16[80,768]{1,0:T(8,128)(2,1)S(1)}, bf16[80,768]{1,0:T(8,128)(2,1)S(1)}, u32[]{:S(2)}, u32[]{:S(2)}) collective-permute-start(bf16[80,768]{1,0:T(8,128)(2,1)S(1)} %slice_bitcast_fusion.20), channel_id=1, source_target_pairs={{0,24},{1,25},{2,26},{3,27},{4,28},{5,29},{6,30},{7,31},{8,16},{9,... | collective-permute-start | bytes 368648 | tf_op jit(solution)/shard_map/ppermute | solution.py:492
  288.8 1.4 collective-permute-start.36
  289.0 3.0 collective-permute-start.49
  292.3 8.8 %collective-permute-start.50 = (bf16[2,96,768]{2,1,0:T(8,128)(2,1)S(1)}, bf16[2,96,768]{2,1,0:T(8,128)(2,1)S(1)}, u32[]{:S(2)}, u32[]{:S(2)}) collective-permute-start(bf16[2,96,768]{2,1,0:T(8,128)(2,1)S(1)} %slice.317), channel_id=1, source_target_pairs={{0,8},{1,9},{2,18},{3,19},{4,12},{5,13},{6,22},{7,23},{8,0},{9,1},... | collective-permute-start | bytes 884744 | tf_op jit(solution)/shard_map/ppermute | solution.py:492
  294.2 13.6 %collective-permute-start.41 = (bf16[4,128,768]{2,1,0:T(8,128)(2,1)S(1)}, bf16[4,128,768]{2,1,0:T(8,128)(2,1)S(1)}, u32[]{:S(2)}, u32[]{:S(2)}) collective-permute-start(bf16[4,128,768]{2,1,0:T(8,128)(2,1)S(1)} %broadcast_select_fusion), channel_id=1, source_target_pairs={{0,2},{1,3},{2,0},{3,1},{4,6},{5,7},{6,4},{7,5},{8,10},{9,11},{10,... | collective-permute-start | bytes 2359304 | tf_op jit(solution)/shard_map/ppermute | solution.py:492
  294.4 13.3 %collective-permute-start.51 = (bf16[96,768]{1,0:T(8,128)(2,1)S(1)}, bf16[96,768]{1,0:T(8,128)(2,1)S(1)}, u32[]{:S(2)}, u32[]{:S(2)}) collective-permute-start(bf16[96,768]{1,0:T(8,128)(2,1)S(1)} %slice_bitcast_fusion.11), channel_id=1, source_target_pairs={{0,24},{1,25},{2,26},{3,27},{4,28},{5,29},{6,30},{7,31},{8,16},{9,... | collective-permute-start | bytes 442376 | tf_op jit(solution)/shard_map/ppermute | solution.py:492
  301.1 6.6 %collective-permute-start.52 = (bf16[96,768]{1,0:T(8,128)(2,1)S(1)}, bf16[96,768]{1,0:T(8,128)(2,1)S(1)}, u32[]{:S(2)}, u32[]{:S(2)}) collective-permute-start(bf16[96,768]{1,0:T(8,128)(2,1)S(1)} %dynamic-slice_bitcast_fusion.4), channel_id=1, source_target_pairs={{0,2},{1,3},{2,0},{3,1},{4,6},{5,7},{6,4},{7,5},{8,10},{9,11},{10,... | collective-permute-start | bytes 442376 | tf_op jit(solution)/shard_map/ppermute | solution.py:492
  308.2 9.7 %collective-permute-start.42 = (bf16[2,128,768]{2,1,0:T(8,128)(2,1)S(1)}, bf16[2,128,768]{2,1,0:T(8,128)(2,1)S(1)}, u32[]{:S(2)}, u32[]{:S(2)}) collective-permute-start(bf16[2,128,768]{2,1,0:T(8,128)(2,1)S(1)} %slice.302), channel_id=1, source_target_pairs={{0,8},{1,9},{2,18},{3,19},{4,12},{5,13},{6,22},{7,23},{8,0},{9,1},... | collective-permute-start | bytes 1179656 | tf_op jit(solution)/shard_map/ppermute | solution.py:492
  308.3 20.9 %copy-start.1 = (bf16[321,12]{0,1:T(8,128)(2,1)S(1)}, bf16[321,12]{0,1:T(8,128)(2,1)}, u32[]{:S(2)}) copy-start(bf16[321,12]{0,1:T(8,128)(2,1)} %param.36) | copy-start | bytes 23116
  308.3 19.0 %collective-permute-start.43 = (bf16[128,768]{1,0:T(8,128)(2,1)S(1)}, bf16[128,768]{1,0:T(8,128)(2,1)S(1)}, u32[]{:S(2)}, u32[]{:S(2)}) collective-permute-start(bf16[128,768]{1,0:T(8,128)(2,1)S(1)} %slice_bitcast_fusion.2), channel_id=1, source_target_pairs={{0,24},{1,25},{2,26},{3,27},{4,28},{5,29},{6,30},{7,31},{8,16},{9,... | collective-permute-start | bytes 589832 | tf_op jit(solution)/shard_map/ppermute | solution.py:492
  317.9 9.8 %collective-permute-start.44 = (bf16[128,768]{1,0:T(8,128)(2,1)S(1)}, bf16[128,768]{1,0:T(8,128)(2,1)S(1)}, u32[]{:S(2)}, u32[]{:S(2)}) collective-permute-start(bf16[128,768]{1,0:T(8,128)(2,1)S(1)} %dynamic-slice_bitcast_fusion.3), channel_id=1, source_target_pairs={{0,2},{1,3},{2,0},{3,1},{4,6},{5,7},{6,4},{7,5},{8,10},{9,11},{10,... | collective-permute-start | bytes 589832 | tf_op jit(solution)/shard_map/ppermute | solution.py:492
  (15 other events, 20.3 us)

commit v2 on v1

--- a/solution.py
+++ b/solution.py
@@ -488,60 +488,45 @@
     return pairs
 
 
-def shift(array, move):
-    return lax.ppermute(array, AXES, route(move))
+def shift(array, move, name="swap"):
+    with jax.named_scope(name):
+        return lax.ppermute(array, AXES, route(move))
 
 
 CORE = ((1, 0), (1, 0))
 SIDE = ((0, 1), (2, 0))
 OTHER_SIDE = ((2, 0), (0, 1))
 PACK = ((0, 1), (0, 1))
-NEAR_Z = ((4, 0), (8, 0))
-FAR_Z = ((12, 0), (12, 0))
-
-
-def gather_units(unit, core):
-    first = core == 0
-    twin = shift(unit, CORE)
-    far = shift(unit, FAR_Z)
-    both = jnp.where(first, jnp.stack([unit, twin]), jnp.stack([twin, unit]))
-    near = shift(both, NEAR_Z)
-    far_twin = shift(far, CORE)
-    near_twin = shift(near, CORE)
-    column = jnp.where(
-        first,
-        jnp.stack([both, near, near_twin, jnp.stack([far, far_twin])], axis=1),
-        jnp.stack([both, near_twin, near, jnp.stack([far_twin, far])], axis=1),
-    )
-    side = shift(column, SIDE)
-    corner = shift(lax.dynamic_index_in_dim(side, core, 0, keepdims=False), OTHER_SIDE)
-    return (column, side, shift(side, CORE), corner, shift(corner, CORE))
-
-
-def scatter_units(parts, core):
-    corner_send, corner_keep, side_send, side_keep, own = parts
-    corner_got = shift(corner_send, CORE)
-    side_got = shift(side_send, CORE)
-    corner = (corner_keep.astype(F32) + corner_got.astype(F32)).astype(LOW)
-    turned = shift(corner, OTHER_SIDE)
-    plane = (jnp.arange(2) == core)[:, None, None, None]
-    side = (
-        side_keep.astype(F32)
-        + side_got.astype(F32)
-        + jnp.where(plane, turned[None].astype(F32), 0.0)
-    ).astype(LOW)
-    column = (own.astype(F32) + shift(side, SIDE).astype(F32)).astype(LOW)
-    of_first = jnp.stack([column[0, 1], column[1, 1], column[0, 3], column[0, 0]])
-    of_second = jnp.stack([column[0, 2], column[1, 2], column[1, 3], column[1, 0]])
-    first = core == 0
-    got = shift(jnp.where(first, of_second, of_first), CORE)
-    total = jnp.where(first, of_first, of_second).astype(F32) + got.astype(F32)
-    total_low = total.astype(LOW)
-    near = shift(total_low[:2], NEAR_Z)
-    far = shift(total_low[2], FAR_Z)
-    near_twin = shift(lax.dynamic_index_in_dim(near, 1 - core, 0, keepdims=False), CORE)
-    near_own = lax.dynamic_index_in_dim(near, core, 0, keepdims=False)
-    return total[3] + near_own.astype(F32) + far.astype(F32) + near_twin.astype(F32)
+ALONG_Z = tuple(((4 * turn, 0), (4 * turn, 0)) for turn in (1, 2, 3))
+
+
+def tied(value, *after):
+    return lax.optimization_barrier((value,) + after)[0]
+
+
+def joined(*groups):
+    return lax.optimization_barrier(groups)
+
+
+def twin(array, name="twin"):
+    return shift(array, CORE, name)
+
+
+def along_z(unit, name):
+    return tuple(shift(unit, move, name + "_z") for move in ALONG_Z)
+
+
+def added(keep, sent):
+    return keep.astype(F32) + twin(sent).astype(F32)
+
+
+def z_sends(plane, name):
+    low = plane.astype(LOW)
+    return tuple(shift(low[n + 1], move, name + "_z") for n, move in enumerate(ALONG_Z))
+
+
+def z_sum(plane, arrived):
+    return plane[0] + sum(part.astype(F32) for part in arrived)
 
 
 def unit_of(place, x_turn, y_turn, z_turn, c):
@@ -549,38 +534,21 @@
     return ((z * 2 + y) * 2 + c) * 2 + x
 
 
-def gathered_copies(place, pieces):
-    column, side, side_twin, corner, corner_twin = pieces
+def planes_of(place):
     c0 = place[3]
     found = []
-    for z in range(4):
-        for c in range(2):
-            found.append((column.at[c, z], unit_of(place, 0, 0, z, c)))
-            found.append((side.at[c, z], unit_of(place, 1 - c0, c0, z, c)))
-            found.append((side_twin.at[c, z], unit_of(place, c0, 1 - c0, z, c)))
-        found.append((corner.at[z], unit_of(place, 1, 1, z, c0)))
-        found.append((corner_twin.at[z], unit_of(place, 1, 1, z, 1 - c0)))
-    return found
-
-
-def scattered_copies(place, parts):
-    corner_send, corner_keep, side_send, side_keep, own = parts
-    c0 = place[3]
-    found = []
-    for z in range(4):
-        for c in range(2):
-            found.append((own.at[c, z], unit_of(place, 0, 0, z, c)))
-            found.append((side_keep.at[c, z], unit_of(place, 1 - c0, c0, z, c)))
-            found.append((side_send.at[c, z], unit_of(place, c0, 1 - c0, z, c)))
-        found.append((corner_keep.at[z], unit_of(place, 1, 1, z, c0)))
-        found.append((corner_send.at[z], unit_of(place, 1, 1, z, 1 - c0)))
+    for plane in range(2):
+        c = c0 if plane == 0 else 1 - c0
+        for z in range(4):
+            for n, (x_turn, y_turn) in enumerate(((0, 0), (1 - c, c), (c, 1 - c), (1, 1))):
+                found.append((4 * plane + n, z, unit_of(place, x_turn, y_turn, z, c)))
     return found
 
 
 def load_units(place, pieces, stage, sems):
     copies = [
-        pltpu.make_async_copy(ref, stage.at[unit], sems.at[n])
-        for n, (ref, unit) in enumerate(gathered_copies(place, pieces))
+        pltpu.make_async_copy(pieces[array].at[z], stage.at[unit], sems.at[n])
+        for n, (array, z, unit) in enumerate(planes_of(place))
     ]
     for copy in copies:
         copy.start()
@@ -589,8 +557,8 @@
 
 def store_units(place, stage, parts, sems):
     copies = [
-        pltpu.make_async_copy(stage.at[unit], ref, sems.at[n])
-        for n, (ref, unit) in enumerate(scattered_copies(place, parts))
+        pltpu.make_async_copy(stage.at[unit], parts[array].at[z], sems.at[n])
+        for n, (array, z, unit) in enumerate(planes_of(place))
     ]
     for copy in copies:
         copy.start()
@@ -599,9 +567,7 @@
 
 
 def part_shapes(rows, width):
-    quarter = jax.ShapeDtypeStruct((4, rows, width), LOW)
-    half = jax.ShapeDtypeStruct((2, 4, rows, width), LOW)
-    return [quarter, quarter, half, half, half]
+    return [jax.ShapeDtypeStruct((4, rows, width), LOW)] * 8
 
 
 def dot_nn(a, b):
@@ -646,27 +612,30 @@
 
 
 def project_kernel(
-    place, own, mate, column, side, side_twin, corner, corner_twin, wide_one, wide_two, wide_four,
-    first, queries, keys, values, weight, vectors, up_bias, stage, small, sems,
+    place, own, other, p0, p1, p2, p3, p4, p5, p6, p7, wide_one, wide_two, wide_four,
+    first, queries, keys, values, weight, vectors, up_bias, mate_live, stage, small, sems,
 ):
     units = stage.shape[0]
     width = own.shape[1]
     rows = stage.shape[1] - PAD
     shard_len = own.shape[0]
-    copies = load_units(place, (column, side, side_twin, corner, corner_twin), stage, sems)
+    copies = load_units(place, (p0, p1, p2, p3, p4, p5, p6, p7), stage, sems)
 
     def normed(frames):
         wide = frames.astype(F32)
         center = wide - jnp.mean(wide, axis=1, keepdims=True)
         return center * lax.rsqrt(jnp.mean(center * center, axis=1, keepdims=True) + EPSILON)
 
-    own_normed, mate_normed = normed(own[...]), normed(mate[...])
+    own_normed, mate_normed = normed(own[...]), normed(other[...])
     for copy in copies:
         copy.wait()
     for unit in range(units):
         top = stage[unit, rows : rows + PAD, :].astype(F32)
         small[0, unit : unit + 1, :] = top[0:1]
         small[1, unit : unit + 1, :] = top[1:2]
+
+    mate = unit_of(place, 1, 0, 0, place[3])
+    mate_live[...] = stage[mate, rows : rows + PAD, : mate_live.shape[1]].astype(F32)
 
     def spread(row, slot, table):
         held = small[row, :, slot * LANES : (slot + 1) * LANES].astype(LOW)
@@ -702,14 +671,36 @@
     return (lax.broadcasted_iota(jnp.int32, shape, 1) // HD) == head
 
 
-def attend_kernel(place, queries, keys, values, curve, hidden_pairs, probs, mixed):
+def attend_kernel(
+    place, lengths, queries, keys, values, curve, own_live, mate_live, probs, mixed, hidden_pairs
+):
     q, k, v = queries[...], keys[...], values[...]
     block_len, span = hidden_pairs.shape
+    step = pl.program_id(0)
+
+    @pl.when(step == 0)
+    def _():
+        start = place[0] * block_len
+        key_pos = lax.broadcasted_iota(jnp.int32, (1, span), 1)
+        query_pos = lax.broadcasted_iota(jnp.int32, (block_len, 1), 0) + start
+        key_doc, query_doc = jnp.zeros_like(key_pos), jnp.zeros_like(query_pos)
+        end = 0
+        for n in range(lengths.shape[1]):
+            end = end + lengths[0, n]
+            key_doc = key_doc + (key_pos >= end).astype(jnp.int32)
+            query_doc = query_doc + (query_pos >= end).astype(jnp.int32)
+        one, two = own_live[...].astype(F32), mate_live[2:3, :]
+        live = jnp.where(
+            place[0] == 0, jnp.concatenate([one, two], axis=1), jnp.concatenate([two, one], axis=1)
+        )
+        allowed = (query_doc == key_doc) & ((live > 0.5) | (query_pos == key_pos))
+        hidden_pairs[...] = jnp.where(allowed, 0.0, MASKED)
+
     total = jnp.zeros(q.shape, F32)
     for head in range(2):
         q_head = jnp.where(half_mask(q.shape, head), q, 0) * (1.0 / math.sqrt(HD))
         bias = pltpu.roll(
-            jnp.broadcast_to(curve[0, head : head + 1, :], (block_len, block_len + span)),
+            jnp.broadcast_to(curve[pl.ds(2 * step + head, 1), :], (block_len, block_len + span)),
             span + 1, 1, stride=1, stride_axis=0,
         )[:, :span]
         logits = dot_nt(q_head.astype(LOW), k) + bias + hidden_pairs[...]
@@ -721,14 +712,15 @@
 
 
 def expand_kernel(
-    place, frames, mixed, vectors, up_bias, column, side, side_twin, corner, corner_twin,
+    place, frames, mixed, vectors, up_bias, p0, p1, p2, p3, p4, p5, p6, p7,
     middle, second, active, slope, context, up, out, stage, sems, out_sems,
 ):
     units, kept, width = stage.shape
-    rows = column.shape[2] - kept
-    found = gathered_copies(place, (column, side, side_twin, corner, corner_twin))
+    rows = p0.shape[1] - kept
+    pieces = (p0, p1, p2, p3, p4, p5, p6, p7)
     copies = []
-    for n, (ref, unit) in enumerate(found):
+    for n, (array, z, unit) in enumerate(planes_of(place)):
+        ref = pieces[array].at[z]
         at = pl.multiple_of(unit * rows, rows)
         copies.append(pltpu.make_async_copy(ref.at[:rows], up.at[pl.ds(at, rows)], sems.at[n]))
         copies.append(pltpu.make_async_copy(ref.at[rows:], stage.at[unit], out_sems.at[n]))
@@ -761,7 +753,7 @@
 
 
 def down_grad_kernel(
-    place, active, cotangent, corner_send, corner_keep, side_send, side_keep, own, bias_grad, stage, sems
+    place, active, cotangent, o0, o1, o2, o3, o4, o5, o6, o7, bias_grad, stage, sems
 ):
     units, rows, width = stage.shape
     each = width // units
@@ -780,44 +772,44 @@
             stage[start + n] = jnp.concatenate(
                 [grad[n * each : (n + 1) * each] for grad in grads], axis=0
             ).astype(LOW)
-    store_units(place, stage, (corner_send, corner_keep, side_send, side_keep, own), sems)
-
-
-def back_kernel(
-    place, cotangent, slope, second, middle, context, vectors, up, out,
-    column, side, side_twin, corner, corner_twin,
-    corner_send, corner_keep, side_send, side_keep, own,
-    down, middle_grad, context_grad, vector_grads, up_bias_grad,
-    stage, hidden_grad, out_stage, up_stage, sems,
+    store_units(place, stage, (o0, o1, o2, o3, o4, o5, o6, o7), sems)
+
+
+def hidden_grad_kernel(
+    place, cotangent, slope, p0, p1, p2, p3, p4, p5, p6, p7,
+    down, up_bias_grad, hidden_grad, stage, sems,
 ):
     units, rows, width = stage.shape
     each = width // units
     folds = rows // each
-    shard_len = cotangent.shape[0]
-    copies = load_units(place, (column, side, side_twin, corner, corner_twin), stage, sems)
+    copies = load_units(place, (p0, p1, p2, p3, p4, p5, p6, p7), stage, sems)
     for copy in copies:
         copy.wait()
     for pair in range(units // 2):
         one, two = stage[2 * pair].astype(F32), stage[2 * pair + 1].astype(F32)
         for fold in range(folds):
-            joined = jnp.concatenate(
+            both = jnp.concatenate(
                 [one[fold * each : (fold + 1) * each], two[fold * each : (fold + 1) * each]], axis=0
             )
             down[2 * each * pair : 2 * each * (pair + 1), fold * width : (fold + 1) * width] = (
-                joined.astype(LOW)
+                both.astype(LOW)
             )
     dy = cotangent[...]
     tile = 2 * LANES
-    up_rows = up.shape[0] // units
-    second_grad = jnp.zeros((shard_len, width), F32)
-    for n in range(up.shape[0] // tile):
+    for n in range(hidden_grad.shape[1] // tile):
         at = slice(n * tile, (n + 1) * tile)
         grad = (dot_nn(dy, down[:, at]) * slope[:, at]).astype(LOW)
         hidden_grad[:, at] = grad
         up_bias_grad[:, at] = jnp.broadcast_to(
             jnp.sum(grad.astype(F32), axis=0, keepdims=True), (up_bias_grad.shape[0], tile)
         )
-        second_grad = second_grad + dot_nn(grad, up[at, :])
+
+
+def middle_grad_kernel(
+    cotangent, hidden_grad, middle, vectors, up, out, middle_grad, context_grad, vector_grads, branch_grad
+):
+    width = cotangent.shape[1]
+    second_grad = dot_nn(hidden_grad[...], up[...])
     mid = middle[...]
     center = mid - jnp.mean(mid, axis=1, keepdims=True)
     inv_std = lax.rsqrt(jnp.mean(center * center, axis=1, keepdims=True) + EPSILON)
@@ -828,7 +820,7 @@
         - jnp.mean(scaled, axis=1, keepdims=True)
         - normed * jnp.mean(scaled * normed, axis=1, keepdims=True)
     )
-    mid_grad = dy.astype(F32) + inner * inv_std
+    mid_grad = cotangent[...].astype(F32) + inner * inv_std
     middle_grad[...] = mid_grad
     branch = mid_grad.astype(LOW)
     vector_grads[...] = jnp.concatenate(
@@ -840,8 +832,18 @@
         ],
         axis=0,
     )
+    branch_grad[...] = branch
     context_grad[...] = dot_nn(branch, out[...]).astype(LOW)
-    out_grad = dot_tn(branch, context[...])
+
+
+def up_grad_kernel(
+    place, hidden_grad, second, branch_grad, context,
+    o0, o1, o2, o3, o4, o5, o6, o7, out_stage, up_stage, sems,
+):
+    units, _, width = up_stage.shape
+    each = width // units
+    up_rows = hidden_grad.shape[1] // units
+    out_grad = dot_tn(branch_grad[...], context[...])
     blank = jnp.zeros((rows_left(each), width), F32)
     for unit in range(units):
         out_stage[unit] = jnp.concatenate(
@@ -854,7 +856,7 @@
         for n in range(batch):
             up_stage[start + n, :up_rows] = grad[n * up_rows : (n + 1) * up_rows]
             up_stage[start + n, up_rows:] = out_stage[start + n]
-    store_units(place, up_stage, (corner_send, corner_keep, side_send, side_keep, own), sems)
+    store_units(place, up_stage, (o0, o1, o2, o3, o4, o5, o6, o7), sems)
 
 
 def rows_left(each):
@@ -888,7 +890,7 @@
         dv = dv + dot_tn(prob, dout_head)
         turned = jnp.concatenate([dot_nn(turn, raw), blank], axis=1)
         sheared = pltpu.roll(turned, 0, 1, stride=1, stride_axis=0)
-        diagonals[0, head : head + 1, :] = jnp.sum(sheared, axis=0, keepdims=True) * math.sqrt(HD)
+        diagonals[pl.ds(2 * pl.program_id(0) + head, 1), :] = jnp.sum(sheared, axis=0, keepdims=True) * math.sqrt(HD)
     query_grad[...] = dq.astype(LOW)
     key_grad[...] = dk.astype(LOW)
     value_grad[...] = dv.astype(LOW)
@@ -897,7 +899,7 @@
 def qkv_grad_kernel(
     place, own_frames, mate_frames, first, query_grad, key_grad, value_grad, weight, vectors,
     diagonals, buckets, vector_grads, down_bias_grad, up_bias_grad, wide_one, wide_two, wide_four,
-    corner_send, corner_keep, side_send, side_keep, own, own_grad, mate_grad, grads, small, stage, sems,
+    o0, o1, o2, o3, o4, o5, o6, o7, own_grad, mate_grad, grads, small, stage, sems,
 ):
     units, full, width = stage.shape
     rows = full - PAD
@@ -959,7 +961,7 @@
             ],
             axis=0,
         ).astype(LOW)
-    store_units(place, stage, (corner_send, corner_keep, side_send, side_keep, own), sems)
+    store_units(place, stage, (o0, o1, o2, o3, o4, o5, o6, o7), sems)
 
 
 def input_grad_kernel(frames, own_grad, mate_part, middle_grad, vectors, frames_grad):
@@ -974,6 +976,41 @@
         - normed * jnp.mean(scaled * normed, axis=1, keepdims=True)
     )
     frames_grad[...] = middle_grad[...] + inner * inv_std
+
+
+def pack_kernel(
+    live, qkv, out, up, down, first_gain, first_shift, second_gain, second_shift, out_bias,
+    down_bias, qv_bias, up_bias, qkv_unit, up_unit, down_unit,
+):
+    each, width = out.shape
+
+    def slots(vectors):
+        parts = []
+        for vector in vectors:
+            wide = vector[...].astype(F32)
+            parts += [wide, jnp.zeros((1, LANES - wide.shape[1]), F32)]
+        left = width - LANES * len(vectors)
+        if left:
+            parts.append(jnp.zeros((1, left), F32))
+        return jnp.concatenate(parts, axis=1)
+
+    narrow = slots((first_gain, first_shift, second_gain, second_shift, out_bias, down_bias))
+    wide = slots((qv_bias, up_bias))
+    seen = live[...].astype(F32)
+    seen = jnp.concatenate([seen, jnp.zeros((1, width - seen.shape[1]), F32)], axis=1)
+    blank = jnp.zeros((PAD - 3, width), F32)
+    qkv_unit[...] = jnp.concatenate([qkv[...].astype(F32), narrow, wide, seen, blank], axis=0).astype(LOW)
+    blank = jnp.zeros((up_unit.shape[0] - up.shape[0] - each, width), F32)
+    up_unit[...] = jnp.concatenate(
+        [up[...].astype(F32), out[...].astype(F32), blank], axis=0
+    ).astype(LOW)
+    down_unit[...] = jnp.concatenate(
+        [
+            down[:, fold * width : (fold + 1) * width].astype(F32)
+            for fold in range(down.shape[1] // width)
+        ],
+        axis=0,
+    ).astype(LOW)
 
 
 def paired_body(
@@ -995,71 +1032,77 @@
     down_rows = each * folds
     out_rows = each + rows_left(each)
 
-    def slot(vector):
-        return jnp.pad(vector, (0, LANES - vector.shape[0]))
-
-    narrow_row = jnp.concatenate(
-        [slot(v) for v in (first_gain, first_shift, second_gain, second_shift, out_bias, down_bias)]
-    )
-    wide_row = jnp.pad(
-        jnp.concatenate([slot(query_value_bias), slot(up_bias)]), (0, width - 2 * LANES)
-    )
-    small_rows = jnp.pad(jnp.stack([narrow_row, wide_row]), ((0, PAD - 2), (0, 0)))
-    qkv_unit = jnp.concatenate([qkv_weight.T, small_rows])
-    out_unit = jnp.concatenate(
-        [up_weight.T, out_weight.T, jnp.zeros((out_rows - each, width), LOW)]
-    )
-    down_unit = jnp.concatenate(
-        [down_weight.T[:, fold * width : (fold + 1) * width] for fold in range(folds)]
-    )
-    live_row = jnp.pad(key_mask.astype(LOW), (0, width - shard_len))
-    sent = jnp.concatenate([frames, jnp.pad(live_row[None], ((0, 15), (0, 0)))])
-    got = shift(sent, PACK)
-    mate_frames, mate_live = got[:shard_len], got[shard_len, :shard_len]
-    qkv_pieces = gather_units(qkv_unit, core)
-    up_pieces = gather_units(out_unit, core)
-    down_pieces = gather_units(down_unit, core)
-
-    seq_ends = jnp.cumsum(seq_lengths[0])
-    key_pos = jnp.arange(span, dtype=jnp.int32)
-    key_doc = doc_numbers(seq_ends, key_pos)
-    query_pos = x * shard_len + jnp.arange(shard_len, dtype=jnp.int32)
-    query_doc = doc_numbers(seq_ends, query_pos)
-    own_live = key_mask.astype(LOW)
-    live = jnp.where(
-        x == 0, jnp.concatenate([own_live, mate_live]), jnp.concatenate([mate_live, own_live])
-    )
-    allowed = (query_doc[:, None] == key_doc[None, :]) & (
-        (live[None, :] > 0.5) | (query_pos[:, None] == key_pos[None, :])
-    )
-    hidden_pairs = jnp.where(allowed, 0.0, MASKED).astype(F32)
+    def shape(*dims, kind=LOW):
+        return jax.ShapeDtypeStruct(dims, kind)
+
+    def row(vector):
+        return vector.reshape(1, vector.shape[0])
+
+    packed = (
+        row(key_mask), qkv_weight.T, out_weight.T, up_weight.T, down_weight.T, row(first_gain),
+        row(first_shift), row(second_gain), row(second_shift), row(out_bias), row(down_bias),
+        row(query_value_bias), row(up_bias),
+    )
+    qkv_unit, up_unit, down_unit = call(
+        pack_kernel,
+        [VMEM] * len(packed),
+        [shape(qkv_rows + PAD, width), shape(up_rows + out_rows, width), shape(down_rows, width)],
+        [VMEM] * 3,
+        [],
+        packed,
+        0,
+        name="pack",
+    )
+    def twins(pieces):
+        return tuple(pieces) + tuple(twin(piece) for piece in pieces)
+
+    qkv_z = along_z(qkv_unit, "qkv")
+    mate_frames = shift(tied(frames, qkv_unit), PACK, "frames_pack")
+    qkv_z, mate_frames = joined(qkv_z, mate_frames)
+    qkv_own = jnp.stack((qkv_unit,) + qkv_z)
+    qkv_side = shift(qkv_own, SIDE, "qkv_1")
+    up_first = tied(up_unit, qkv_own)
+    up_z = [shift(up_first, move, "up_z") for move in ALONG_Z[:2]]
+    qkv_side, up_z = joined(qkv_side, up_z)
+    qkv_other = shift(qkv_own, OTHER_SIDE, "qkv_2")
+    qkv_across = shift(qkv_side, OTHER_SIDE, "qkv_3")
+    up_z.append(shift(tied(up_unit, qkv_side), ALONG_Z[2], "up_z"))
+    up_z, qkv_other, qkv_across = joined(up_z, qkv_other, qkv_across)
+    qkv_pieces = twins((qkv_own, qkv_side, qkv_other, qkv_across))
+    up_own = jnp.stack([up_unit] + up_z)
+    up_side = shift(up_own, SIDE, "up_1")
+    down_first = tied(down_unit, up_own)
+    down_z = [shift(down_first, move, "down_z") for move in ALONG_Z[:2]]
+
     distance = jnp.arange(span + shard_len, dtype=jnp.int32) - (shard_len - 1) - x * shard_len
     bucket = jnp.clip(distance, -MAXREL, MAXREL) + MAXREL
     bucket_lanes = 3 * LANES
     buckets = (bucket[:, None] == jnp.arange(bucket_lanes, dtype=jnp.int32)[None, :]).astype(LOW)
-    curve = jnp.dot(buckets[:, :BUCKETS], rel_bias, preferred_element_type=F32).T
-    curve = curve.reshape(H // 2, 2, span + shard_len)
+    curve = lax.dot_general(
+        rel_bias, buckets[:, :BUCKETS], (((0,), (1,)), ((), ())), preferred_element_type=F32
+    )
     spreads = spread_tables(units, width)
-
-    def shape(*dims, kind=LOW):
-        return jax.ShapeDtypeStruct(dims, kind)
-
     unit_sems = pltpu.SemaphoreType.DMA((units,))
-    first, queries, keys, values, weight, vectors, up_bias_all = call(
+    first, queries, keys, values, weight, vectors, up_bias_all, mate_live = call(
         project_kernel,
-        [SMEM, VMEM, VMEM] + [ANY] * 5 + [VMEM] * 3,
+        [SMEM, VMEM, VMEM] + [ANY] * 8 + [VMEM] * 3,
         [
             shape(span, width), shape(shard_len, width), shape(span, width), shape(span, width),
             shape(3 * width, width), shape(8, width, kind=F32), shape(8, ff, kind=F32),
+            shape(PAD, shard_len, kind=F32),
         ],
-        [VMEM] * 7,
+        [VMEM] * 8,
         [
             pltpu.VMEM((units, qkv_rows + PAD, width), LOW), pltpu.VMEM((2, units, width), F32), unit_sems,
         ],
-        (place, frames, mate_frames) + qkv_pieces + tuple(spreads),
+        (tied(place, up_own), frames, mate_frames) + qkv_pieces + tuple(spreads),
         2 * shard_len * width * 5 * width,
         name="project",
     )
+    up_side, keys, down_z = joined(up_side, keys, down_z)
+    up_other = shift(up_own, OTHER_SIDE, "up_2")
+    up_across = shift(up_side, OTHER_SIDE, "up_3")
+    down_z.append(shift(tied(down_unit, keys), ALONG_Z[2], "down_z"))
     pairs = H // 2
     pair_lanes = 2 * HD
 
@@ -1068,78 +1111,110 @@
 
     def heads_of(*dims):
         return pl.BlockSpec(dims, lambda n: (n,) + (0,) * (len(dims) - 1))
+
+    def whole(*dims):
+        return pl.BlockSpec(dims, lambda n: (0,) * len(dims))
 
     probs, mixed = call(
         attend_kernel,
         [
-            SMEM, lanes_of(shard_len), lanes_of(span), lanes_of(span), heads_of(1, 2, span + shard_len),
-            pl.BlockSpec((shard_len, span), lambda n: (0, 0)),
+            SMEM, SMEM, lanes_of(shard_len), lanes_of(span), lanes_of(span), whole(H, span + shard_len),
+            whole(1, shard_len), whole(PAD, shard_len),
         ],
         [shape(H, shard_len, span), shape(shard_len, width, kind=F32)],
         [heads_of(2, shard_len, span), lanes_of(shard_len)],
-        [],
-        (place, queries, keys, values, curve, hidden_pairs),
+        [pltpu.VMEM((shard_len, span), F32)],
+        (
+            tied(place, up_side), seq_lengths, queries, keys, values, curve, row(key_mask), mate_live,
+        ),
         8 * shard_len * span * width,
         grid=(pairs,),
         name="attend",
     )
+    up_other, up_across, mixed, down_z = joined(up_other, up_across, mixed, down_z)
+    up_pieces = twins((up_own, up_side, up_other, up_across))
+    down_own = jnp.stack([down_unit] + down_z)
+    down_side = shift(down_own, SIDE, "down_1")
+    down_other = shift(down_own, OTHER_SIDE, "down_2")
     middle, second, active, slope, context, up, out = call(
         expand_kernel,
-        [SMEM] + [VMEM] * 4 + [ANY] * 5,
+        [SMEM] + [VMEM] * 4 + [ANY] * 8,
         [
             shape(shard_len, width, kind=F32), shape(shard_len, width), shape(shard_len, ff),
             shape(shard_len, ff, kind=F32), shape(shard_len, width), shape(ff, width), shape(width, width),
         ],
         [VMEM] * 7,
         [pltpu.VMEM((units, out_rows, width), LOW), unit_sems, unit_sems],
-        (place, frames, mixed, vectors, up_bias_all) + up_pieces,
+        (tied(place, down_own), frames, mixed, vectors, up_bias_all) + up_pieces,
         2 * shard_len * width * (width + ff),
         name="expand",
     )
+    down_side, down_other, active = joined(down_side, down_other, active)
+    down_across = shift(down_side, OTHER_SIDE, "down_3")
     down_parts = call(
         down_grad_kernel,
         [SMEM, VMEM, VMEM],
         part_shapes(down_rows, width) + [shape(8, width, kind=F32)],
-        [ANY] * 5 + [VMEM],
+        [ANY] * 8 + [VMEM],
         [pltpu.VMEM((units, down_rows, width), LOW), unit_sems],
-        (place, active, cotangent),
+        (tied(place, down_side), active, cotangent),
         2 * shard_len * width * ff,
         name="down_grad",
     )
-    down_bias_grad = down_parts[5]
-    down_sum = scatter_units(down_parts[:5], core)
-    back = call(
-        back_kernel,
-        [SMEM] + [VMEM] * 8 + [ANY] * 5,
-        part_shapes(up_rows + out_rows, width)
-        + [
-            shape(width, ff), shape(shard_len, width, kind=F32), shape(shard_len, width),
-            shape(8, width, kind=F32), shape(8, ff, kind=F32),
+    down_bias_grad = down_parts[8]
+    down_pieces = twins((down_own, down_side, down_other, down_across))
+    corner = added(down_parts[3], down_parts[7]).astype(LOW)
+    turned = shift(corner, OTHER_SIDE, "rs_down_3")
+    other = added(down_parts[2], down_parts[6]).astype(LOW)
+    side = added(down_parts[1], down_parts[5])
+    down, up_bias_grad, hidden_grad = call(
+        hidden_grad_kernel,
+        [SMEM] + [VMEM] * 2 + [ANY] * 8,
+        [shape(width, ff), shape(8, ff, kind=F32), shape(shard_len, ff)],
+        [VMEM] * 3,
+        [pltpu.VMEM((units, down_rows, width), LOW), unit_sems],
+        (tied(place, corner), cotangent, slope) + down_pieces,
+        2 * shard_len * width * ff,
+        name="hidden_grad",
+    )
+    turned, other, hidden_grad = joined(turned, other, hidden_grad)
+    down_two = shift(other, OTHER_SIDE, "rs_down_2")
+    side = (side + turned.astype(F32)).astype(LOW)
+    middle_grad, context_grad, vector_grads, branch_grad = call(
+        middle_grad_kernel,
+        [VMEM] * 6,
+        [
+            shape(shard_len, width, kind=F32), shape(shard_len, width), shape(8, width, kind=F32),
+            shape(shard_len, width),
         ],
-        [ANY] * 5 + [VMEM] * 5,
+        [VMEM] * 4,
+        [],
+        (tied(cotangent, side), hidden_grad, middle, vectors, up, out),
+        2 * shard_len * width * (ff + width),
+        name="middle_grad",
+    )
+    down_two, side, branch_grad = joined(down_two, side, branch_grad)
+    down_one = shift(side, SIDE, "rs_down_1")
+    up_parts = call(
+        up_grad_kernel,
+        [SMEM] + [VMEM] * 4,
+        part_shapes(up_rows + out_rows, width),
+        [ANY] * 8,
         [
-            pltpu.VMEM((units, down_rows, width), LOW), pltpu.VMEM((shard_len, ff), LOW),
             pltpu.VMEM((units, out_rows, width), LOW),
             pltpu.VMEM((units, up_rows + out_rows, width), LOW), unit_sems,
         ],
-        (place, cotangent, slope, second, middle, context, vectors, up, out) + down_pieces,
-        2 * shard_len * width * (3 * ff + 2 * width),
-        name="back",
-    )
-    down, middle_grad, context_grad, vector_grads, up_bias_grad = back[5:]
-    up_sum = scatter_units(back[:5], core)
-    layer_out = call(
-        finish_kernel, [VMEM] * 4, shape(shard_len, width, kind=F32), VMEM, [],
-        (active, down, middle, vectors), 2 * shard_len * width * ff, name="finish",
-    ) if False else pl.pallas_call(
-        finish_kernel,
-        out_shape=shape(shard_len, width, kind=F32),
-        compiler_params=pltpu.CompilerParams(vmem_limit_bytes=VMEM_BYTES),
-        cost_estimate=pl.CostEstimate(
-            flops=2 * shard_len * width * ff, bytes_accessed=8 * shard_len * ff, transcendentals=0
-        ),
-        name="finish",
-    )(active, down, middle, vectors)
+        (place, hidden_grad, second, branch_grad, context),
+        2 * shard_len * width * (ff + width),
+        name="up_grad",
+    )
+    down_one, up_parts = joined(down_one, up_parts)
+    corner = added(up_parts[3], up_parts[7]).astype(LOW)
+    turned = shift(corner, OTHER_SIDE, "rs_up_3")
+    other = added(up_parts[2], up_parts[6]).astype(LOW)
+    side = added(up_parts[1], up_parts[5])
+    down_sum = added(down_parts[0], down_parts[4]) + down_one.astype(F32) + down_two.astype(F32)
+    down_far = shift(down_sum[2:].astype(LOW), ALONG_Z[1], "rs_down_z2")
     query_grad, key_grad, value_grad, diagonals = call(
         attend_back_kernel,
         [
@@ -1148,41 +1223,78 @@
         ],
         [
             shape(shard_len, width), shape(span, width), shape(span, width),
-            shape(pairs, 2, span + shard_len, kind=F32),
+            shape(H, span + shard_len, kind=F32),
         ],
-        [lanes_of(shard_len), lanes_of(span), lanes_of(span), heads_of(1, 2, span + shard_len)],
+        [lanes_of(shard_len), lanes_of(span), lanes_of(span), whole(H, span + shard_len)],
         [],
-        (queries, keys, values, context_grad, mixed, probs),
+        (queries, keys, values, tied(context_grad, corner, down_sum), mixed, probs),
         16 * shard_len * span * width,
         grid=(pairs,),
         name="attend_back",
     )
+    turned, other, query_grad, down_far = joined(turned, other, query_grad, down_far)
+    down_two = down_sum[:2] + down_far.astype(F32)
+    down_near = shift(down_two[1].astype(LOW), ALONG_Z[0], "rs_down_z1")
+    up_two = shift(other, OTHER_SIDE, "rs_up_2")
+    side = (side + turned.astype(F32)).astype(LOW)
+    up_one = shift(side, SIDE, "rs_up_1")
     qkv_parts = call(
         qkv_grad_kernel,
         [SMEM] + [VMEM] * 16,
         part_shapes(qkv_rows + PAD, width) + [shape(shard_len, width, kind=F32), shape(shard_len, width)],
-        [ANY] * 5 + [VMEM] * 2,
+        [ANY] * 8 + [VMEM] * 2,
         [
             pltpu.VMEM((3 * width, width), F32), pltpu.VMEM((2, units, width), F32),
             pltpu.VMEM((units, qkv_rows + PAD, width), LOW), unit_sems,
         ],
         (
-            place, frames, mate_frames, first, query_grad, key_grad, value_grad, weight, vectors,
-            diagonals.reshape(H, span + shard_len), buckets.astype(F32), vector_grads, down_bias_grad,
-            up_bias_grad,
+            tied(place, side, down_two), frames, mate_frames, first, query_grad, key_grad, value_grad, weight,
+            vectors, diagonals, buckets.astype(F32), vector_grads, down_bias_grad, up_bias_grad,
         ) + tuple(spreads),
         2 * shard_len * width * 10 * width,
         name="qkv_grad",
     )
-    own_grad, mate_grad = qkv_parts[5:]
-    mate_part = shift(mate_grad, PACK)
-    qkv_sum = scatter_units(qkv_parts[:5], core)
-    frames_grad = pl.pallas_call(
+    down_near, up_one, up_two, qkv_parts = joined(down_near, up_one, up_two, qkv_parts)
+    own_grad, mate_grad = qkv_parts[8:]
+    corner = added(qkv_parts[3], qkv_parts[7]).astype(LOW)
+    turned = shift(corner, OTHER_SIDE, "rs_qkv_3")
+    up_sum = added(up_parts[0], up_parts[4]) + up_one.astype(F32) + up_two.astype(F32)
+    up_low = up_sum.astype(LOW)
+    up_z = [shift(up_low[n + 1], ALONG_Z[n], "rs_up_z") for n in range(2)]
+    other = added(qkv_parts[2], qkv_parts[6]).astype(LOW)
+    side = added(qkv_parts[1], qkv_parts[5])
+    layer_out = call(
+        finish_kernel,
+        [VMEM] * 4,
+        [shape(shard_len, width, kind=F32)],
+        [VMEM],
+        [],
+        (tied(active, corner, up_low), down, middle, vectors),
+        2 * shard_len * width * ff,
+        name="finish",
+    )[0]
+    down_sum = down_two[0] + down_near.astype(F32)
+    turned, other, up_z, layer_out = joined(turned, other, up_z, layer_out)
+    side = (side + turned.astype(F32)).astype(LOW)
+    qkv_two = shift(other, OTHER_SIDE, "rs_qkv_2")
+    qkv_one = shift(side, SIDE, "rs_qkv_1")
+    up_z.append(shift(tied(up_low[3], side), ALONG_Z[2], "rs_up_z"))
+    qkv_one, qkv_two, up_z = joined(qkv_one, qkv_two, up_z)
+    qkv_sum = added(qkv_parts[0], qkv_parts[4]) + qkv_one.astype(F32) + qkv_two.astype(F32)
+    qkv_z = z_sends(qkv_sum, "rs_qkv")
+    mate_part = shift(tied(mate_grad, qkv_sum), PACK, "grad_pack")
+    up_sum = z_sum(tied(up_sum, qkv_sum), up_z)
+    qkv_sum = z_sum(qkv_sum, qkv_z)
+    frames_grad = call(
         input_grad_kernel,
-        out_shape=shape(shard_len, width, kind=F32),
-        compiler_params=pltpu.CompilerParams(vmem_limit_bytes=VMEM_BYTES),
+        [VMEM] * 5,
+        [shape(shard_len, width, kind=F32)],
+        [VMEM],
+        [],
+        (frames, own_grad, mate_part, middle_grad, vectors),
+        0,
         name="input_grad",
-    )(frames, own_grad, mate_part, middle_grad, vectors)
+    )[0]
 
     down_grad = jnp.concatenate(
         [down_sum[fold * each : (fold + 1) * each] for fold in range(folds)], axis=1

time: 330 us -> 238 us (0.72)
  waiting for transfers between devices: 114 us -> 67.3 us
  local copies, waits for them, and re-layouts: 27.3 us -> 8.16 us
  starting transfers between devices: 73.9 us -> 55 us
  other arithmetic: 22.5 us -> 10.5 us
  Pallas kernels: 88.1 us -> 94.2 us
    ppermute x53 -> x61, waiting for transfers between devices: 114 us -> 67.3 us  [shift(): return lax.ppermute(array, AXES, route(move))]
    ppermute x53 -> x61, starting transfers between devices: 73.9 us -> 55 us  [shift(): return lax.ppermute(array, AXES, route(move))]
    pallas_call x7 -> x12, Pallas kernels: 79.8 us -> 94.2 us  [call(): pl.pallas_call(kernel, out_shape=outs, in_specs=in_specs, out_specs=out_s...]
    pallas_call x2 -> x0, Pallas kernels: 8.38 us -> none  [the longest x1 5.39 us: paired_body(): pl.pallas_call(finish_kernel, out_shape=shape(shard_len, width, kind=F32)...]
    convert_element_type x16 -> x11, other arithmetic: 9.97 us -> 4.62 us  [the longest x1 1.41 us: paired_body(): corner = added(down_parts[3], down_parts[7]).astype(LOW)]
    squeeze x9 -> x2, local copies, waits for them, and re-layouts: 5.11 us -> 0.07 us  [the longest x1 0.04 us: paired_body(): up_z.append(shift(tied(up_low[3], side), ALONG_Z[2], 'rs_up_z'))]
    select_n x16 -> x0, other arithmetic: 4.47 us -> none  [the longest x3 1.98 us: gather_units(): jnp.where(first, jnp.stack([both, near, near_twin, jnp.stack([far, far_tw...]
    pad x8 -> x0, local copies, waits for them, and re-layouts: 3.97 us -> none  [the longest x6 3.96 us: slot(): return jnp.pad(vector, (0, LANES - vector.shape[0]))]
  transfers between devices with their start and end apart: 53 -> 61, of which waited for: 17 -> 19; matrix products, arithmetic and copies ran while one was open for 11% -> 5% of each run, Pallas kernels for 12% -> 35%
where the time goes in v2:
time: 238 us; the launch traced here: 237 us
  Pallas kernels  94.2 us (40%)
  waiting for transfers between devices  67.3 us (28%)
  starting transfers between devices  55 us (23%)
  other arithmetic  10.5 us (4%)
  local copies, waits for them, and re-layouts  8.16 us (3%)
    pallas_call x12, Pallas kernels, call(): pl.pallas_call(kernel, out_shape=outs, in_specs=in_specs, out_specs=out_s...  94.2 us
    ppermute x61, waiting for transfers between devices, shift(): return lax.ppermute(array, AXES, route(move))  67.3 us
    ppermute x61, starting transfers between devices, shift(): return lax.ppermute(array, AXES, route(move))  55 us
  transfers between devices with their start and end apart: 61, of which 19 were waited for; matrix products, arithmetic and copies ran while one was open for 5% of the time, Pallas kernels for 35%

profile of v2, /device:TPU:0, one launch (start us, length us, event | category | flops | bytes accessed | tf_op | source)
XLA Modules:
  0.0 237.4 jit_solution(2016479096745796321)
XLA Ops:
  0.7 1.9 pack.1
  2.6 2.9 %collective-permute-start.3 = (bf16[256,768]{1,0:T(8,128)(2,1)}, bf16[256,768]{1,0:T(8,128)(2,1)S(1)}, u32[]{:S(2)}, u32[]{:S(2)}) collective-permute-start(bf16[256,768]{1,0:T(8,128)(2,1)} %frames.3), channel_id=1, source_target_pairs={{0,1},{1,0},{2,3},{3,2},{4,5},{5,4},{6,7},{7,6},{8,9},{9,8},{10,11... | collective-permute-start | bytes 1179656 | tf_op jit(solution)/shard_map/frames_pack/ppermute | solution.py:493
  5.5 1.6 collective-permute-start
  7.1 2.6 %collective-permute-start.1 = (bf16[80,768]{1,0:T(8,128)(2,1)}, bf16[80,768]{1,0:T(8,128)(2,1)S(1)}, u32[]{:S(2)}, u32[]{:S(2)}) collective-permute-start(bf16[80,768]{1,0:T(8,128)(2,1)} %get-tuple-element.159), channel_id=1, source_target_pairs={{0,16},{1,17},{2,18},{3,19},{4,20},{5,21},{6,22},{7,23},{8,24},{9,... | collective-permute-start | bytes 368648 | tf_op jit(solution)/shard_map/qkv_z/ppermute | solution.py:493
  9.9 2.0 collective-permute-done
  12.0 7.4 %collective-permute-done.1 = bf16[80,768]{1,0:T(8,128)(2,1)S(1)} collective-permute-done((bf16[80,768]{1,0:T(8,128)(2,1)}, bf16[80,768]{1,0:T(8,128)(2,1)S(1)}, u32[]{:S(2)}, u32[]{:S(2)}) %collective-permute-start.1) | collective-permute-done | bytes 122912 | tf_op jit(solution)/shard_map/qkv_z/ppermute | solution.py:493
  20.1 1.0 pad_maximum_fusion.2.p0
  21.7 1.9 collective-permute-start.5
  23.6 1.1 collective-permute-start.6
  24.7 1.5 collective-permute-start.8
  26.3 5.7 %collective-permute-done.5 = bf16[128,768]{1,0:T(8,128)(2,1)S(1)} collective-permute-done((bf16[128,768]{1,0:T(8,128)(2,1)}, bf16[128,768]{1,0:T(8,128)(2,1)S(1)}, u32[]{:S(2)}, u32[]{:S(2)}) %collective-permute-start.5) | collective-permute-done | bytes 196640 | tf_op jit(solution)/shard_map/up_z/ppermute | solution.py:493
  31.9 2.7 %collective-permute-done.6 = bf16[128,768]{1,0:T(8,128)(2,1)S(1)} collective-permute-done((bf16[128,768]{1,0:T(8,128)(2,1)}, bf16[128,768]{1,0:T(8,128)(2,1)S(1)}, u32[]{:S(2)}, u32[]{:S(2)}) %collective-permute-start.6) | collective-permute-done | bytes 196640 | tf_op jit(solution)/shard_map/up_z/ppermute | solution.py:493
  34.7 1.8 collective-permute-start.9
  36.5 2.7 %collective-permute-start.7 = (bf16[128,768]{1,0:T(8,128)(2,1)}, bf16[128,768]{1,0:T(8,128)(2,1)S(1)}, u32[]{:S(2)}, u32[]{:S(2)}) collective-permute-start(bf16[128,768]{1,0:T(8,128)(2,1)} %get-tuple-element.168), channel_id=1, source_target_pairs={{0,24},{1,25},{2,26},{3,27},{4,28},{5,29},{6,30},{7,31},{8,16},{9,... | collective-permute-start | bytes 589832 | tf_op jit(solution)/shard_map/up_z/ppermute | solution.py:493
  39.2 5.1 %collective-permute-done.7 = bf16[128,768]{1,0:T(8,128)(2,1)S(1)} collective-permute-done((bf16[128,768]{1,0:T(8,128)(2,1)}, bf16[128,768]{1,0:T(8,128)(2,1)S(1)}, u32[]{:S(2)}, u32[]{:S(2)}) %collective-permute-start.7) | collective-permute-done | bytes 196640 | tf_op jit(solution)/shard_map/up_z/ppermute | solution.py:493
  44.3 1.0 pad_maximum_fusion.p0
  46.9 1.0 collective-permute-done.12.p4
  47.9 2.2 collective-permute-start.16
  50.1 2.5 %collective-permute-start.17 = (bf16[96,768]{1,0:T(8,128)(2,1)S(1)}, bf16[96,768]{1,0:T(8,128)(2,1)S(1)}, u32[]{:S(2)}, u32[]{:S(2)}) collective-permute-start(bf16[96,768]{1,0:T(8,128)(2,1)S(1)} %copy-done.32), channel_id=1, source_target_pairs={{0,16},{1,17},{2,18},{3,19},{4,20},{5,21},{6,22},{7,23},{8,24},{9,... | collective-permute-start | bytes 442376 | tf_op jit(solution)/shard_map/down_z/ppermute | solution.py:493
  53.3 1.4 collective-permute-start.10
  54.7 8.7 %project.1 = (bf16[512,768]{1,0:T(8,128)(2,1)}, bf16[256,768]{1,0:T(8,128)(2,1)}, bf16[512,768]{1,0:T(8,128)(2,1)}, bf16[512,768]{1,0:T(8,128)(2,1)}, bf16[2304,...) custom-call(s32[4]{0:T(128)} %pad_add_fusion.place, bf16[256,768]{1,0:T(8,128)(2,1)} %frames.3, ...), custom_call_target="tpu_custom_call" | custom-call | flops 1509949440 | bytes 12861456 | tf_op jit(solution)/shard_map/project/pallas_call | solution.py:592
  64.9 1.4 convert_convert_fusion
  66.3 1.2 collective-permute-start.19
  67.5 0.9 fusion.2.curve
  68.6 9.7 %attend.1 = (bf16[12,256,512]{2,1,0:T(8,128)(2,1)}, f32[256,768]{1,0:T(8,128)}) custom-call(s32[4]{0:T(128)} %pad_add_fusion.place, s32[1,4]{1,0:T(1,128)} %lengths.1, bf16[256,768]{1,0:T(8,128)(2,1)} %get-tuple-element.180.queries, bf16[512,768]{1,0:T(8,128)(2,1)} %get-tuple-element.181.keys, bf16[512,768]{1,0:T(8,128)(2,1)} %get-tuple-element.182.values, ...), custom_call_target="tpu_custom_call" | custom-call | flops 805306368 | bytes 5944352 | tf_op jit(solution)/shard_map/attend/pallas_call | solution.py:592
  79.0 1.6 collective-permute-start.20
  80.6 0.9 collective-permute-start.21
  83.0 14.6 %expand.1 = (f32[256,768]{1,0:T(8,128)}, bf16[256,768]{1,0:T(8,128)(2,1)}, bf16[256,3072]{1,0:T(8,128)(2,1)}, f32[256,3072]{1,0:T(8,128)}, bf16[256,768]{1,0:T(8...) custom-call(s32[4]{0:T(128)} %pad_add_fusion.place, bf16[256,768]{1,0:T(8,128)(2,1)} %frames.3, ...), custom_call_target="tpu_custom_call" | custom-call | flops 1509949440 | bytes 19783696 | tf_op jit(solution)/shard_map/expand/pallas_call | solution.py:592
  97.6 6.3 %down_grad.1 = (bf16[4,96,768]{2,1,0:T(8,128)(2,1)}, bf16[4,96,768]{2,1,0:T(8,128)(2,1)}, bf16[4,96,768]{2,1,0:T(8,128)(2,1)}, bf16[4,96,768]{2,1,0:T(8,128)(2,1...) custom-call(s32[4]{0:T(128)} %pad_add_fusion.place, ...), custom_call_target="tpu_custom_call" | custom-call | flops 1207959552 | bytes 6709264 | tf_op jit(solution)/shard_map/down_grad/pallas_call | solution.py:592
  104.3 0.9 collective-permute-start.30
  106.6 7.7 %collective-permute-done.30.p3 = bf16[4,96,768]{2,1,0:T(8,128)(2,1)S(1)} collective-permute-done((bf16[4,96,768]{2,1,0:T(8,128)(2,1)S(1)}, bf16[4,96,768]{2,1,0:T(8,128)(2,1)S(1)}, u32[]{:S(2)}, u32[]{:S(2)}) %collective-permute-start.30) | collective-permute-done | bytes 589856 | tf_op jit(solution)/shard_map/down_3/ppermute | solution.py:493
  114.2 1.4 add_convert_fusion.5
  115.7 1.0 collective-permute-start.28
  118.6 8.7 %hidden_grad.1 = (bf16[768,3072]{1,0:T(8,128)(2,1)}, f32[8,3072]{1,0:T(8,128)}, bf16[256,3072]{1,0:T(8,128)(2,1)}) custom-call(s32[4]{0:T(128)} %pad_add_fusion.place, bf16[256,768]{1,0:T(8,128)(2,1)} %cotangent.4, f32[256,3072]{1,0:T(8,128)} %get-tuple-element.208.slope, bf16[4,96,768]{2,1,0:T(8,128)(2,1)} %copy-done.3, bf16[4,96,768]{2,1,0:T(8,128)(2,1)} %copy-done.14, ...), custom_call_target="tpu_custom_call" | custom-call | flops 1207959552 | bytes 14647312 | tf_op jit(solution)/shard_map/hidden_grad/pallas_call | solution.py:592
  127.3 1.0 collective-permute-start.35
  128.6 6.8 %middle_grad.1 = (f32[256,768]{1,0:T(8,128)}, bf16[256,768]{1,0:T(8,128)(2,1)}, f32[8,768]{1,0:T(8,128)}, bf16[256,768]{1,0:T(8,128)(2,1)}) custom-call(bf16[256,768]{1,0:T(8,128)(2,1)} %cotangent.4, bf16[256,3072]{1,0:T(8,128)(2,1)} %get-tuple-element.216.hidden_grad, f32[256,768]{1,0:T(8,128)} %get-tuple-element.217.middle, ...), custom_call_target="tpu_custom_call" | custom-call | flops 1509949440 | bytes 10272768 | tf_op jit(solution)/shard_map/middle_grad/pallas_call | solution.py:592
  135.4 1.9 collective-permute-done.35
  137.3 1.0 collective-permute-start.37
  138.2 6.6 %up_grad.1 = (bf16[4,128,768]{2,1,0:T(8,128)(2,1)}, bf16[4,128,768]{2,1,0:T(8,128)(2,1)}, bf16[4,128,768]{2,1,0:T(8,128)(2,1)}, bf16[4,128,768]{2,1,0:T(8,128)(2...) custom-call(s32[4]{0:T(128)} %pad_add_fusion.place, ...), custom_call_target="tpu_custom_call" | custom-call | flops 1509949440 | bytes 9043984 | tf_op jit(solution)/shard_map/up_grad/pallas_call | solution.py:592
  144.9 2.3 collective-permute-done.37
  147.7 2.8 %collective-permute-done.38 = bf16[4,128,768]{2,1,0:T(8,128)(2,1)S(1)} collective-permute-done((bf16[4,128,768]{2,1,0:T(8,128)(2,1)}, bf16[4,128,768]{2,1,0:T(8,128)(2,1)S(1)}, u32[]{:S(2)}, u32[]{:S(2)}) %collective-permute-start.38) | collective-permute-done | bytes 786464 | tf_op jit(solution)/shard_map/twin/ppermute | solution.py:493
  150.5 1.3 add_convert_fusion.2
  151.8 1.0 collective-permute-start.39
  153.2 1.4 collective-permute-start.41
  154.6 9.8 %attend_back.1 = (bf16[256,768]{1,0:T(8,128)(2,1)}, bf16[512,768]{1,0:T(8,128)(2,1)}, bf16[512,768]{1,0:T(8,128)(2,1)}, f32[12,768]{1,0:T(8,128)}) custom-call(bf16[256,768]{1,0:T(8,128)(2,1)} %get-tuple-element.180.queries, bf16[512,768]{1,0:T(8,128)(2,1)} %get-tuple-element.181.keys, bf16[512,768]{1,0:T(8,128)(2,1)} %get-tuple-element.182.values, ...), custom_call_target="tpu_custom_call" | custom-call | flops 1610612736 | bytes 8294400 | tf_op jit(solution)/shard_map/attend_back/pallas_call | solution.py:592
  164.6 5.3 %collective-permute-done.41 = bf16[2,96,768]{2,1,0:T(8,128)(2,1)S(1)} collective-permute-done((bf16[2,96,768]{2,1,0:T(8,128)(2,1)S(1)}, bf16[2,96,768]{2,1,0:T(8,128)(2,1)S(1)}, u32[]{:S(2)}, u32[]{:S(2)}) %collective-permute-start.41) | collective-permute-done | bytes 294944 | tf_op jit(solution)/shard_map/rs_down_z2/ppermute | solution.py:493
  170.2 1.1 collective-permute-start.44
  171.3 1.0 collective-permute-start.45
  172.5 12.5 %qkv_grad.1 = (bf16[4,80,768]{2,1,0:T(8,128)(2,1)}, bf16[4,80,768]{2,1,0:T(8,128)(2,1)}, bf16[4,80,768]{2,1,0:T(8,128)(2,1)}, bf16[4,80,768]{2,1,0:T(8,128)(2,1)...) custom-call(s32[4]{0:T(128)} %pad_add_fusion.place, ...), custom_call_target="tpu_custom_call" | custom-call | flops 3019898880 | bytes 15298576 | tf_op jit(solution)/shard_map/qkv_grad/pallas_call | solution.py:592
  185.0 5.5 %collective-permute-done.44 = bf16[4,128,768]{2,1,0:T(8,128)(2,1)S(1)} collective-permute-done((bf16[4,128,768]{2,1,0:T(8,128)(2,1)S(1)}, bf16[4,128,768]{2,1,0:T(8,128)(2,1)S(1)}, u32[]{:S(2)}, u32[]{:S(2)}) %collective-permute-start.44) | collective-permute-done | bytes 786464 | tf_op jit(solution)/shard_map/rs_up_1/ppermute | solution.py:493
  191.6 2.4 collective-permute-start.51
  194.1 1.0 collective-permute-start.47
  195.2 5.4 %finish.1 = f32[256,768]{1,0:T(8,128)} custom-call(bf16[256,3072]{1,0:T(8,128)(2,1)} %get-tuple-element.276.active, bf16[768,3072]{1,0:T(8,128)(2,1)} %get-tuple-element.277.down, f32[256,768]{1,0:T(8,128)} %get-tuple-element.217.middle, f32[8,768]{1,0:T(8,128)} %get-tuple-element.193.vectors), custom_call_target="tpu_custom_call" | custom-call | flops 1207959552 | bytes 7888896 | tf_op jit(solution)/shard_map/finish/pallas_call | solution.py:592
  201.8 1.9 collective-permute-done.51
  204.6 1.4 collective-permute-start.55
  206.0 1.9 collective-permute-start.56
  208.6 5.0 %collective-permute-done.56 = bf16[128,768]{1,0:T(8,128)(2,1)S(1)} collective-permute-done((bf16[128,768]{1,0:T(8,128)(2,1)S(1)}, bf16[128,768]{1,0:T(8,128)(2,1)S(1)}, u32[]{:S(2)}, u32[]{:S(2)}) %collective-permute-start.56) | collective-permute-done | bytes 196640 | tf_op jit(solution)/shard_map/rs_up_z/ppermute | solution.py:493
  213.6 3.1 %collective-permute-done.54 = bf16[4,80,768]{2,1,0:T(8,128)(2,1)S(1)} collective-permute-done((bf16[4,80,768]{2,1,0:T(8,128)(2,1)S(1)}, bf16[4,80,768]{2,1,0:T(8,128)(2,1)S(1)}, u32[]{:S(2)}, u32[]{:S(2)}) %collective-permute-start.54) | collective-permute-done | bytes 491552 | tf_op jit(solution)/shard_map/rs_qkv_1/ppermute | solution.py:493
  217.0 1.2 collective-permute-start.57
  218.2 2.1 collective-permute-start.60
  220.2 2.4 %collective-permute-start.58 = (bf16[80,768]{1,0:T(8,128)(2,1)S(1)}, bf16[80,768]{1,0:T(8,128)(2,1)S(1)}, u32[]{:S(2)}, u32[]{:S(2)}) collective-permute-start(bf16[80,768]{1,0:T(8,128)(2,1)S(1)} %get-tuple-element.306), channel_id=1, source_target_pairs={{0,8},{1,9},{2,10},{3,11},{4,12},{5,13},{6,14},{7,15},{8,0},{9,1},... | collective-permute-start | bytes 368648 | tf_op jit(solution)/shard_map/rs_qkv_z/ppermute | solution.py:493
  224.1 2.2 collective-permute-done.60
  226.3 4.4 %collective-permute-done.59 = bf16[80,768]{1,0:T(8,128)(2,1)S(1)} collective-permute-done((bf16[80,768]{1,0:T(8,128)(2,1)S(1)}, bf16[80,768]{1,0:T(8,128)(2,1)S(1)}, u32[]{:S(2)}, u32[]{:S(2)}) %collective-permute-start.59) | collective-permute-done | bytes 122912 | tf_op jit(solution)/shard_map/rs_qkv_z/ppermute | solution.py:493
  234.4 3.0 %input_grad.1 = f32[256,768]{1,0:T(8,128)} custom-call(bf16[256,768]{1,0:T(8,128)(2,1)} %frames.3, f32[256,768]{1,0:T(8,128)} %get-tuple-element.279.own_grad, bf16[256,768]{1,0:T(8,128)(2,1)} %copy-done.31, f32[256,768]{1,0:T(8,128)} %get-tuple-element.293.middle_grad, f32[8,768]{1,0:T(8,128)} %get-tuple-element.193.vectors), custom_call_target="tpu_custom_call" | custom-call | bytes 3170304 | tf_op jit(solution)/shard_map/input_grad/pallas_call | solution.py:592
  (191 shorter events, 22.3 us)
Async XLA Ops:
  0.7 66.8 %copy-start = (bf16[321,12]{0,1:T(8,128)(2,1)S(1)}, bf16[321,12]{0,1:T(8,128)(2,1)}, u32[]{:S(2)}) copy-start(bf16[321,12]{0,1:T(8,128)(2,1)} %param.36) | copy-start | bytes 23116
  2.6 45.3 %copy-start.32 = (bf16[96,768]{1,0:T(8,128)(2,1)S(1)}, bf16[96,768]{1,0:T(8,128)(2,1)}, u32[]{:S(2)}) copy-start(bf16[96,768]{1,0:T(8,128)(2,1)} %get-tuple-element.187) | copy-start | bytes 442372
  2.6 16.8 %collective-permute-start.3 = (bf16[256,768]{1,0:T(8,128)(2,1)}, bf16[256,768]{1,0:T(8,128)(2,1)S(1)}, u32[]{:S(2)}, u32[]{:S(2)}) collective-permute-start(bf16[256,768]{1,0:T(8,128)(2,1)} %frames.3), channel_id=1, source_target_pairs={{0,1},{1,0},{2,3},{3,2},{4,5},{5,4},{6,7},{7,6},{8,9},{9,8},{10,11... | collective-permute-start | bytes 1179656 | tf_op jit(solution)/shard_map/frames_pack/ppermute | solution.py:493
  5.5 6.4 %collective-permute-start = (bf16[80,768]{1,0:T(8,128)(2,1)}, bf16[80,768]{1,0:T(8,128)(2,1)S(1)}, u32[]{:S(2)}, u32[]{:S(2)}) collective-permute-start(bf16[80,768]{1,0:T(8,128)(2,1)} %get-tuple-element.159), channel_id=1, source_target_pairs={{0,8},{1,9},{2,10},{3,11},{4,12},{5,13},{6,14},{7,15},{8,0},{9,1},... | collective-permute-start | bytes 368648 | tf_op jit(solution)/shard_map/qkv_z/ppermute | solution.py:493
  7.1 12.3 %collective-permute-start.1 = (bf16[80,768]{1,0:T(8,128)(2,1)}, bf16[80,768]{1,0:T(8,128)(2,1)S(1)}, u32[]{:S(2)}, u32[]{:S(2)}) collective-permute-start(bf16[80,768]{1,0:T(8,128)(2,1)} %get-tuple-element.159), channel_id=1, source_target_pairs={{0,16},{1,17},{2,18},{3,19},{4,20},{5,21},{6,22},{7,23},{8,24},{9,... | collective-permute-start | bytes 368648 | tf_op jit(solution)/shard_map/qkv_z/ppermute | solution.py:493
  9.7 9.7 %collective-permute-start.2 = (bf16[80,768]{1,0:T(8,128)(2,1)}, bf16[80,768]{1,0:T(8,128)(2,1)S(1)}, u32[]{:S(2)}, u32[]{:S(2)}) collective-permute-start(bf16[80,768]{1,0:T(8,128)(2,1)} %get-tuple-element.159), channel_id=1, source_target_pairs={{0,24},{1,25},{2,26},{3,27},{4,28},{5,29},{6,30},{7,31},{8,16},{9,... | collective-permute-start | bytes 368648 | tf_op jit(solution)/shard_map/qkv_z/ppermute | solution.py:493
  21.1 33.6 %copy-start.4 = (bf16[4,80,768]{2,1,0:T(8,128)(2,1)}, bf16[4,80,768]{2,1,0:T(8,128)(2,1)S(1)}, u32[]{:S(2)}) copy-start(bf16[4,80,768]{2,1,0:T(8,128)(2,1)S(1)} %pad_maximum_fusion.2.p0) | copy-start | bytes 1474564
  21.1 13.6 %collective-permute-start.4 = (bf16[4,80,768]{2,1,0:T(8,128)(2,1)S(1)}, bf16[4,80,768]{2,1,0:T(8,128)(2,1)S(1)}, u32[]{:S(2)}, u32[]{:S(2)}) collective-permute-start(bf16[4,80,768]{2,1,0:T(8,128)(2,1)S(1)} %pad_maximum_fusion.2.p0), channel_id=1, source_target_pairs={{0,1},{1,0},{2,6},{3,7},{4,5},{5,4},{6,2},{7,3},{8,9},{9,8},{10,14... | collective-permute-start | bytes 1474568 | tf_op jit(solution)/shard_map/qkv_1/ppermute | solution.py:493
  21.7 10.2 %collective-permute-start.5 = (bf16[128,768]{1,0:T(8,128)(2,1)}, bf16[128,768]{1,0:T(8,128)(2,1)S(1)}, u32[]{:S(2)}, u32[]{:S(2)}) collective-permute-start(bf16[128,768]{1,0:T(8,128)(2,1)} %get-tuple-element.168), channel_id=1, source_target_pairs={{0,8},{1,9},{2,10},{3,11},{4,12},{5,13},{6,14},{7,15},{8,0},{9,1},... | collective-permute-start | bytes 589832 | tf_op jit(solution)/shard_map/up_z/ppermute | solution.py:493
  23.6 11.1 %collective-permute-start.6 = (bf16[128,768]{1,0:T(8,128)(2,1)}, bf16[128,768]{1,0:T(8,128)(2,1)S(1)}, u32[]{:S(2)}, u32[]{:S(2)}) collective-permute-start(bf16[128,768]{1,0:T(8,128)(2,1)} %get-tuple-element.168), channel_id=1, source_target_pairs={{0,16},{1,17},{2,18},{3,19},{4,20},{5,21},{6,22},{7,23},{8,24},{9,... | collective-permute-start | bytes 589832 | tf_op jit(solution)/shard_map/up_z/ppermute | solution.py:493
  24.7 14.5 %collective-permute-start.8 = (bf16[4,80,768]{2,1,0:T(8,128)(2,1)S(1)}, bf16[4,80,768]{2,1,0:T(8,128)(2,1)S(1)}, u32[]{:S(2)}, u32[]{:S(2)}) collective-permute-start(bf16[4,80,768]{2,1,0:T(8,128)(2,1)S(1)} %pad_maximum_fusion.2.p0), channel_id=1, source_target_pairs={{0,4},{1,5},{2,3},{3,2},{4,0},{5,1},{6,7},{7,6},{8,12},{9,13},{10,... | collective-permute-start | bytes 1474568 | tf_op jit(solution)/shard_map/qkv_2/ppermute | solution.py:493
  34.7 9.6 %collective-permute-start.9 = (bf16[4,80,768]{2,1,0:T(8,128)(2,1)S(1)}, bf16[4,80,768]{2,1,0:T(8,128)(2,1)}, u32[]{:S(2)}, u32[]{:S(2)}) collective-permute-start(bf16[4,80,768]{2,1,0:T(8,128)(2,1)S(1)} %collective-permute-done.4.p1), channel_id=1, source_target_pairs={{0,4},{1,5},{2,3},{3,2},{4,0},{5,1},{6,7},{7,6},{8,12},{9,13},{10,... | collective-permute-start | bytes 1474568 | tf_op jit(solution)/shard_map/qkv_3/ppermute | solution.py:493
  36.5 7.8 %collective-permute-start.7 = (bf16[128,768]{1,0:T(8,128)(2,1)}, bf16[128,768]{1,0:T(8,128)(2,1)S(1)}, u32[]{:S(2)}, u32[]{:S(2)}) collective-permute-start(bf16[128,768]{1,0:T(8,128)(2,1)} %get-tuple-element.168), channel_id=1, source_target_pairs={{0,24},{1,25},{2,26},{3,27},{4,28},{5,29},{6,30},{7,31},{8,16},{9,... | collective-permute-start | bytes 589832 | tf_op jit(solution)/shard_map/up_z/ppermute | solution.py:493
  45.3 18.2 %collective-permute-start.11 = (bf16[4,128,768]{2,1,0:T(8,128)(2,1)S(1)}, bf16[4,128,768]{2,1,0:T(8,128)(2,1)S(1)}, u32[]{:S(2)}, u32[]{:S(2)}) collective-permute-start(bf16[4,128,768]{2,1,0:T(8,128)(2,1)S(1)} %pad_maximum_fusion.p0), channel_id=1, source_target_pairs={{0,1},{1,0},{2,6},{3,7},{4,5},{5,4},{6,2},{7,3},{8,9},{9,8},{10,14... | collective-permute-start | bytes 2359304 | tf_op jit(solution)/shard_map/up_1/ppermute | solution.py:493
  45.9 2.0 collective-permute-start.12
  45.9 4.2 %collective-permute-start.13 = (bf16[4,80,768]{2,1,0:T(8,128)(2,1)S(1)}, bf16[4,80,768]{2,1,0:T(8,128)(2,1)}, u32[]{:S(2)}, u32[]{:S(2)}) collective-permute-start(bf16[4,80,768]{2,1,0:T(8,128)(2,1)S(1)} %collective-permute-done.4.p1), channel_id=1, source_target_pairs={{0,2},{1,3},{2,0},{3,1},{4,6},{5,7},{6,4},{7,5},{8,10},{9,11},{10,... | collective-permute-start | bytes 1474568 | tf_op jit(solution)/shard_map/twin/ppermute | solution.py:493
  46.4 6.8 %collective-permute-start.14 = (bf16[4,80,768]{2,1,0:T(8,128)(2,1)S(1)}, bf16[4,80,768]{2,1,0:T(8,128)(2,1)}, u32[]{:S(2)}, u32[]{:S(2)}) collective-permute-start(bf16[4,80,768]{2,1,0:T(8,128)(2,1)S(1)} %collective-permute-done.8.p2), channel_id=1, source_target_pairs={{0,2},{1,3},{2,0},{3,1},{4,6},{5,7},{6,4},{7,5},{8,10},{9,11},{10,... | collective-permute-start | bytes 1474568 | tf_op jit(solution)/shard_map/twin/ppermute | solution.py:493
  46.4 8.2 %collective-permute-start.15 = (bf16[4,80,768]{2,1,0:T(8,128)(2,1)}, bf16[4,80,768]{2,1,0:T(8,128)(2,1)}, u32[]{:S(2)}, u32[]{:S(2)}) collective-permute-start(bf16[4,80,768]{2,1,0:T(8,128)(2,1)} %collective-permute-done.9.p3), channel_id=1, source_target_pairs={{0,2},{1,3},{2,0},{3,1},{4,6},{5,7},{6,4},{7,5},{8,10},{9,11},{10,... | collective-permute-start | bytes 1474568 | tf_op jit(solution)/shard_map/twin/ppermute | solution.py:493
  47.9 15.5 %collective-permute-start.16 = (bf16[96,768]{1,0:T(8,128)(2,1)S(1)}, bf16[96,768]{1,0:T(8,128)(2,1)S(1)}, u32[]{:S(2)}, u32[]{:S(2)}) collective-permute-start(bf16[96,768]{1,0:T(8,128)(2,1)S(1)} %copy-done.32), channel_id=1, source_target_pairs={{0,8},{1,9},{2,10},{3,11},{4,12},{5,13},{6,14},{7,15},{8,0},{9,1},... | collective-permute-start | bytes 442376 | tf_op jit(solution)/shard_map/down_z/ppermute | solution.py:493
  50.1 13.3 %collective-permute-start.17 = (bf16[96,768]{1,0:T(8,128)(2,1)S(1)}, bf16[96,768]{1,0:T(8,128)(2,1)S(1)}, u32[]{:S(2)}, u32[]{:S(2)}) collective-permute-start(bf16[96,768]{1,0:T(8,128)(2,1)S(1)} %copy-done.32), channel_id=1, source_target_pairs={{0,16},{1,17},{2,18},{3,19},{4,20},{5,21},{6,22},{7,23},{8,24},{9,... | collective-permute-start | bytes 442376 | tf_op jit(solution)/shard_map/down_z/ppermute | solution.py:493
  53.3 25.0 %collective-permute-start.10 = (bf16[4,128,768]{2,1,0:T(8,128)(2,1)S(1)}, bf16[4,128,768]{2,1,0:T(8,128)(2,1)S(1)}, u32[]{:S(2)}, u32[]{:S(2)}) collective-permute-start(bf16[4,128,768]{2,1,0:T(8,128)(2,1)S(1)} %pad_maximum_fusion.p0), channel_id=1, source_target_pairs={{0,4},{1,5},{2,3},{3,2},{4,0},{5,1},{6,7},{7,6},{8,12},{9,13},{10,... | collective-permute-start | bytes 2359304 | tf_op jit(solution)/shard_map/up_2/ppermute | solution.py:493
  64.2 14.2 %collective-permute-start.18 = (bf16[4,128,768]{2,1,0:T(8,128)(2,1)S(1)}, bf16[4,128,768]{2,1,0:T(8,128)(2,1)}, u32[]{:S(2)}, u32[]{:S(2)}) collective-permute-start(bf16[4,128,768]{2,1,0:T(8,128)(2,1)S(1)} %collective-permute-done.11.p1), channel_id=1, source_target_pairs={{0,4},{1,5},{2,3},{3,2},{4,0},{5,1},{6,7},{7,6},{8,12},{9,13},{10,... | collective-permute-start | bytes 2359304 | tf_op jit(solution)/shard_map/up_3/ppermute | solution.py:493
  64.8 15.8 %collective-permute-start.22 = (bf16[4,128,768]{2,1,0:T(8,128)(2,1)S(1)}, bf16[4,128,768]{2,1,0:T(8,128)(2,1)S(1)}, u32[]{:S(2)}, u32[]{:S(2)}) collective-permute-start(bf16[4,128,768]{2,1,0:T(8,128)(2,1)S(1)} %pad_maximum_fusion.p0), channel_id=1, source_target_pairs={{0,2},{1,3},{2,0},{3,1},{4,6},{5,7},{6,4},{7,5},{8,10},{9,11},{10,... | collective-permute-start | bytes 2359304 | tf_op jit(solution)/shard_map/twin/ppermute | solution.py:493
  66.3 12.1 %collective-permute-start.19 = (bf16[96,768]{1,0:T(8,128)(2,1)S(1)}, bf16[96,768]{1,0:T(8,128)(2,1)S(1)}, u32[]{:S(2)}, u32[]{:S(2)}) collective-permute-start(bf16[96,768]{1,0:T(8,128)(2,1)S(1)} %copy-done.32), channel_id=1, source_target_pairs={{0,24},{1,25},{2,26},{3,27},{4,28},{5,29},{6,30},{7,31},{8,16},{9,... | collective-permute-start | bytes 442376 | tf_op jit(solution)/shard_map/down_z/ppermute | solution.py:493
  68.4 13.1 %collective-permute-start.23 = (bf16[4,128,768]{2,1,0:T(8,128)(2,1)S(1)}, bf16[4,128,768]{2,1,0:T(8,128)(2,1)S(1)}, u32[]{:S(2)}, u32[]{:S(2)}) collective-permute-start(bf16[4,128,768]{2,1,0:T(8,128)(2,1)S(1)} %collective-permute-done.11.p1), channel_id=1, source_target_pairs={{0,2},{1,3},{2,0},{3,1},{4,6},{5,7},{6,4},{7,5},{8,10},{9,11},{10,... | collective-permute-start | bytes 2359304 | tf_op jit(solution)/shard_map/twin/ppermute | solution.py:493
  78.4 3.2 %collective-permute-start.24 = (bf16[4,128,768]{2,1,0:T(8,128)(2,1)S(1)}, bf16[4,128,768]{2,1,0:T(8,128)(2,1)S(1)}, u32[]{:S(2)}, u32[]{:S(2)}) collective-permute-start(bf16[4,128,768]{2,1,0:T(8,128)(2,1)S(1)} %collective-permute-done.10.p2), channel_id=1, source_target_pairs={{0,2},{1,3},{2,0},{3,1},{4,6},{5,7},{6,4},{7,5},{8,10},{9,11},{10,... | collective-permute-start | bytes 2359304 | tf_op jit(solution)/shard_map/twin/ppermute | solution.py:493
  78.7 3.3 %collective-permute-start.25 = (bf16[4,128,768]{2,1,0:T(8,128)(2,1)}, bf16[4,128,768]{2,1,0:T(8,128)(2,1)S(1)}, u32[]{:S(2)}, u32[]{:S(2)}) collective-permute-start(bf16[4,128,768]{2,1,0:T(8,128)(2,1)} %collective-permute-done.18.p3), channel_id=1, source_target_pairs={{0,2},{1,3},{2,0},{3,1},{4,6},{5,7},{6,4},{7,5},{8,10},{9,11},{10,... | collective-permute-start | bytes 2359304 | tf_op jit(solution)/shard_map/twin/ppermute | solution.py:493
  79.0 18.6 %collective-permute-start.20 = (bf16[4,96,768]{2,1,0:T(8,128)(2,1)S(1)}, bf16[4,96,768]{2,1,0:T(8,128)(2,1)S(1)}, u32[]{:S(2)}, u32[]{:S(2)}) collective-permute-start(bf16[4,96,768]{2,1,0:T(8,128)(2,1)S(1)} %pad_maximum_fusion.1.p0), channel_id=1, source_target_pairs={{0,1},{1,0},{2,6},{3,7},{4,5},{5,4},{6,2},{7,3},{8,9},{9,8},{10,14... | collective-permute-start | bytes 1769480 | tf_op jit(solution)/shard_map/down_1/ppermute | solution.py:493
  80.6 17.0 %collective-permute-start.21 = (bf16[4,96,768]{2,1,0:T(8,128)(2,1)S(1)}, bf16[4,96,768]{2,1,0:T(8,128)(2,1)S(1)}, u32[]{:S(2)}, u32[]{:S(2)}) collective-permute-start(bf16[4,96,768]{2,1,0:T(8,128)(2,1)S(1)} %pad_maximum_fusion.1.p0), channel_id=1, source_target_pairs={{0,4},{1,5},{2,3},{3,2},{4,0},{5,1},{6,7},{7,6},{8,12},{9,13},{10,... | collective-permute-start | bytes 1769480 | tf_op jit(solution)/shard_map/down_2/ppermute | solution.py:493
  104.0 2.3 collective-permute-start.27
  104.3 9.9 %collective-permute-start.30 = (bf16[4,96,768]{2,1,0:T(8,128)(2,1)S(1)}, bf16[4,96,768]{2,1,0:T(8,128)(2,1)S(1)}, u32[]{:S(2)}, u32[]{:S(2)}) collective-permute-start(bf16[4,96,768]{2,1,0:T(8,128)(2,1)S(1)} %collective-permute-done.20.p1), channel_id=1, source_target_pairs={{0,4},{1,5},{2,3},{3,2},{4,0},{5,1},{6,7},{7,6},{8,12},{9,13},{10,... | collective-permute-start | bytes 1769480 | tf_op jit(solution)/shard_map/down_3/ppermute | solution.py:493
  105.3 10.4 %collective-permute-start.31 = (bf16[4,96,768]{2,1,0:T(8,128)(2,1)S(1)}, bf16[4,96,768]{2,1,0:T(8,128)(2,1)S(1)}, u32[]{:S(2)}, u32[]{:S(2)}) collective-permute-start(bf16[4,96,768]{2,1,0:T(8,128)(2,1)S(1)} %pad_maximum_fusion.1.p0), channel_id=1, source_target_pairs={{0,2},{1,3},{2,0},{3,1},{4,6},{5,7},{6,4},{7,5},{8,10},{9,11},{10,... | collective-permute-start | bytes 1769480 | tf_op jit(solution)/shard_map/twin/ppermute | solution.py:493
  105.8 10.9 %collective-permute-start.29 = (bf16[4,96,768]{2,1,0:T(8,128)(2,1)}, bf16[4,96,768]{2,1,0:T(8,128)(2,1)S(1)}, u32[]{:S(2)}, u32[]{:S(2)}) collective-permute-start(bf16[4,96,768]{2,1,0:T(8,128)(2,1)} %get-tuple-element.206), channel_id=1, source_target_pairs={{0,2},{1,3},{2,0},{3,1},{4,6},{5,7},{6,4},{7,5},{8,10},{9,11},{10,... | collective-permute-start | bytes 1769480 | tf_op jit(solution)/shard_map/twin/ppermute | solution.py:493
  105.8 11.6 %collective-permute-start.32 = (bf16[4,96,768]{2,1,0:T(8,128)(2,1)S(1)}, bf16[4,96,768]{2,1,0:T(8,128)(2,1)S(1)}, u32[]{:S(2)}, u32[]{:S(2)}) collective-permute-start(bf16[4,96,768]{2,1,0:T(8,128)(2,1)S(1)} %collective-permute-done.20.p1), channel_id=1, source_target_pairs={{0,2},{1,3},{2,0},{3,1},{4,6},{5,7},{6,4},{7,5},{8,10},{9,11},{10,... | collective-permute-start | bytes 1769480 | tf_op jit(solution)/shard_map/twin/ppermute | solution.py:493
  106.3 11.1 %collective-permute-start.33 = (bf16[4,96,768]{2,1,0:T(8,128)(2,1)S(1)}, bf16[4,96,768]{2,1,0:T(8,128)(2,1)S(1)}, u32[]{:S(2)}, u32[]{:S(2)}) collective-permute-start(bf16[4,96,768]{2,1,0:T(8,128)(2,1)S(1)} %collective-permute-done.21.p2), channel_id=1, source_target_pairs={{0,2},{1,3},{2,0},{3,1},{4,6},{5,7},{6,4},{7,5},{8,10},{9,11},{10,... | collective-permute-start | bytes 1769480 | tf_op jit(solution)/shard_map/twin/ppermute | solution.py:493
  114.2 3.2 %collective-permute-start.34 = (bf16[4,96,768]{2,1,0:T(8,128)(2,1)S(1)}, bf16[4,96,768]{2,1,0:T(8,128)(2,1)S(1)}, u32[]{:S(2)}, u32[]{:S(2)}) collective-permute-start(bf16[4,96,768]{2,1,0:T(8,128)(2,1)S(1)} %collective-permute-done.30.p3), channel_id=1, source_target_pairs={{0,2},{1,3},{2,0},{3,1},{4,6},{5,7},{6,4},{7,5},{8,10},{9,11},{10,... | collective-permute-start | bytes 1769480 | tf_op jit(solution)/shard_map/twin/ppermute | solution.py:493
  115.7 11.7 %collective-permute-start.28 = (bf16[4,96,768]{2,1,0:T(8,128)(2,1)S(1)}, bf16[4,96,768]{2,1,0:T(8,128)(2,1)S(1)}, u32[]{:S(2)}, u32[]{:S(2)}) collective-permute-start(bf16[4,96,768]{2,1,0:T(8,128)(2,1)S(1)} %add_convert_fusion.5), channel_id=1, source_target_pairs={{0,4},{1,5},{2,3},{3,2},{4,0},{5,1},{6,7},{7,6},{8,12},{9,13},{10,... | collective-permute-start | bytes 1769480 | tf_op jit(solution)/shard_map/rs_down_3/ppermute | solution.py:493
  116.7 11.7 %collective-permute-start.36 = (bf16[4,96,768]{2,1,0:T(8,128)(2,1)S(1)}, bf16[4,96,768]{2,1,0:T(8,128)(2,1)S(1)}, u32[]{:S(2)}, u32[]{:S(2)}) collective-permute-start(bf16[4,96,768]{2,1,0:T(8,128)(2,1)S(1)} %copy-done.39), channel_id=1, source_target_pairs={{0,2},{1,3},{2,0},{3,1},{4,6},{5,7},{6,4},{7,5},{8,10},{9,11},{10,... | collective-permute-start | bytes 1769480 | tf_op jit(solution)/shard_map/twin/ppermute | solution.py:493
  127.3 9.9 %collective-permute-start.35 = (bf16[4,96,768]{2,1,0:T(8,128)(2,1)S(1)}, bf16[4,96,768]{2,1,0:T(8,128)(2,1)S(1)}, u32[]{:S(2)}, u32[]{:S(2)}) collective-permute-start(bf16[4,96,768]{2,1,0:T(8,128)(2,1)S(1)} %add_convert_fusion.4), channel_id=1, source_target_pairs={{0,4},{1,5},{2,3},{3,2},{4,0},{5,1},{6,7},{7,6},{8,12},{9,13},{10,... | collective-permute-start | bytes 1769480 | tf_op jit(solution)/shard_map/rs_down_2/ppermute | solution.py:493
  137.3 9.9 %collective-permute-start.37 = (bf16[4,96,768]{2,1,0:T(8,128)(2,1)S(1)}, bf16[4,96,768]{2,1,0:T(8,128)(2,1)S(1)}, u32[]{:S(2)}, u32[]{:S(2)}) collective-permute-start(bf16[4,96,768]{2,1,0:T(8,128)(2,1)S(1)} %add_convert_fusion.3), channel_id=1, source_target_pairs={{0,1},{1,0},{2,6},{3,7},{4,5},{5,4},{6,2},{7,3},{8,9},{9,8},{10,14... | collective-permute-start | bytes 1769480 | tf_op jit(solution)/shard_map/rs_down_1/ppermute | solution.py:493
  147.2 3.3 %collective-permute-start.38 = (bf16[4,128,768]{2,1,0:T(8,128)(2,1)}, bf16[4,128,768]{2,1,0:T(8,128)(2,1)S(1)}, u32[]{:S(2)}, u32[]{:S(2)}) collective-permute-start(bf16[4,128,768]{2,1,0:T(8,128)(2,1)} %get-tuple-element.236), channel_id=1, source_target_pairs={{0,2},{1,3},{2,0},{3,1},{4,6},{5,7},{6,4},{7,5},{8,10},{9,11},{10,... | collective-permute-start | bytes 2359304 | tf_op jit(solution)/shard_map/twin/ppermute | solution.py:493
  147.2 5.7 %collective-permute-start.26 = (bf16[4,96,768]{2,1,0:T(8,128)(2,1)S(1)}, bf16[4,96,768]{2,1,0:T(8,128)(2,1)S(1)}, u32[]{:S(2)}, u32[]{:S(2)}) collective-permute-start(bf16[4,96,768]{2,1,0:T(8,128)(2,1)S(1)} %copy-done.38), channel_id=1, source_target_pairs={{0,2},{1,3},{2,0},{3,1},{4,6},{5,7},{6,4},{7,5},{8,10},{9,11},{10,... | collective-permute-start | bytes 1769480 | tf_op jit(solution)/shard_map/twin/ppermute | solution.py:493
  147.7 16.7 %collective-permute-start.40 = (bf16[4,128,768]{2,1,0:T(8,128)(2,1)}, bf16[4,128,768]{2,1,0:T(8,128)(2,1)S(1)}, u32[]{:S(2)}, u32[]{:S(2)}) collective-permute-start(bf16[4,128,768]{2,1,0:T(8,128)(2,1)} %get-tuple-element.238), channel_id=1, source_target_pairs={{0,2},{1,3},{2,0},{3,1},{4,6},{5,7},{6,4},{7,5},{8,10},{9,11},{10,... | collective-permute-start | bytes 2359304 | tf_op jit(solution)/shard_map/twin/ppermute | solution.py:493
  151.8 18.1 %collective-permute-start.39 = (bf16[4,128,768]{2,1,0:T(8,128)(2,1)S(1)}, bf16[4,128,768]{2,1,0:T(8,128)(2,1)S(1)}, u32[]{:S(2)}, u32[]{:S(2)}) collective-permute-start(bf16[4,128,768]{2,1,0:T(8,128)(2,1)S(1)} %add_convert_fusion.2), channel_id=1, source_target_pairs={{0,4},{1,5},{2,3},{3,2},{4,0},{5,1},{6,7},{7,6},{8,12},{9,13},{10,... | collective-permute-start | bytes 2359304 | tf_op jit(solution)/shard_map/rs_up_3/ppermute | solution.py:493
  152.8 17.1 %collective-permute-start.43 = (bf16[4,128,768]{2,1,0:T(8,128)(2,1)}, bf16[4,128,768]{2,1,0:T(8,128)(2,1)S(1)}, u32[]{:S(2)}, u32[]{:S(2)}) collective-permute-start(bf16[4,128,768]{2,1,0:T(8,128)(2,1)} %get-tuple-element.245), channel_id=1, source_target_pairs={{0,2},{1,3},{2,0},{3,1},{4,6},{5,7},{6,4},{7,5},{8,10},{9,11},{10,... | collective-permute-start | bytes 2359304 | tf_op jit(solution)/shard_map/twin/ppermute | solution.py:493
  153.2 16.7 %collective-permute-start.41 = (bf16[2,96,768]{2,1,0:T(8,128)(2,1)S(1)}, bf16[2,96,768]{2,1,0:T(8,128)(2,1)S(1)}, u32[]{:S(2)}, u32[]{:S(2)}) collective-permute-start(bf16[2,96,768]{2,1,0:T(8,128)(2,1)S(1)} %slice.229), channel_id=1, source_target_pairs={{0,16},{1,17},{2,18},{3,19},{4,20},{5,21},{6,22},{7,23},{8,24},{9,... | collective-permute-start | bytes 884744 | tf_op jit(solution)/shard_map/rs_down_z2/ppermute | solution.py:493
  170.2 20.4 %collective-permute-start.44 = (bf16[4,128,768]{2,1,0:T(8,128)(2,1)S(1)}, bf16[4,128,768]{2,1,0:T(8,128)(2,1)S(1)}, u32[]{:S(2)}, u32[]{:S(2)}) collective-permute-start(bf16[4,128,768]{2,1,0:T(8,128)(2,1)S(1)} %add_convert_fusion), channel_id=1, source_target_pairs={{0,1},{1,0},{2,6},{3,7},{4,5},{5,4},{6,2},{7,3},{8,9},{9,8},{10,14... | collective-permute-start | bytes 2359304 | tf_op jit(solution)/shard_map/rs_up_1/ppermute | solution.py:493
  171.3 19.2 %collective-permute-start.45 = (bf16[4,128,768]{2,1,0:T(8,128)(2,1)S(1)}, bf16[4,128,768]{2,1,0:T(8,128)(2,1)S(1)}, u32[]{:S(2)}, u32[]{:S(2)}) collective-permute-start(bf16[4,128,768]{2,1,0:T(8,128)(2,1)S(1)} %add_convert_fusion.1), channel_id=1, source_target_pairs={{0,4},{1,5},{2,3},{3,2},{4,0},{5,1},{6,7},{7,6},{8,12},{9,13},{10,... | collective-permute-start | bytes 2359304 | tf_op jit(solution)/shard_map/rs_up_2/ppermute | solution.py:493
  172.3 18.8 %collective-permute-start.49 = (bf16[4,128,768]{2,1,0:T(8,128)(2,1)S(1)}, bf16[4,128,768]{2,1,0:T(8,128)(2,1)S(1)}, u32[]{:S(2)}, u32[]{:S(2)}) collective-permute-start(bf16[4,128,768]{2,1,0:T(8,128)(2,1)S(1)} %copy-done.37), channel_id=1, source_target_pairs={{0,2},{1,3},{2,0},{3,1},{4,6},{5,7},{6,4},{7,5},{8,10},{9,11},{10,... | collective-permute-start | bytes 2359304 | tf_op jit(solution)/shard_map/twin/ppermute | solution.py:493
  172.4 12.6 %collective-permute-start.42 = (bf16[96,768]{1,0:T(8,128)(2,1)S(1)}, bf16[96,768]{1,0:T(8,128)(2,1)S(1)}, u32[]{:S(2)}, u32[]{:S(2)}) collective-permute-start(bf16[96,768]{1,0:T(8,128)(2,1)S(1)} %fusion.7), channel_id=1, source_target_pairs={{0,8},{1,9},{2,10},{3,11},{4,12},{5,13},{6,14},{7,15},{8,0},{9,1},... | collective-permute-start | bytes 442376 | tf_op jit(solution)/shard_map/rs_down_z1/ppermute | solution.py:493
  190.6 3.4 %collective-permute-start.46 = (bf16[4,80,768]{2,1,0:T(8,128)(2,1)}, bf16[4,80,768]{2,1,0:T(8,128)(2,1)S(1)}, u32[]{:S(2)}, u32[]{:S(2)}) collective-permute-start(bf16[4,80,768]{2,1,0:T(8,128)(2,1)} %get-tuple-element.269), channel_id=1, source_target_pairs={{0,2},{1,3},{2,0},{3,1},{4,6},{5,7},{6,4},{7,5},{8,10},{9,11},{10,... | collective-permute-start | bytes 1474568 | tf_op jit(solution)/shard_map/twin/ppermute | solution.py:493
  190.6 10.0 %collective-permute-start.48 = (bf16[4,80,768]{2,1,0:T(8,128)(2,1)}, bf16[4,80,768]{2,1,0:T(8,128)(2,1)S(1)}, u32[]{:S(2)}, u32[]{:S(2)}) collective-permute-start(bf16[4,80,768]{2,1,0:T(8,128)(2,1)} %get-tuple-element.271), channel_id=1, source_target_pairs={{0,2},{1,3},{2,0},{3,1},{4,6},{5,7},{6,4},{7,5},{8,10},{9,11},{10,... | collective-permute-start | bytes 1474568 | tf_op jit(solution)/shard_map/twin/ppermute | solution.py:493
  191.5 10.3 %collective-permute-start.50 = (bf16[128,768]{1,0:T(8,128)(2,1)S(1)}, bf16[128,768]{1,0:T(8,128)(2,1)S(1)}, u32[]{:S(2)}, u32[]{:S(2)}) collective-permute-start(bf16[128,768]{1,0:T(8,128)(2,1)S(1)} %get-tuple-element.305), channel_id=1, source_target_pairs={{0,8},{1,9},{2,10},{3,11},{4,12},{5,13},{6,14},{7,15},{8,0},{9,1},... | collective-permute-start | bytes 589832 | tf_op jit(solution)/shard_map/rs_up_z/ppermute | solution.py:493
  191.6 12.1 %collective-permute-start.51 = (bf16[128,768]{1,0:T(8,128)(2,1)S(1)}, bf16[128,768]{1,0:T(8,128)(2,1)S(1)}, u32[]{:S(2)}, u32[]{:S(2)}) collective-permute-start(bf16[128,768]{1,0:T(8,128)(2,1)S(1)} %get-tuple-element.304), channel_id=1, source_target_pairs={{0,16},{1,17},{2,18},{3,19},{4,20},{5,21},{6,22},{7,23},{8,24},{9,... | collective-permute-start | bytes 589832 | tf_op jit(solution)/shard_map/rs_up_z/ppermute | solution.py:493
  194.0 9.7 %collective-permute-start.53 = (bf16[4,80,768]{2,1,0:T(8,128)(2,1)}, bf16[4,80,768]{2,1,0:T(8,128)(2,1)S(1)}, u32[]{:S(2)}, u32[]{:S(2)}) collective-permute-start(bf16[4,80,768]{2,1,0:T(8,128)(2,1)} %get-tuple-element.284), channel_id=1, source_target_pairs={{0,2},{1,3},{2,0},{3,1},{4,6},{5,7},{6,4},{7,5},{8,10},{9,11},{10,... | collective-permute-start | bytes 1474568 | tf_op jit(solution)/shard_map/twin/ppermute | solution.py:493
  194.1 9.6 %collective-permute-start.47 = (bf16[4,80,768]{2,1,0:T(8,128)(2,1)S(1)}, bf16[4,80,768]{2,1,0:T(8,128)(2,1)S(1)}, u32[]{:S(2)}, u32[]{:S(2)}) collective-permute-start(bf16[4,80,768]{2,1,0:T(8,128)(2,1)S(1)} %add_convert_fusion.8), channel_id=1, source_target_pairs={{0,4},{1,5},{2,3},{3,2},{4,0},{5,1},{6,7},{7,6},{8,12},{9,13},{10,... | collective-permute-start | bytes 1474568 | tf_op jit(solution)/shard_map/rs_qkv_3/ppermute | solution.py:493
  200.6 16.1 %collective-permute-start.52 = (bf16[4,80,768]{2,1,0:T(8,128)(2,1)S(1)}, bf16[4,80,768]{2,1,0:T(8,128)(2,1)S(1)}, u32[]{:S(2)}, u32[]{:S(2)}) collective-permute-start(bf16[4,80,768]{2,1,0:T(8,128)(2,1)S(1)} %copy-done.40), channel_id=1, source_target_pairs={{0,2},{1,3},{2,0},{3,1},{4,6},{5,7},{6,4},{7,5},{8,10},{9,11},{10,... | collective-permute-start | bytes 1474568 | tf_op jit(solution)/shard_map/twin/ppermute | solution.py:493
  203.9 12.8 %collective-permute-start.54 = (bf16[4,80,768]{2,1,0:T(8,128)(2,1)S(1)}, bf16[4,80,768]{2,1,0:T(8,128)(2,1)S(1)}, u32[]{:S(2)}, u32[]{:S(2)}) collective-permute-start(bf16[4,80,768]{2,1,0:T(8,128)(2,1)S(1)} %add_convert_fusion.6), channel_id=1, source_target_pairs={{0,1},{1,0},{2,6},{3,7},{4,5},{5,4},{6,2},{7,3},{8,9},{9,8},{10,14... | collective-permute-start | bytes 1474568 | tf_op jit(solution)/shard_map/rs_qkv_1/ppermute | solution.py:493
  204.6 12.1 %collective-permute-start.55 = (bf16[4,80,768]{2,1,0:T(8,128)(2,1)S(1)}, bf16[4,80,768]{2,1,0:T(8,128)(2,1)S(1)}, u32[]{:S(2)}, u32[]{:S(2)}) collective-permute-start(bf16[4,80,768]{2,1,0:T(8,128)(2,1)S(1)} %add_convert_fusion.7), channel_id=1, source_target_pairs={{0,4},{1,5},{2,3},{3,2},{4,0},{5,1},{6,7},{7,6},{8,12},{9,13},{10,... | collective-permute-start | bytes 1474568 | tf_op jit(solution)/shard_map/rs_qkv_2/ppermute | solution.py:493
  206.0 7.6 %collective-permute-start.56 = (bf16[128,768]{1,0:T(8,128)(2,1)S(1)}, bf16[128,768]{1,0:T(8,128)(2,1)S(1)}, u32[]{:S(2)}, u32[]{:S(2)}) collective-permute-start(bf16[128,768]{1,0:T(8,128)(2,1)S(1)} %get-tuple-element.289), channel_id=1, source_target_pairs={{0,24},{1,25},{2,26},{3,27},{4,28},{5,29},{6,30},{7,31},{8,16},{9,... | collective-permute-start | bytes 589832 | tf_op jit(solution)/shard_map/rs_up_z/ppermute | solution.py:493
  217.0 16.7 %collective-permute-start.57 = (bf16[256,768]{1,0:T(8,128)(2,1)S(1)}, bf16[256,768]{1,0:T(8,128)(2,1)S(1)}, u32[]{:S(2)}, u32[]{:S(2)}) collective-permute-start(bf16[256,768]{1,0:T(8,128)(2,1)S(1)} %copy-done.41), channel_id=1, source_target_pairs={{0,1},{1,0},{2,3},{3,2},{4,5},{5,4},{6,7},{7,6},{8,9},{9,8},{10,11... | collective-permute-start | bytes 1179656 | tf_op jit(solution)/shard_map/grad_pack/ppermute | solution.py:493
  218.2 8.1 %collective-permute-start.60 = (bf16[80,768]{1,0:T(8,128)(2,1)S(1)}, bf16[80,768]{1,0:T(8,128)(2,1)S(1)}, u32[]{:S(2)}, u32[]{:S(2)}) collective-permute-start(bf16[80,768]{1,0:T(8,128)(2,1)S(1)} %get-tuple-element.307), channel_id=1, source_target_pairs={{0,24},{1,25},{2,26},{3,27},{4,28},{5,29},{6,30},{7,31},{8,16},{9,... | collective-permute-start | bytes 368648 | tf_op jit(solution)/shard_map/rs_qkv_z/ppermute | solution.py:493
  220.2 10.5 %collective-permute-start.59 = (bf16[80,768]{1,0:T(8,128)(2,1)S(1)}, bf16[80,768]{1,0:T(8,128)(2,1)S(1)}, u32[]{:S(2)}, u32[]{:S(2)}) collective-permute-start(bf16[80,768]{1,0:T(8,128)(2,1)S(1)} %get-tuple-element.308), channel_id=1, source_target_pairs={{0,16},{1,17},{2,18},{3,19},{4,20},{5,21},{6,22},{7,23},{8,24},{9,... | collective-permute-start | bytes 368648 | tf_op jit(solution)/shard_map/rs_qkv_z/ppermute | solution.py:493
  220.2 10.5 %collective-permute-start.58 = (bf16[80,768]{1,0:T(8,128)(2,1)S(1)}, bf16[80,768]{1,0:T(8,128)(2,1)S(1)}, u32[]{:S(2)}, u32[]{:S(2)}) collective-permute-start(bf16[80,768]{1,0:T(8,128)(2,1)S(1)} %get-tuple-element.306), channel_id=1, source_target_pairs={{0,8},{1,9},{2,10},{3,11},{4,12},{5,13},{6,14},{7,15},{8,0},{9,1},... | collective-permute-start | bytes 368648 | tf_op jit(solution)/shard_map/rs_qkv_z/ppermute | solution.py:493
  (39 other events, 285.4 us)
